TPU v7x, 32 devices: a whole 2x2x4 slice. The times are simulated.
32 devices in a mesh: dp: 4 (over x, core), tm: 8 (over z, y).
Axes of the slice: x: 2, y: 2, z: 4, core: 2. Of those that a mesh axis runs over, the one named last changes fastest.
Arguments:
- latents: bfloat16 [4, 17, 16, 64, 256], P('dp', None, 'tm'), may hold values from -6 to 6
- cotangent: bfloat16 [4, 17, 16, 64, 256], P('dp', None, 'tm'), may hold values from -6 to 6
- spatial_weight: bfloat16 [3, 3, 256, 256], replicated, may hold values from -0.125 to 0.125
- temporal_weight: bfloat16 [3, 256, 256], replicated, may hold values from -0.21875 to 0.21875
Outputs:
- block_out: bfloat16 [4, 17, 16, 64, 256], P('dp', None, 'tm')
- latents_grad: bfloat16 [4, 17, 16, 64, 256], P('dp', None, 'tm')
- spatial_grad: float32 [3, 3, 256, 256], replicated
- temporal_grad: float32 [3, 256, 256], replicated
All inputs are finite; a program needn't handle non-finite values.
Results may differ from a plain program's by a relative error of at most 0.0085.
Values may be sent and summed in bfloat16 or wider, within the bound.
No kernel may reach another device: no remote copies, remote signals or barrier semaphores. Data moves between devices by JAX's collectives and lax.ppermute only.
A program may use at most 64 MiB of HBM per device.

v0:
```python
import jax
import jax.numpy as jnp
from jax import lax
from jax.sharding import PartitionSpec as P


def with_halo(cells, sides, width):
    for axis, dim in sides:
        count = lax.axis_size(axis)
        ends = count - 1
        head = lax.slice_in_dim(cells, 0, width, axis=dim)
        tail = lax.slice_in_dim(cells, cells.shape[dim] - width, cells.shape[dim], axis=dim)
        cells = jnp.concatenate(
            [
                lax.ppermute(tail, axis, [(i, (i + 1) % count) for i in range(ends)]),
                cells,
                lax.ppermute(head, axis, [((i + 1) % count, i) for i in range(ends)]),
            ],
            axis=dim,
        )
    return cells


def band_patches(extended, rows_out, flipped):
    padded = jnp.pad(extended, ((0, 0), (0, 0), (1, 1), (0, 0)))
    cols = extended.shape[2]
    pieces = []
    for first in range(3):
        for second in range(3):
            top = 2 - first if flipped else first
            left = 2 - second if flipped else second
            pieces.append(padded[:, top : top + rows_out, left : left + cols, :])
    return jnp.concatenate(pieces, axis=3).reshape(-1, 9 * extended.shape[3])


def causal_mix(act, weight):
    clips, frames, cells, chans = act.shape
    padded = jnp.pad(act, ((0, 0), (2, 0), (0, 0), (0, 0)))
    total = jnp.zeros((clips * frames * cells, chans), jnp.float32)
    for tap in range(3):
        earlier = padded[:, 2 - tap : 2 - tap + frames].reshape(-1, chans)
        total = total + jnp.dot(earlier, weight[tap], preferred_element_type=jnp.float32)
    return total.astype(jnp.bfloat16)


def anti_mix(cot, weight):
    clips, frames, cells, chans = cot.shape
    padded = jnp.pad(cot, ((0, 0), (0, 2), (0, 0), (0, 0)))
    total = jnp.zeros((clips * frames * cells, chans), jnp.float32)
    for tap in range(3):
        later = padded[:, tap : tap + frames].reshape(-1, chans)
        total = total + lax.dot_general(
            later, weight[tap], (((1,), (1,)), ((), ())), preferred_element_type=jnp.float32
        )
    return total.astype(jnp.bfloat16)


def tap_grads(act, cot):
    clips, frames, cells, chans = act.shape
    padded = jnp.pad(act, ((0, 0), (2, 0), (0, 0), (0, 0)))
    cot_flat = cot.reshape(-1, chans)
    parts = []
    for tap in range(3):
        earlier = padded[:, 2 - tap : 2 - tap + frames].reshape(-1, chans)
        parts.append(
            lax.dot_general(
                earlier, cot_flat, (((0,), (0,)), ((), ())), preferred_element_type=jnp.float32
            )
        )
    return jnp.stack(parts)


def silu_grad(act_grad, pre):
    sig = jax.nn.sigmoid(pre)
    return (act_grad.astype(jnp.float32) * sig * (1.0 + pre * (1.0 - sig))).astype(jnp.bfloat16)


def body(latents, cotangent, spatial_weight, temporal_weight):
    clips, frames, rows, cols, chans = latents.shape
    flat_w = spatial_weight.reshape(9 * chans, chans)
    flip_w = jnp.transpose(spatial_weight, (0, 1, 3, 2)).reshape(9 * chans, chans)
    cot_band = cotangent.reshape(clips, frames, rows * cols, chans)
    extended = with_halo(latents, (("tm", 2),), 1)
    patches = band_patches(extended.reshape(clips * frames, rows + 2, cols, chans), rows, False)
    pre = jnp.dot(patches, flat_w, preferred_element_type=jnp.float32)
    act = jax.nn.silu(pre).astype(jnp.bfloat16).reshape(clips, frames, rows * cols, chans)
    mixed = causal_mix(act, temporal_weight)
    act_grad = anti_mix(cot_band, temporal_weight)
    pre_grad = silu_grad(act_grad, pre)
    grad_ext = with_halo(pre_grad.reshape(clips, frames, rows, cols, chans), (("tm", 2),), 1)
    back = jnp.dot(
        band_patches(grad_ext.reshape(clips * frames, rows + 2, cols, chans), rows, True),
        flip_w,
        preferred_element_type=jnp.float32,
    )
    temporal_local = tap_grads(act, cot_band)
    block_out = (latents.reshape(-1, chans).astype(jnp.float32) + mixed.astype(jnp.float32)).astype(
        jnp.bfloat16
    )
    latents_grad = (cotangent.reshape(-1, chans).astype(jnp.float32) + back).astype(jnp.bfloat16)
    spatial_local = lax.dot_general(
        patches, pre_grad, (((0,), (0,)), ((), ())), preferred_element_type=jnp.float32
    )
    spatial_sum, temporal_sum = lax.psum((spatial_local, temporal_local), ("dp", "tm"))
    scale = (clips * lax.axis_size("dp") * frames * rows * lax.axis_size("tm") * cols) ** (-0.5)
    return (
        block_out.reshape(latents.shape),
        latents_grad.reshape(latents.shape),
        (spatial_sum * scale).reshape(3, 3, chans, chans),
        temporal_sum * scale,
    )


def solution(mesh):
    in_specs = (P("dp", None, "tm", None, None), P("dp", None, "tm", None, None), P(), P())
    out_specs = (P("dp", None, "tm", None, None), P("dp", None, "tm", None, None), P(), P())
    return jax.shard_map(body, mesh=mesh, in_specs=in_specs, out_specs=out_specs, check_vma=False)
```

profile of v0, /device:TPU:0, one launch (start us, length us, event | category | flops | bytes accessed | tf_op | source)
XLA Modules:
  0.0 221.9 jit_solution(1711821189721772850)
XLA Ops:
  7.2 0.0 copy-start
  7.2 0.0 all-reduce.7.cloned.1.call-start
  7.2 2.4 %fusion.37 = (bf16[1,17,1,64,256]{4,3,2,1,0:T(8,128)(2,1)}, bf16[1,17,1,64,256]{4,3,2,1,0:T(8,128)(2,1)}) fusion(bf16[1,17,2,64,256]{4,3,2,1,0:T(8,128)(2,1)} %param.4), kind=kLoop, calls=%fused_computation.74 | loop fusion | bytes 2228224 | tf_op jit(solution)/shard_map/slice | solution.py:12
  9.6 5.8 %collective-permute-start = (bf16[1,17,1,64,256]{4,3,2,1,0:T(8,128)(2,1)}, bf16[1,17,1,64,256]{4,3,2,1,0:T(8,128)(2,1)}, u32[]{:S(2)}, u32[]{:S(2)}) collective-permute-start(bf16[1,17,1,64,256]{4,3,2,1,0:T(8,128)(2,1)} %get-tuple-element.12), channel_id=1, source_target_pairs={{0,1},{1,2},{2,3},{3,4},{4,5},{5,6},{6,7},{8,9},{9,10},{10,11},{11... | collective-permute-start | bytes 1671176 | tf_op jit(solution)/shard_map/ppermute | solution.py:15
  15.5 1.3 collective-permute-start.1
  16.7 0.0 copy-done
  16.8 2.8 %fusion.26 = f32[2176,256]{1,0:T(8,128)} fusion(bf16[2176,256]{1,0:T(8,128)(2,1)S(1)} %bitcast.62, bf16[3,256,256]{2,1,0:T(8,128)(2,1)} %param.7), kind=kOutput, calls=%fused_computation.63 | convolution fusion | flops 285212672 | bytes 3473408 | tf_op jit(solution)/shard_map/dot_general | solution.py:52
  19.5 0.0 copy-done.6
  19.5 1.5 copy.8
  21.1 0.2 pad_slice_fusion.12
  21.2 1.4 copy-done.3
  22.7 0.0 copy-done.8
  22.7 0.5 convolution_add_fusion.1
  23.2 15.6 %collective-permute-done = bf16[1,17,1,64,256]{4,3,2,1,0:T(8,128)(2,1)} collective-permute-done((bf16[1,17,1,64,256]{4,3,2,1,0:T(8,128)(2,1)}, bf16[1,17,1,64,256]{4,3,2,1,0:T(8,128)(2,1)}, u32[]{:S(2)}, u32[]{:S(2)}) %collective-permute-start) | collective-permute-done | bytes 557088 | tf_op jit(solution)/shard_map/ppermute | solution.py:15
  38.8 0.0 collective-permute-done.1
  38.8 0.0 copy-done.1
  38.8 1.5 maximum_bitcast_fusion
  40.2 0.4 fusion.10
  40.6 0.1 slice_dynamic-update-slice_fusion.5
  40.7 0.6 fusion.11
  41.3 0.7 fusion.12
  42.0 0.1 slice_dynamic-update-slice_fusion.4
  42.1 0.6 fusion.13
  42.7 0.7 fusion.14
  43.4 0.1 slice_dynamic-update-slice_fusion.3
  43.5 0.6 fusion.15
  44.1 2.9 %multiply_convert_fusion = (bf16[2176,256]{1,0:T(8,128)(2,1)S(1)}, f32[2176,256]{1,0:T(8,128)S(1)}) fusion(bf16[2176,2304]{1,0:T(8,128)(2,1)S(1)} %bitcast.82, bf16[2304,256]{1,0:T(8,128)(2,1)S(1)} %bitcast.78), kind=kOutput, calls=%fused_computation.17 | convolution fusion | flops 2569699328 | bytes 14548992 | tf_op jit(solution)/shard_map/dot_general | solution.py:85
  47.0 0.5 convolution_bitcast_fusion.2
  47.6 1.8 fusion.28
  49.4 1.0 fusion.9
  50.4 0.0 copy-start.4
  50.4 4.4 %fusion.38 = f32[2304,256]{1,0:T(8,128)} fusion(bf16[2176,2304]{1,0:T(8,128)(2,1)S(1)} %bitcast.83, bf16[2176,256]{1,0:T(8,128)(2,1)S(1)} %fusion.9), kind=kOutput, calls=%fused_computation.75 | convolution fusion | flops 2566914048 | bytes 13500416 | tf_op jit(solution)/shard_map/dot_general | solution.py:101
  54.8 0.0 copy-done.4
  54.8 1.2 fusion.36
  56.0 5.2 %collective-permute-start.2 = (bf16[1,17,1,64,256]{4,3,2,1,0:T(8,128)(2,1)}, bf16[1,17,1,64,256]{4,3,2,1,0:T(8,128)(2,1)}, u32[]{:S(2)}, u32[]{:S(2)}) collective-permute-start(bf16[1,17,1,64,256]{4,3,2,1,0:T(8,128)(2,1)} %get-tuple-element.6), channel_id=1, source_target_pairs={{0,1},{1,2},{2,3},{3,4},{4,5},{5,6},{6,7},{8,9},{9,10},{10,11},{11... | collective-permute-start | bytes 1671176 | tf_op jit(solution)/shard_map/ppermute | solution.py:15
  61.3 1.3 collective-permute-start.3
  62.6 0.1 pad_slice_fusion.14
  62.7 0.0 copy-start.2
  62.7 0.5 convolution_bitcast_fusion
  63.2 0.5 convolution_bitcast_fusion.1
  63.8 0.0 copy-done.2
  63.8 0.9 pad_maximum_fusion
  64.7 0.0 all-reduce.7.cloned.1.call-update
  64.7 2.5 %convolution_add_fusion.3 = f32[2176,256]{1,0:T(8,128)S(1)} fusion(f32[2176,256]{1,0:T(8,128)} %fusion.28, bf16[2176,256]{1,0:T(8,128)(2,1)} %bitcast.73, bf16[3,256,256]{2,1,0:T(8,128)(2,1)} %param.7), kind=kOutput, calls=%fused_computation.3 | convolution fusion | flops 285769728 | bytes 5701632 | tf_op jit(solution)/shard_map/dot_general | solution.py:42
  67.2 2.5 %fusion.4 = bf16[2176,256]{1,0:T(8,128)(2,1)} fusion(f32[2176,256]{1,0:T(8,128)S(1)} %convolution_add_fusion.3, bf16[2176,256]{1,0:T(8,128)(2,1)S(1)} %bitcast.71, bf16[2176,256]{1,0:T(8,128)(2,1)S(1)} %bitcast.68, bf16[3,256,256]{2,1,0:T(8,128)(2,1)} %param.7), kind=kOutput, calls=%fused_computation.9 | convolution fusion | flops 288555008 | bytes 5701632 | tf_op jit(solution)/shard_map/dot_general | solution.py:42
  69.7 20.3 %collective-permute-done.2 = bf16[1,17,1,64,256]{4,3,2,1,0:T(8,128)(2,1)} collective-permute-done((bf16[1,17,1,64,256]{4,3,2,1,0:T(8,128)(2,1)}, bf16[1,17,1,64,256]{4,3,2,1,0:T(8,128)(2,1)}, u32[]{:S(2)}, u32[]{:S(2)}) %collective-permute-start.2) | collective-permute-done | bytes 557088 | tf_op jit(solution)/shard_map/ppermute | solution.py:15
  90.1 0.0 collective-permute-done.3
  90.1 1.5 maximum_bitcast_fusion.1
  91.5 0.3 fusion.16
  91.9 0.1 slice_dynamic-update-slice_fusion.2
  92.0 0.7 fusion.17
  92.7 0.6 fusion.18
  93.3 0.1 slice_dynamic-update-slice_fusion.1
  93.4 0.7 fusion.19
  94.1 0.6 fusion.20
  94.7 0.1 slice_dynamic-update-slice_fusion
  94.8 0.0 copy-start.7
  94.8 0.7 fusion.21
  95.5 0.6 copy-done.7
  96.1 3.8 %fusion = bf16[2176,256]{1,0:T(8,128)(2,1)} fusion(bf16[2176,2304]{1,0:T(8,128)(2,1)S(1)} %bitcast.84, bf16[2304,256]{1,0:T(8,128)(2,1)S(1)} %bitcast.79, bf16[2176,256]{1,0:T(8,128)(2,1)S(1)} %bitcast.67), kind=kOutput, calls=%fused_computation.5 | convolution fusion | flops 2568585216 | bytes 13434880 | tf_op jit(solution)/shard_map/dot_general | solution.py:91
  99.9 110.9 %all-reduce.7.cloned.1.call-done = (f32[2304,256]{1,0:T(8,128)}, f32[3,256,256]{2,1,0:T(8,128)}) async-done(((f32[2304,256]{1,0:T(8,128)}, f32[3,256,256]{2,1,0:T(8,128)}), (f32[2304,256]{1,0:T(8,128)}, f32[3,256,256]{2,1,0:T(8,128)})) %all-reduce.7.cloned.1.call-update) | async-done | bytes 3145744 | tf_op jit(solution)/shard_map/psum | solution.py:104
  210.8 3.3 %broadcast_multiply_fusion = f32[2304,256]{1,0:T(8,128)} fusion(f32[2304,256]{1,0:T(8,128)} %get-tuple-element.4), kind=kLoop, calls=%fused_computation.31 | loop fusion | flops 589824 | bytes 4718592 | tf_op jit(solution)/shard_map/mul | solution.py:109
  214.1 0.0 copy-done.9
  214.1 0.9 broadcast_multiply_fusion.1
  (7 shorter events, 0.0 us)
Async XLA Ops:
  7.2 9.6 %copy-start = (bf16[1,17,2,64,256]{4,3,2,1,0:T(8,128)(2,1)S(1)}, bf16[1,17,2,64,256]{4,3,2,1,0:T(8,128)(2,1)}, u32[]{:S(2)}) copy-start(bf16[1,17,2,64,256]{4,3,2,1,0:T(8,128)(2,1)} %param.5) | copy-start | bytes 3342340
  7.2 203.6 %all-reduce.7.cloned.1.call-start = ((), (), s32[]{:S(2)}) async-start(), calls=%async_computation | async-start | bytes 6291456 | tf_op jit(solution)/shard_map/psum | solution.py:104
  9.6 9.9 %copy-start.6 = (bf16[3,3,256,256]{3,2,1,0:T(8,128)(2,1)S(1)}, bf16[3,3,256,256]{3,2,1,0:T(8,128)(2,1)}, u32[]{:S(2)}) copy-start(bf16[3,3,256,256]{3,2,1,0:T(8,128)(2,1)} %param.6) | copy-start | bytes 3538948
  9.6 29.1 %collective-permute-start = (bf16[1,17,1,64,256]{4,3,2,1,0:T(8,128)(2,1)}, bf16[1,17,1,64,256]{4,3,2,1,0:T(8,128)(2,1)}, u32[]{:S(2)}, u32[]{:S(2)}) collective-permute-start(bf16[1,17,1,64,256]{4,3,2,1,0:T(8,128)(2,1)} %get-tuple-element.12), channel_id=1, source_target_pairs={{0,1},{1,2},{2,3},{3,4},{4,5},{5,6},{6,7},{8,9},{9,10},{10,11},{11... | collective-permute-start | bytes 1671176 | tf_op jit(solution)/shard_map/ppermute | solution.py:15
  15.5 23.3 %collective-permute-start.1 = (bf16[1,17,1,64,256]{4,3,2,1,0:T(8,128)(2,1)}, bf16[1,17,1,64,256]{4,3,2,1,0:T(8,128)(2,1)}, u32[]{:S(2)}, u32[]{:S(2)}) collective-permute-start(bf16[1,17,1,64,256]{4,3,2,1,0:T(8,128)(2,1)} %get-tuple-element.13), channel_id=1, source_target_pairs={{1,0},{2,1},{3,2},{4,3},{5,4},{6,5},{7,6},{9,8},{10,9},{11,10},{12... | collective-permute-start | bytes 1671176 | tf_op jit(solution)/shard_map/ppermute | solution.py:17
  21.1 1.6 copy-start.3
  21.1 1.7 copy-start.8
  22.7 16.0 %copy-start.1 = (bf16[1,17,2,64,256]{4,3,2,1,0:T(8,128)(2,1)S(1)}, bf16[1,17,2,64,256]{4,3,2,1,0:T(8,128)(2,1)}, u32[]{:S(2)}) copy-start(bf16[1,17,2,64,256]{4,3,2,1,0:T(8,128)(2,1)} %param.4) | copy-start | bytes 3342340
  50.4 4.4 %copy-start.4 = (bf16[2176,256]{1,0:T(8,128)(2,1)}, bf16[2176,256]{1,0:T(8,128)(2,1)S(1)}, u32[]{:S(2)}) copy-start(bf16[2176,256]{1,0:T(8,128)(2,1)S(1)} %fusion.9) | copy-start | bytes 3342340
  56.0 34.0 %collective-permute-start.2 = (bf16[1,17,1,64,256]{4,3,2,1,0:T(8,128)(2,1)}, bf16[1,17,1,64,256]{4,3,2,1,0:T(8,128)(2,1)}, u32[]{:S(2)}, u32[]{:S(2)}) collective-permute-start(bf16[1,17,1,64,256]{4,3,2,1,0:T(8,128)(2,1)} %get-tuple-element.6), channel_id=1, source_target_pairs={{0,1},{1,2},{2,3},{3,4},{4,5},{5,6},{6,7},{8,9},{9,10},{10,11},{11... | collective-permute-start | bytes 1671176 | tf_op jit(solution)/shard_map/ppermute | solution.py:15
  61.3 28.8 %collective-permute-start.3 = (bf16[1,17,1,64,256]{4,3,2,1,0:T(8,128)(2,1)}, bf16[1,17,1,64,256]{4,3,2,1,0:T(8,128)(2,1)}, u32[]{:S(2)}, u32[]{:S(2)}) collective-permute-start(bf16[1,17,1,64,256]{4,3,2,1,0:T(8,128)(2,1)} %get-tuple-element.7), channel_id=1, source_target_pairs={{1,0},{2,1},{3,2},{4,3},{5,4},{6,5},{7,6},{9,8},{10,9},{11,10},{12... | collective-permute-start | bytes 1671176 | tf_op jit(solution)/shard_map/ppermute | solution.py:17
  62.7 1.0 copy-start.2
  67.2 22.8 %copy-start.5 = (bf16[2176,256]{1,0:T(8,128)(2,1)S(1)}, bf16[2176,256]{1,0:T(8,128)(2,1)}, u32[]{:S(2)}) copy-start(bf16[2176,256]{1,0:T(8,128)(2,1)} %copy-done.4) | copy-start | bytes 3342340
  94.8 1.3 copy-start.7
  210.8 3.4 %copy-start.9 = (f32[3,256,256]{2,1,0:T(8,128)S(1)}, f32[3,256,256]{2,1,0:T(8,128)}, u32[]{:S(2)}) copy-start(f32[3,256,256]{2,1,0:T(8,128)} %get-tuple-element.5) | copy-start | bytes 2359300
Sparse Core Ops, SparseCore 0:
  64.8 145.8 all-reduce.6
where the time goes:
time: 222 us
  waiting for transfers between devices  147 us (66%)
  matrix products  23.6 us (11%)
  local copies, waits for them, and re-layouts  15.4 us (7%)
  between operations  14.3 us (6%)
  starting transfers between devices  13.6 us (6%)
  other arithmetic  8.18 us (4%)
    psum x1, waiting for transfers between devices, body(): lax.psum((spatial_local, temporal_local), ('dp', 'tm'))  111 us
    ppermute x2, waiting for transfers between devices, with_halo(): lax.ppermute(tail, axis, [(i, (i + 1) % count) for i in range(ends)])  35.9 us
    ppermute x2, starting transfers between devices, with_halo(): lax.ppermute(tail, axis, [(i, (i + 1) % count) for i in range(ends)])  11 us
    unnamed x37, local copies, waits for them, and re-layouts  10.1 us
    dot_general x3, matrix products, causal_mix(): jnp.dot(earlier, weight[tap], preferred_element_type=jnp.float32)  6.78 us
  transfers between devices with their start and end apart: 5, of which 3 were waited for; matrix products, arithmetic and copies ran while one was open for 10% of the time, Pallas kernels for 0%

commit v1 on v0

v1 whole, which is shorter than its diff:
```python
import functools

import jax
import jax.numpy as jnp
from jax import lax
from jax.experimental import pallas as pl
from jax.experimental.pallas import tpu as pltpu
from jax.sharding import PartitionSpec as P

BF16 = jnp.bfloat16
F32 = jnp.float32
TILE_ROWS = 16
VMEM = pl.BlockSpec(memory_space=pltpu.VMEM)
SMEM = pl.BlockSpec(memory_space=pltpu.SMEM)


def mm(a, b):
    return jnp.dot(a, b, preferred_element_type=F32)


def mm_t(a, b):
    return lax.dot_general(a, b, (((1,), (1,)), ((), ())), preferred_element_type=F32)


def outer(a, b):
    return lax.dot_general(a, b, (((0,), (0,)), ((), ())), preferred_element_type=F32)


def call(kernel, outs, scratch, vmem_mb, flops, *args):
    size = sum(a.size * a.dtype.itemsize for a in args)
    size += sum(o.size * o.dtype.itemsize for o in outs)
    return pl.pallas_call(
        kernel,
        out_shape=outs,
        in_specs=[SMEM if a.dtype == jnp.int32 else VMEM for a in args],
        out_specs=[VMEM] * len(outs),
        scratch_shapes=scratch,
        compiler_params=pltpu.CompilerParams(vmem_limit_bytes=vmem_mb << 20),
        cost_estimate=pl.CostEstimate(flops=flops, bytes_accessed=size, transcendentals=0),
    )(*args)


def shift_right(tile):
    w = lax.broadcasted_iota(jnp.int32, tile.shape, 0)
    return jnp.where(w == 0, 0.0, pltpu.roll(tile, 1, 0))


def shift_left(tile):
    w = lax.broadcasted_iota(jnp.int32, tile.shape, 0)
    last = tile.shape[0] - 1
    return jnp.where(w == last, 0.0, pltpu.roll(tile, last, 0))


def row_of(ref, row):
    frames, _, cols, chans = ref.shape
    return ref[:, row].reshape(frames * cols, chans)


def first_kernel(shift, lat, cot, ws, wt, pre_loc, act_grad, taps, cot_pad):
    frames, rows, cols, chans = lat.shape
    cells = frames * cols
    for row in range(rows):
        for b in range(3):
            total = None
            for a in range(3):
                if 0 <= row + a - 1 < rows:
                    part = mm(row_of(lat, row + a - 1), ws[a, b])
                    total = part if total is None else total + part
            taps[b] = total

        @pl.loop(0, frames)
        def _(f):
            at = pl.ds(pl.multiple_of(f * cols, cols), cols)
            pre_loc[row, at] = shift_right(taps[0, at]) + taps[1, at] + shift_left(taps[2, at])

        cot_pad[:cells] = row_of(cot, row)
        cot_pad[cells:] = jnp.zeros((2 * shift, chans), BF16)
        total = mm_t(cot_pad[:cells], wt[0])
        total += mm_t(cot_pad[pl.ds(shift, cells)], wt[1])
        total += mm_t(cot_pad[pl.ds(2 * shift, cells)], wt[2])
        act_grad[row] = total.astype(BF16)


def grads_kernel(
    shift, slots, scale, code, lat, cot, above, below, pre_loc, act_grad, ws, act, pg, sums, taps, spread, cots, total
):
    frames, rows, cols, chans = lat.shape
    cells = frames * cols
    for row in range(rows):
        halos = []
        if row == 0:
            halos.append((0, above))
        if row == rows - 1:
            halos.append((2, below))
        for b in range(3):
            for n, (a, halo) in enumerate(halos):
                part = mm(halo[...], ws[a, b])
                taps[b] = part if n == 0 else taps[b] + part

        @pl.loop(0, frames)
        def _(f):
            at = pl.ds(pl.multiple_of(f * cols, cols), cols)
            pre = pre_loc[row, at]
            if halos:
                pre += shift_right(taps[0, at]) + taps[1, at] + shift_left(taps[2, at])
            sig = 1.0 / (1.0 + jnp.exp(-pre))
            act[row, at] = (pre * sig).astype(BF16)
            grad = act_grad[row, at].astype(F32) * sig * (1.0 + pre * (1.0 - sig))
            grad16 = grad.astype(BF16)
            pg[row, at] = grad16
            grad = grad16.astype(F32)
            spread[at, :chans] = shift_left(grad).astype(BF16)
            spread[at, chans : 2 * chans] = grad16
            spread[at, 2 * chans :] = shift_right(grad).astype(BF16)

        cot_row = row_of(cot, row)
        for k in range(3):
            cots[: cells - k * shift, k * chans : (k + 1) * chans] = cot_row[k * shift :]
            if k:
                cots[cells - k * shift :, k * chans : (k + 1) * chans] = jnp.zeros((k * shift, chans), BF16)
        for a in range(3):
            at = row + a - 1
            cells_in = above[...] if at < 0 else below[...] if at == rows else row_of(lat, at)
            part = outer(cells_in, spread[...])
            total[a * chans : (a + 1) * chans] = part if row == 0 else total[a * chans : (a + 1) * chans] + part
        part = outer(act[row], cots[...])
        total[3 * chans :] = part if row == 0 else total[3 * chans :] + part
    size = total.shape[0] // slots
    for slot in range(slots):
        at = pl.multiple_of((slot ^ code[0]) * size, size)
        sums[slot * size : (slot + 1) * size] = (total[pl.ds(at, size)] * scale).astype(BF16)


def out_kernel(shift, lat, cot, act, pg, ws, wt, block_out, back_loc, taps, act_pad):
    frames, rows, cols, chans = lat.shape
    cells = frames * cols
    for row in range(rows):
        act_pad[: 2 * shift] = jnp.zeros((2 * shift, chans), BF16)
        act_pad[2 * shift :] = act[row]
        mixed = mm(act_pad[pl.ds(2 * shift, cells)], wt[0])
        mixed += mm(act_pad[pl.ds(shift, cells)], wt[1])
        mixed += mm(act_pad[:cells], wt[2])
        mixed = mixed.astype(BF16).astype(F32).reshape(frames, cols, chans)
        block_out[:, row] = (lat[:, row].astype(F32) + mixed).astype(BF16)
        for b in range(3):
            total = None
            for a in range(3):
                if 0 <= row - a + 1 < rows:
                    part = mm_t(pg[row - a + 1], ws[a, b])
                    total = part if total is None else total + part
            taps[b] = total

        @pl.loop(0, frames)
        def _(f):
            at = pl.ds(pl.multiple_of(f * cols, cols), cols)
            back = shift_left(taps[0, at]) + taps[1, at] + shift_right(taps[2, at])
            back_loc[row, at] = cot[f, row].astype(F32) + back


def last_kernel(above, below, back_loc, ws, latents_grad, taps):
    frames, rows, cols, chans = latents_grad.shape
    for row in range(rows):
        halos = []
        if row == 0:
            halos.append((2, above))
        if row == rows - 1:
            halos.append((0, below))
        for b in range(3):
            for n, (a, halo) in enumerate(halos):
                part = mm_t(halo[...], ws[a, b])
                taps[b] = part if n == 0 else taps[b] + part

        @pl.loop(0, frames)
        def _(f):
            at = pl.ds(pl.multiple_of(f * cols, cols), cols)
            back = back_loc[row, at]
            if halos:
                back += shift_left(taps[0, at]) + taps[1, at] + shift_right(taps[2, at])
            latents_grad[f, row] = back.astype(BF16)


def order_kernel(slots, code, sums, spatial, temporal, total):
    chans = spatial.shape[-1]
    size = total.shape[0] // slots
    for slot in range(slots):
        at = pl.multiple_of((slot ^ code[0]) * size, size)
        total[pl.ds(at, size)] = sums[slot * size : (slot + 1) * size].astype(F32)
    for a in range(3):
        for b in range(3):
            spatial[a, b] = total[a * chans : (a + 1) * chans, b * chans : (b + 1) * chans]
    for k in range(3):
        temporal[k] = total[3 * chans :, k * chans : (k + 1) * chans]


def partners(count):
    return [bit for bit in (1 << n for n in range(count.bit_length())) if bit < count]


def swap(x, axis, bit):
    return lax.ppermute(x, axis, [(i, i ^ bit) for i in range(lax.axis_size(axis))])


def plus(x, y):
    return (x.astype(F32) + y.astype(F32)).astype(BF16)


def stages(rows):
    steps = [("dp", bit) for bit in partners(lax.axis_size("dp"))]
    steps += [("tm", bit) for bit in partners(lax.axis_size("tm"))[1:]]
    steps += [("tm", 1)]
    halved = 0
    while halved < len(steps) and rows % (2 * TILE_ROWS << halved) == 0:
        halved += 1
    return steps, halved


def slot_code(steps, halved):
    code = 0
    for n, (axis, bit) in enumerate(steps[:halved]):
        mine = (lax.axis_index(axis) // bit) % 2
        code = code + mine * (1 << (halved - 1 - n))
    return code


def add_up(sums, steps, halved):
    for n, (axis, bit) in enumerate(steps):
        if n < halved:
            half = sums.shape[0] // 2
            sums = plus(sums[:half], swap(sums[half:], axis, bit))
        else:
            sums = plus(sums, swap(sums, axis, bit))
    for axis, bit in steps[:halved][::-1]:
        sums = jnp.concatenate([sums, swap(sums, axis, bit)], axis=0)
    return sums


def halo(first, last):
    ends = lax.axis_size("tm") - 1
    above = lax.ppermute(last, "tm", [(i, i + 1) for i in range(ends)])
    below = lax.ppermute(first, "tm", [(i + 1, i) for i in range(ends)])
    return above, below


def body(latents, cotangent, spatial_weight, temporal_weight):
    clips, frames, rows, cols, chans = latents.shape
    planes, shift = frames * clips, clips * cols
    cells = planes * cols
    lat = jnp.swapaxes(latents, 0, 1).reshape(planes, rows, cols, chans)
    cot = jnp.swapaxes(cotangent, 0, 1).reshape(planes, rows, cols, chans)
    scale = (clips * lax.axis_size("dp") * frames * rows * lax.axis_size("tm") * cols) ** (-0.5)
    steps, halved = stages(4 * chans)
    code = jnp.asarray(slot_code(steps, halved), jnp.int32).reshape(1)
    unit = 2 * cells * chans * chans

    above, below = halo(lat[:, 0].reshape(cells, chans), lat[:, rows - 1].reshape(cells, chans))
    wide = jax.ShapeDtypeStruct((rows, cells, chans), F32)
    narrow = jax.ShapeDtypeStruct((rows, cells, chans), BF16)
    taps = pltpu.VMEM((3, cells, chans), F32)
    padded = pltpu.VMEM((cells + 2 * shift, chans), BF16)
    pre_loc, act_grad = call(
        functools.partial(first_kernel, shift), [wide, narrow], [taps, padded], 56,
        (9 * rows - 6 + 3 * rows) * unit, lat, cot, spatial_weight, temporal_weight,
    )
    act, pg, sums = call(
        functools.partial(grads_kernel, shift, 1 << halved, scale),
        [narrow, narrow, jax.ShapeDtypeStruct((4 * chans, 3 * chans), BF16)],
        [
            taps,
            pltpu.VMEM((cells, 3 * chans), BF16),
            pltpu.VMEM((cells, 3 * chans), BF16),
            pltpu.VMEM((4 * chans, 3 * chans), F32),
        ],
        56, (6 + 12 * rows) * unit,
        code, lat, cot, above, below, pre_loc, act_grad, spatial_weight,
    )
    sums = add_up(sums, steps, halved)
    pg_above, pg_below = halo(pg[0], pg[rows - 1])
    image = jax.ShapeDtypeStruct(lat.shape, BF16)
    block_out, back_loc = call(
        functools.partial(out_kernel, shift), [image, wide], [taps, padded], 56,
        (9 * rows - 6 + 3 * rows) * unit, lat, cot, act, pg, spatial_weight, temporal_weight,
    )
    (latents_grad,) = call(
        last_kernel, [image], [taps], 56, 6 * unit, pg_above, pg_below, back_loc, spatial_weight
    )
    spatial_grad, temporal_grad = call(
        functools.partial(order_kernel, 1 << halved),
        [jax.ShapeDtypeStruct((3, 3, chans, chans), F32), jax.ShapeDtypeStruct((3, chans, chans), F32)],
        [pltpu.VMEM((4 * chans, 3 * chans), F32)], 40, 0, code, sums,
    )

    def back(x):
        return jnp.swapaxes(x.reshape(frames, clips, rows, cols, chans), 0, 1)

    return back(block_out), back(latents_grad), spatial_grad, temporal_grad


def solution(mesh):
    in_specs = (P("dp", None, "tm", None, None), P("dp", None, "tm", None, None), P(), P())
    out_specs = (P("dp", None, "tm", None, None), P("dp", None, "tm", None, None), P(), P())
    return jax.shard_map(body, mesh=mesh, in_specs=in_specs, out_specs=out_specs, check_vma=False)
```

time: 222 us -> 139 us (0.63)
  waiting for transfers between devices: 147 us -> 65.6 us
  Pallas kernels: 0 us -> 36.4 us
  matrix products: 23.6 us -> 0 us
  starting transfers between devices: 13.6 us -> 30.3 us
  between operations: 14.3 us -> 0.9 us
  local copies, waits for them, and re-layouts: 15.4 us -> 4.69 us
  other arithmetic: 8.18 us -> 0.41 us
    psum x1 -> x0, waiting for transfers between devices: 111 us -> none  [body(): lax.psum((spatial_local, temporal_local), ('dp', 'tm'))]
    pallas_call x0 -> x5, Pallas kernels: none -> 36.4 us  [call(): pl.pallas_call(kernel, out_shape=outs, in_specs=[SMEM if a.dtype == jnp.i...]
    ppermute x4 -> x14, waiting for transfers between devices: 35.9 us -> 65.6 us  [the longest x10 37.5 us: swap(): lax.ppermute(x, axis, [(i, i ^ bit) for i in range(lax.axis_size(axis))])]
    dot_general x12 -> x0, matrix products: 23.6 us -> none  [the longest x3 6.78 us: causal_mix(): jnp.dot(earlier, weight[tap], preferred_element_type=jnp.float32)]
    ppermute x4 -> x14, starting transfers between devices: 13.6 us -> 30.3 us  [the longest x10 18.1 us: swap(): lax.ppermute(x, axis, [(i, i ^ bit) for i in range(lax.axis_size(axis))])]
    unnamed x37 -> x16, local copies, waits for them, and re-layouts: 10.1 us -> 1.85 us
    mul x2 -> x0, other arithmetic: 4.3 us -> none  [the longest x1 3.35 us: body(): spatial_sum * scale]
    reshape x2 -> x0, other arithmetic: 2.95 us -> none  [the longest x1 1.48 us: body(): grad_ext.reshape(clips * frames, rows + 2, cols, chans)]
  transfers between devices with their start and end apart: 5 -> 14, of which waited for: 3 -> 12; matrix products, arithmetic and copies ran while one was open for 10% -> 0% of each run, Pallas kernels for 0% -> 16%
where the time goes in v1:
time: 139 us; the launch traced here: 138 us
  waiting for transfers between devices  65.6 us (47%)
  Pallas kernels  36.4 us (26%)
  starting transfers between devices  30.3 us (22%)
  local copies, waits for them, and re-layouts  4.69 us (3%)
    ppermute x10, waiting for transfers between devices, swap(): lax.ppermute(x, axis, [(i, i ^ bit) for i in range(lax.axis_size(axis))])  37.5 us
    pallas_call x5, Pallas kernels, call(): pl.pallas_call(kernel, out_shape=outs, in_specs=[SMEM if a.dtype == jnp.i...  36.4 us
    ppermute x2, waiting for transfers between devices, halo(): above = lax.ppermute(last, 'tm', [(i, i + 1) for i in range(ends)])  25.6 us
    ppermute x10, starting transfers between devices, swap(): lax.ppermute(x, axis, [(i, i ^ bit) for i in range(lax.axis_size(axis))])  18.1 us
    ppermute x2, starting transfers between devices, halo(): above = lax.ppermute(last, 'tm', [(i, i + 1) for i in range(ends)])  9.67 us
  transfers between devices with their start and end apart: 14, of which 12 were waited for; matrix products, arithmetic and copies ran while one was open for 0% of the time, Pallas kernels for 16%

profile of v1, /device:TPU:0, one launch (start us, length us, event | category | flops | bytes accessed | tf_op | source)
XLA Modules:
  0.0 138.3 jit_solution(17618621422957994216)
XLA Ops:
  0.6 1.3 fusion
  1.9 4.9 %collective-permute-start = (bf16[1088,256]{1,0:T(8,128)(2,1)S(1)}, bf16[1088,256]{1,0:T(8,128)(2,1)S(1)}, u32[]{:S(2)}, u32[]{:S(2)}) collective-permute-start(bf16[1088,256]{1,0:T(8,128)(2,1)S(1)} %bitcast.17), channel_id=1, source_target_pairs={{0,1},{1,2},{2,3},{3,4},{4,5},{5,6},{6,7},{8,9},{9,10},{10,11},{11... | collective-permute-start | bytes 1671176 | tf_op jit(solution)/shard_map/ppermute | solution.py:239
  6.8 1.3 collective-permute-start.1
  8.2 7.9 %shard_map.75 = (f32[2,1088,256]{2,1,0:T(8,128)}, bf16[2,1088,256]{2,1,0:T(8,128)(2,1)}) custom-call(bf16[17,2,64,256]{3,2,1,0:T(8,128)(2,1)} %bitcast.12, bf16[17,2,64,256]{3,2,1,0:T(8,128)(2,1)} %bitcast.18, bf16[3,3,256,256]{3,2,1,0:T(8,128)(2,1)} %ws.7, bf16[3,256,256]{2,1,0:T(8,128)(2,1)} %wt.3), custom_call_target="tpu_custom_call" | custom-call | flops 2566914048 | bytes 7143424 | tf_op jit(solution)/shard_map/pallas_call | solution.py:32
  16.2 14.4 %collective-permute-done.above = bf16[1088,256]{1,0:T(8,128)(2,1)S(1)} collective-permute-done((bf16[1088,256]{1,0:T(8,128)(2,1)S(1)}, bf16[1088,256]{1,0:T(8,128)(2,1)S(1)}, u32[]{:S(2)}, u32[]{:S(2)}) %collective-permute-start) | collective-permute-done | bytes 557088 | tf_op jit(solution)/shard_map/ppermute | solution.py:239
  30.6 0.0 copy-start.4
  30.6 0.0 collective-permute-done.1.below
  30.6 0.0 copy-start.5
  30.6 0.8 copy-done.4
  31.4 0.2 copy-done.5
  31.6 12.5 %shard_map.76 = (bf16[2,1088,256]{2,1,0:T(8,128)(2,1)}, bf16[2,1088,256]{2,1,0:T(8,128)(2,1)}, bf16[1024,768]{1,0:T(8,128)(2,1)}) custom-call(s32[1]{0:T(128)} %bitcast.2.code, bf16[17,2,64,256]{3,2,1,0:T(8,128)(2,1)} %bitcast.13, bf16[17,2,64,256]{3,2,1,0:T(8,128)(2,1)} %bitcast.19, bf16[1088,256]{1,0:T(8,128)(2,1)} %copy-done.4, ...), custom_call_target="tpu_custom_call" | custom-call | flops 4278190080 | bytes 11665412 | tf_op jit(solution)/shard_map/pallas_call | solution.py:32
  44.1 0.0 copy-start
  44.1 1.3 slice.47
  45.4 0.1 collective-permute-start.4
  45.5 2.3 %collective-permute-done.4 = bf16[512,768]{1,0:T(8,128)(2,1)S(1)} collective-permute-done((bf16[512,768]{1,0:T(8,128)(2,1)S(1)}, bf16[512,768]{1,0:T(8,128)(2,1)S(1)}, u32[]{:S(2)}, u32[]{:S(2)}) %collective-permute-start.4) | collective-permute-done | bytes 786464 | tf_op jit(solution)/shard_map/ppermute | solution.py:200
  47.7 0.0 copy-done
  47.7 0.2 add_convert_fusion
  48.0 1.5 %collective-permute-start.5 = (bf16[256,768]{1,0:T(8,128)(2,1)S(1)}, bf16[256,768]{1,0:T(8,128)(2,1)S(1)}, u32[]{:S(2)}, u32[]{:S(2)}) collective-permute-start(bf16[256,768]{1,0:T(8,128)(2,1)S(1)} %slice.59), channel_id=1, source_target_pairs={{0,16},{8,24},{16,0},{24,8},{1,17},{9,25},{17,1},{25,9},{2,18},{10... | collective-permute-start | bytes 1179656 | tf_op jit(solution)/shard_map/ppermute | solution.py:200
  49.5 9.7 %collective-permute-done.5 = bf16[256,768]{1,0:T(8,128)(2,1)S(1)} collective-permute-done((bf16[256,768]{1,0:T(8,128)(2,1)S(1)}, bf16[256,768]{1,0:T(8,128)(2,1)S(1)}, u32[]{:S(2)}, u32[]{:S(2)}) %collective-permute-start.5) | collective-permute-done | bytes 393248 | tf_op jit(solution)/shard_map/ppermute | solution.py:200
  59.2 0.1 add_convert_fusion.1
  59.3 3.3 %collective-permute-start.6 = (bf16[128,768]{1,0:T(8,128)(2,1)S(1)}, bf16[128,768]{1,0:T(8,128)(2,1)S(1)}, u32[]{:S(2)}, u32[]{:S(2)}) collective-permute-start(bf16[128,768]{1,0:T(8,128)(2,1)S(1)} %slice.61), channel_id=1, source_target_pairs={{0,2},{1,3},{2,0},{3,1},{4,6},{5,7},{6,4},{7,5},{8,10},{9,11},{10,... | collective-permute-start | bytes 589832 | tf_op jit(solution)/shard_map/ppermute | solution.py:200
  62.6 4.4 %collective-permute-done.6 = bf16[128,768]{1,0:T(8,128)(2,1)S(1)} collective-permute-done((bf16[128,768]{1,0:T(8,128)(2,1)S(1)}, bf16[128,768]{1,0:T(8,128)(2,1)S(1)}, u32[]{:S(2)}, u32[]{:S(2)}) %collective-permute-start.6) | collective-permute-done | bytes 196640 | tf_op jit(solution)/shard_map/ppermute | solution.py:200
  67.1 2.8 %collective-permute-start.7 = (bf16[64,768]{1,0:T(8,128)(2,1)S(1)}, bf16[64,768]{1,0:T(8,128)(2,1)S(1)}, u32[]{:S(2)}, u32[]{:S(2)}) collective-permute-start(bf16[64,768]{1,0:T(8,128)(2,1)S(1)} %slice.63), channel_id=1, source_target_pairs={{0,4},{1,5},{2,6},{3,7},{4,0},{5,1},{6,2},{7,3},{8,12},{9,13},{10,... | collective-permute-start | bytes 294920 | tf_op jit(solution)/shard_map/ppermute | solution.py:200
  69.9 2.8 %collective-permute-done.7 = bf16[64,768]{1,0:T(8,128)(2,1)S(1)} collective-permute-done((bf16[64,768]{1,0:T(8,128)(2,1)S(1)}, bf16[64,768]{1,0:T(8,128)(2,1)S(1)}, u32[]{:S(2)}, u32[]{:S(2)}) %collective-permute-start.7) | collective-permute-done | bytes 98336 | tf_op jit(solution)/shard_map/ppermute | solution.py:200
  72.7 1.0 collective-permute-start.8
  73.7 3.1 %collective-permute-done.8 = bf16[32,768]{1,0:T(8,128)(2,1)S(1)} collective-permute-done((bf16[32,768]{1,0:T(8,128)(2,1)S(1)}, bf16[32,768]{1,0:T(8,128)(2,1)S(1)}, u32[]{:S(2)}, u32[]{:S(2)}) %collective-permute-start.8) | collective-permute-done | bytes 49184 | tf_op jit(solution)/shard_map/ppermute | solution.py:200
  76.9 1.5 %collective-permute-start.9 = (bf16[32,768]{1,0:T(8,128)(2,1)S(1)}, bf16[32,768]{1,0:T(8,128)(2,1)S(1)}, u32[]{:S(2)}, u32[]{:S(2)}) collective-permute-start(bf16[32,768]{1,0:T(8,128)(2,1)S(1)} %get-tuple-element.23), channel_id=1, source_target_pairs={{0,1},{1,0},{2,3},{3,2},{4,5},{5,4},{6,7},{7,6},{8,9},{9,8},{10,11... | collective-permute-start | bytes 147464 | tf_op jit(solution)/shard_map/ppermute | solution.py:200
  78.4 2.6 %collective-permute-done.9 = bf16[32,768]{1,0:T(8,128)(2,1)S(1)} collective-permute-done((bf16[32,768]{1,0:T(8,128)(2,1)S(1)}, bf16[32,768]{1,0:T(8,128)(2,1)S(1)}, u32[]{:S(2)}, u32[]{:S(2)}) %collective-permute-start.9) | collective-permute-done | bytes 49184 | tf_op jit(solution)/shard_map/ppermute | solution.py:200
  81.0 2.9 %collective-permute-start.10 = (bf16[64,768]{1,0:T(8,128)(2,1)S(1)}, bf16[64,768]{1,0:T(8,128)(2,1)S(1)}, u32[]{:S(2)}, u32[]{:S(2)}) collective-permute-start(bf16[64,768]{1,0:T(8,128)(2,1)S(1)} %pad_maximum_fusion.2), channel_id=1, source_target_pairs={{0,4},{1,5},{2,6},{3,7},{4,0},{5,1},{6,2},{7,3},{8,12},{9,13},{10,... | collective-permute-start | bytes 294920 | tf_op jit(solution)/shard_map/ppermute | solution.py:200
  84.0 2.8 %collective-permute-done.10 = bf16[64,768]{1,0:T(8,128)(2,1)S(1)} collective-permute-done((bf16[64,768]{1,0:T(8,128)(2,1)S(1)}, bf16[64,768]{1,0:T(8,128)(2,1)S(1)}, u32[]{:S(2)}, u32[]{:S(2)}) %collective-permute-start.10) | collective-permute-done | bytes 98336 | tf_op jit(solution)/shard_map/ppermute | solution.py:200
  86.7 0.0 copy-start.1
  86.8 3.2 %collective-permute-start.11 = (bf16[128,768]{1,0:T(8,128)(2,1)S(1)}, bf16[128,768]{1,0:T(8,128)(2,1)S(1)}, u32[]{:S(2)}, u32[]{:S(2)}) collective-permute-start(bf16[128,768]{1,0:T(8,128)(2,1)S(1)} %pad_maximum_fusion.1), channel_id=1, source_target_pairs={{0,2},{1,3},{2,0},{3,1},{4,6},{5,7},{6,4},{7,5},{8,10},{9,11},{10,... | collective-permute-start | bytes 589832 | tf_op jit(solution)/shard_map/ppermute | solution.py:200
  90.0 3.6 %collective-permute-done.11 = bf16[128,768]{1,0:T(8,128)(2,1)S(1)} collective-permute-done((bf16[128,768]{1,0:T(8,128)(2,1)S(1)}, bf16[128,768]{1,0:T(8,128)(2,1)S(1)}, u32[]{:S(2)}, u32[]{:S(2)}) %collective-permute-start.11) | collective-permute-done | bytes 196640 | tf_op jit(solution)/shard_map/ppermute | solution.py:200
  93.7 1.5 %collective-permute-start.12 = (bf16[256,768]{1,0:T(8,128)(2,1)S(1)}, bf16[256,768]{1,0:T(8,128)(2,1)S(1)}, u32[]{:S(2)}, u32[]{:S(2)}) collective-permute-start(bf16[256,768]{1,0:T(8,128)(2,1)S(1)} %pad_maximum_fusion), channel_id=1, source_target_pairs={{0,16},{8,24},{16,0},{24,8},{1,17},{9,25},{17,1},{25,9},{2,18},{10... | collective-permute-start | bytes 1179656 | tf_op jit(solution)/shard_map/ppermute | solution.py:200
  95.3 6.2 %collective-permute-done.12 = bf16[256,768]{1,0:T(8,128)(2,1)S(1)} collective-permute-done((bf16[256,768]{1,0:T(8,128)(2,1)S(1)}, bf16[256,768]{1,0:T(8,128)(2,1)S(1)}, u32[]{:S(2)}, u32[]{:S(2)}) %collective-permute-start.12) | collective-permute-done | bytes 393248 | tf_op jit(solution)/shard_map/ppermute | solution.py:200
  101.5 0.1 constant_dynamic-update-slice_fusion
  101.6 0.1 collective-permute-start.13
  101.6 0.0 copy-done.1
  101.6 0.1 slice_bitcast_fusion
  101.7 1.3 collective-permute-start.3
  103.0 4.8 %collective-permute-start.2 = (bf16[1088,256]{1,0:T(8,128)(2,1)S(1)}, bf16[1088,256]{1,0:T(8,128)(2,1)S(1)}, u32[]{:S(2)}, u32[]{:S(2)}) collective-permute-start(bf16[1088,256]{1,0:T(8,128)(2,1)S(1)} %get-tuple-element.25), channel_id=1, source_target_pairs={{0,1},{1,2},{2,3},{3,4},{4,5},{5,6},{6,7},{8,9},{9,10},{10,11},{11... | collective-permute-start | bytes 1671176 | tf_op jit(solution)/shard_map/ppermute | solution.py:239
  107.8 8.4 %shard_map.77 = (bf16[17,2,64,256]{3,2,1,0:T(8,128)(2,1)}, f32[2,1088,256]{2,1,0:T(8,128)}) custom-call(bf16[17,2,64,256]{3,2,1,0:T(8,128)(2,1)} %bitcast.14, bf16[17,2,64,256]{3,2,1,0:T(8,128)(2,1)} %bitcast.20, bf16[2,1088,256]{2,1,0:T(8,128)(2,1)} %get-tuple-element.15.act, bf16[2,1088,256]{2,1,0:T(8,128)(2,1)} %get-tuple-element.16.pg, ...), custom_call_target="tpu_custom_call" | custom-call | flops 2566914048 | bytes 9371648 | tf_op jit(solution)/shard_map/pallas_call | solution.py:32
  116.2 2.5 %collective-permute-done.3.below = bf16[1088,256]{1,0:T(8,128)(2,1)S(1)} collective-permute-done((bf16[1088,256]{1,0:T(8,128)(2,1)S(1)}, bf16[1088,256]{1,0:T(8,128)(2,1)S(1)}, u32[]{:S(2)}, u32[]{:S(2)}) %collective-permute-start.3) | collective-permute-done | bytes 557088 | tf_op jit(solution)/shard_map/ppermute | solution.py:240
  118.6 0.0 copy-start.2
  118.6 11.2 %collective-permute-done.2.above = bf16[1088,256]{1,0:T(8,128)(2,1)S(1)} collective-permute-done((bf16[1088,256]{1,0:T(8,128)(2,1)S(1)}, bf16[1088,256]{1,0:T(8,128)(2,1)S(1)}, u32[]{:S(2)}, u32[]{:S(2)}) %collective-permute-start.2) | collective-permute-done | bytes 557088 | tf_op jit(solution)/shard_map/ppermute | solution.py:239
  129.8 0.0 copy-start.3
  129.8 0.0 copy-done.2
  129.8 0.8 copy-done.3
  130.6 5.6 %shard_map.78 = bf16[17,2,64,256]{3,2,1,0:T(8,128)(2,1)} custom-call(bf16[1088,256]{1,0:T(8,128)(2,1)} %copy-done.3, bf16[1088,256]{1,0:T(8,128)(2,1)} %copy-done.2, f32[2,1088,256]{2,1,0:T(8,128)} %get-tuple-element.18.back_loc, bf16[3,3,256,256]{3,2,1,0:T(8,128)(2,1)} %ws.7), custom_call_target="tpu_custom_call" | custom-call | flops 855638016 | bytes 5636096 | tf_op jit(solution)/shard_map/pallas_call | solution.py:32
  136.3 0.0 collective-permute-done.13
  136.3 0.1 constant_dynamic-update-slice_fusion.5.sums
  136.3 2.0 %shard_map.79 = (f32[3,3,256,256]{3,2,1,0:T(8,128)}, f32[3,256,256]{2,1,0:T(8,128)}) custom-call(s32[1]{0:T(128)} %bitcast.2.code, bf16[1024,768]{1,0:T(8,128)(2,1)S(1)} %constant_dynamic-update-slice_fusion.5.sums), custom_call_target="tpu_custom_call" | custom-call | bytes 4718596 | tf_op jit(solution)/shard_map/pallas_call | solution.py:32
  (14 shorter events, 0.2 us)
Async XLA Ops:
  1.9 28.7 %collective-permute-start = (bf16[1088,256]{1,0:T(8,128)(2,1)S(1)}, bf16[1088,256]{1,0:T(8,128)(2,1)S(1)}, u32[]{:S(2)}, u32[]{:S(2)}) collective-permute-start(bf16[1088,256]{1,0:T(8,128)(2,1)S(1)} %bitcast.17), channel_id=1, source_target_pairs={{0,1},{1,2},{2,3},{3,4},{4,5},{5,6},{6,7},{8,9},{9,10},{10,11},{11... | collective-permute-start | bytes 1671176 | tf_op jit(solution)/shard_map/ppermute | solution.py:239
  6.8 23.8 %collective-permute-start.1 = (bf16[1088,256]{1,0:T(8,128)(2,1)S(1)}, bf16[1088,256]{1,0:T(8,128)(2,1)S(1)}, u32[]{:S(2)}, u32[]{:S(2)}) collective-permute-start(bf16[1088,256]{1,0:T(8,128)(2,1)S(1)} %bitcast.16), channel_id=1, source_target_pairs={{1,0},{2,1},{3,2},{4,3},{5,4},{6,5},{7,6},{9,8},{10,9},{11,10},{12... | collective-permute-start | bytes 1671176 | tf_op jit(solution)/shard_map/ppermute | solution.py:240
  30.6 0.8 copy-start.4
  30.6 1.0 copy-start.5
  44.1 3.7 %copy-start = (bf16[1024,768]{1,0:T(8,128)(2,1)S(1)}, bf16[1024,768]{1,0:T(8,128)(2,1)}, u32[]{:S(2)}) copy-start(bf16[1024,768]{1,0:T(8,128)(2,1)} %get-tuple-element.19) | copy-start | bytes 4718596
  45.4 2.4 %collective-permute-start.4 = (bf16[512,768]{1,0:T(8,128)(2,1)S(1)}, bf16[512,768]{1,0:T(8,128)(2,1)S(1)}, u32[]{:S(2)}, u32[]{:S(2)}) collective-permute-start(bf16[512,768]{1,0:T(8,128)(2,1)S(1)} %slice.47), channel_id=1, source_target_pairs={{0,8},{8,0},{16,24},{24,16},{1,9},{9,1},{17,25},{25,17},{2,10},{10... | collective-permute-start | bytes 2359304 | tf_op jit(solution)/shard_map/ppermute | solution.py:200
  48.0 11.2 %collective-permute-start.5 = (bf16[256,768]{1,0:T(8,128)(2,1)S(1)}, bf16[256,768]{1,0:T(8,128)(2,1)S(1)}, u32[]{:S(2)}, u32[]{:S(2)}) collective-permute-start(bf16[256,768]{1,0:T(8,128)(2,1)S(1)} %slice.59), channel_id=1, source_target_pairs={{0,16},{8,24},{16,0},{24,8},{1,17},{9,25},{17,1},{25,9},{2,18},{10... | collective-permute-start | bytes 1179656 | tf_op jit(solution)/shard_map/ppermute | solution.py:200
  59.3 7.7 %collective-permute-start.6 = (bf16[128,768]{1,0:T(8,128)(2,1)S(1)}, bf16[128,768]{1,0:T(8,128)(2,1)S(1)}, u32[]{:S(2)}, u32[]{:S(2)}) collective-permute-start(bf16[128,768]{1,0:T(8,128)(2,1)S(1)} %slice.61), channel_id=1, source_target_pairs={{0,2},{1,3},{2,0},{3,1},{4,6},{5,7},{6,4},{7,5},{8,10},{9,11},{10,... | collective-permute-start | bytes 589832 | tf_op jit(solution)/shard_map/ppermute | solution.py:200
  67.1 5.6 %collective-permute-start.7 = (bf16[64,768]{1,0:T(8,128)(2,1)S(1)}, bf16[64,768]{1,0:T(8,128)(2,1)S(1)}, u32[]{:S(2)}, u32[]{:S(2)}) collective-permute-start(bf16[64,768]{1,0:T(8,128)(2,1)S(1)} %slice.63), channel_id=1, source_target_pairs={{0,4},{1,5},{2,6},{3,7},{4,0},{5,1},{6,2},{7,3},{8,12},{9,13},{10,... | collective-permute-start | bytes 294920 | tf_op jit(solution)/shard_map/ppermute | solution.py:200
  72.7 4.2 %collective-permute-start.8 = (bf16[32,768]{1,0:T(8,128)(2,1)S(1)}, bf16[32,768]{1,0:T(8,128)(2,1)S(1)}, u32[]{:S(2)}, u32[]{:S(2)}) collective-permute-start(bf16[32,768]{1,0:T(8,128)(2,1)S(1)} %slice.65), channel_id=1, source_target_pairs={{0,1},{1,0},{2,3},{3,2},{4,5},{5,4},{6,7},{7,6},{8,9},{9,8},{10,11... | collective-permute-start | bytes 147464 | tf_op jit(solution)/shard_map/ppermute | solution.py:200
  76.9 4.2 %collective-permute-start.9 = (bf16[32,768]{1,0:T(8,128)(2,1)S(1)}, bf16[32,768]{1,0:T(8,128)(2,1)S(1)}, u32[]{:S(2)}, u32[]{:S(2)}) collective-permute-start(bf16[32,768]{1,0:T(8,128)(2,1)S(1)} %get-tuple-element.23), channel_id=1, source_target_pairs={{0,1},{1,0},{2,3},{3,2},{4,5},{5,4},{6,7},{7,6},{8,9},{9,8},{10,11... | collective-permute-start | bytes 147464 | tf_op jit(solution)/shard_map/ppermute | solution.py:200
  81.0 5.7 %collective-permute-start.10 = (bf16[64,768]{1,0:T(8,128)(2,1)S(1)}, bf16[64,768]{1,0:T(8,128)(2,1)S(1)}, u32[]{:S(2)}, u32[]{:S(2)}) collective-permute-start(bf16[64,768]{1,0:T(8,128)(2,1)S(1)} %pad_maximum_fusion.2), channel_id=1, source_target_pairs={{0,4},{1,5},{2,6},{3,7},{4,0},{5,1},{6,2},{7,3},{8,12},{9,13},{10,... | collective-permute-start | bytes 294920 | tf_op jit(solution)/shard_map/ppermute | solution.py:200
  86.7 14.9 %copy-start.1 = (bf16[2,1088,256]{2,1,0:T(8,128)(2,1)S(1)}, bf16[2,1088,256]{2,1,0:T(8,128)(2,1)}, u32[]{:S(2)}) copy-start(bf16[2,1088,256]{2,1,0:T(8,128)(2,1)} %get-tuple-element.16.pg) | copy-start | bytes 3342340
  86.8 6.9 %collective-permute-start.11 = (bf16[128,768]{1,0:T(8,128)(2,1)S(1)}, bf16[128,768]{1,0:T(8,128)(2,1)S(1)}, u32[]{:S(2)}, u32[]{:S(2)}) collective-permute-start(bf16[128,768]{1,0:T(8,128)(2,1)S(1)} %pad_maximum_fusion.1), channel_id=1, source_target_pairs={{0,2},{1,3},{2,0},{3,1},{4,6},{5,7},{6,4},{7,5},{8,10},{9,11},{10,... | collective-permute-start | bytes 589832 | tf_op jit(solution)/shard_map/ppermute | solution.py:200
  93.7 7.8 %collective-permute-start.12 = (bf16[256,768]{1,0:T(8,128)(2,1)S(1)}, bf16[256,768]{1,0:T(8,128)(2,1)S(1)}, u32[]{:S(2)}, u32[]{:S(2)}) collective-permute-start(bf16[256,768]{1,0:T(8,128)(2,1)S(1)} %pad_maximum_fusion), channel_id=1, source_target_pairs={{0,16},{8,24},{16,0},{24,8},{1,17},{9,25},{17,1},{25,9},{2,18},{10... | collective-permute-start | bytes 1179656 | tf_op jit(solution)/shard_map/ppermute | solution.py:200
  101.6 34.7 %collective-permute-start.13 = (bf16[512,768]{1,0:T(8,128)(2,1)S(1)}, bf16[512,768]{1,0:T(8,128)(2,1)S(1)}, u32[]{:S(2)}, u32[]{:S(2)}) collective-permute-start(bf16[512,768]{1,0:T(8,128)(2,1)S(1)} %get-tuple-element.28), channel_id=1, source_target_pairs={{0,8},{8,0},{16,24},{24,16},{1,9},{9,1},{17,25},{25,17},{2,10},{10... | collective-permute-start | bytes 2359304 | tf_op jit(solution)/shard_map/ppermute | solution.py:200
  101.7 16.9 %collective-permute-start.3 = (bf16[1088,256]{1,0:T(8,128)(2,1)S(1)}, bf16[1088,256]{1,0:T(8,128)(2,1)S(1)}, u32[]{:S(2)}, u32[]{:S(2)}) collective-permute-start(bf16[1088,256]{1,0:T(8,128)(2,1)S(1)} %get-tuple-element.24), channel_id=1, source_target_pairs={{1,0},{2,1},{3,2},{4,3},{5,4},{6,5},{7,6},{9,8},{10,9},{11,10},{12... | collective-permute-start | bytes 1671176 | tf_op jit(solution)/shard_map/ppermute | solution.py:240
  103.0 26.8 %collective-permute-start.2 = (bf16[1088,256]{1,0:T(8,128)(2,1)S(1)}, bf16[1088,256]{1,0:T(8,128)(2,1)S(1)}, u32[]{:S(2)}, u32[]{:S(2)}) collective-permute-start(bf16[1088,256]{1,0:T(8,128)(2,1)S(1)} %get-tuple-element.25), channel_id=1, source_target_pairs={{0,1},{1,2},{2,3},{3,4},{4,5},{5,6},{6,7},{8,9},{9,10},{10,11},{11... | collective-permute-start | bytes 1671176 | tf_op jit(solution)/shard_map/ppermute | solution.py:239
  118.6 11.2 %copy-start.2 = (bf16[1088,256]{1,0:T(8,128)(2,1)}, bf16[1088,256]{1,0:T(8,128)(2,1)S(1)}, u32[]{:S(2)}) copy-start(bf16[1088,256]{1,0:T(8,128)(2,1)S(1)} %collective-permute-done.3.below) | copy-start | bytes 1671172
  129.8 0.8 copy-start.3

commit v2 on v1

v2 whole, which is shorter than its diff:
```python
import functools
import itertools
import math

import jax
import jax.numpy as jnp
from jax import lax
from jax.experimental import pallas as pl
from jax.experimental.pallas import tpu as pltpu
from jax.sharding import PartitionSpec as P

BF16 = jnp.bfloat16
F32 = jnp.float32
TILE_ROWS = 16
LATENT_PARTS = (0.7,)
GRAD_PARTS = (0.4, 0.7)
VMEM = pl.BlockSpec(memory_space=pltpu.VMEM)
SMEM = pl.BlockSpec(memory_space=pltpu.SMEM)


def mm(a, b):
    return jnp.dot(a, b, preferred_element_type=F32)


def mm_t(a, b):
    return lax.dot_general(a, b, (((1,), (1,)), ((), ())), preferred_element_type=F32)


def outer(a, b):
    return lax.dot_general(a, b, (((0,), (0,)), ((), ())), preferred_element_type=F32)


def keep(x):
    return pltpu.with_memory_space_constraint(x, pltpu.VMEM)


def call(kernel, outs, scratch, vmem_mb, flops, args, aliases=None):
    size = sum(a.size * a.dtype.itemsize for a in args)
    size += sum(math.prod(o.shape) * jnp.dtype(o.dtype).itemsize for o in outs)
    return pl.pallas_call(
        kernel,
        out_shape=outs,
        in_specs=[SMEM if a.dtype == jnp.int32 else VMEM for a in args],
        out_specs=[VMEM] * len(outs),
        scratch_shapes=scratch,
        input_output_aliases=aliases or {},
        compiler_params=pltpu.CompilerParams(vmem_limit_bytes=vmem_mb << 20),
        cost_estimate=pl.CostEstimate(flops=flops, bytes_accessed=size, transcendentals=0),
    )(*args)


def shift_right(tile):
    w = lax.broadcasted_iota(jnp.int32, tile.shape, 0)
    return jnp.where(w == 0, 0.0, pltpu.roll(tile, 1, 0))


def shift_left(tile):
    w = lax.broadcasted_iota(jnp.int32, tile.shape, 0)
    last = tile.shape[0] - 1
    return jnp.where(w == last, 0.0, pltpu.roll(tile, last, 0))


def row_of(ref, row, first=0, last=None):
    planes, _, cols, chans = ref.shape
    last = planes if last is None else last
    return ref[first:last, row].reshape((last - first) * cols, chans)


def first_kernel(shift, lat, cot, ws, wt, pre_loc, act_grad, taps, cot_pad):
    planes, rows, cols, chans = lat.shape
    cells = planes * cols
    for row in range(rows):
        for b in range(3):
            total = None
            for a in range(3):
                if 0 <= row + a - 1 < rows:
                    part = mm(row_of(lat, row + a - 1), ws[a, b])
                    total = part if total is None else total + part
            taps[b] = total

        @pl.loop(0, planes)
        def _(f):
            at = pl.ds(pl.multiple_of(f * cols, cols), cols)
            pre_loc[row, at] = shift_right(taps[0, at]) + taps[1, at] + shift_left(taps[2, at])

        cot_pad[:cells] = row_of(cot, row)
        cot_pad[cells:] = jnp.zeros((2 * shift, chans), BF16)
        total = mm_t(cot_pad[:cells], wt[0])
        total += mm_t(cot_pad[pl.ds(shift, cells)], wt[1])
        total += mm_t(cot_pad[pl.ds(2 * shift, cells)], wt[2])
        act_grad[row] = total.astype(BF16)


def grads_kernel(part, rows, shift, ends, scale, *refs):
    first, last, final = part
    refs = list(refs)
    code = refs.pop(0) if final else None
    lat, cot, above, below, pre_loc, act_grad, ws = refs[:7]
    refs = refs[7:]
    before = refs.pop(0) if first else None
    acts, pgs, outs = refs[:rows], refs[rows : 2 * rows], refs[2 * rows : 2 * rows + (2 if final else 1)]
    taps, ext, spread, cots, total = refs[2 * rows + len(outs) :]
    planes, _, cols, chans = lat.shape
    cells, base = (last - first) * cols, first * cols
    ext[0] = above[...]
    ext[rows + 1] = below[...]
    for row in range(rows):
        ext[row + 1] = row_of(lat, row, first, last)
        halos = []
        if row == 0:
            halos.append((0, above))
        if row == rows - 1:
            halos.append((2, below))
        for b in range(3):
            for n, (a, halo) in enumerate(halos):
                out = mm(halo[...], ws[a, b])
                taps[b] = out if n == 0 else taps[b] + out

        @pl.loop(0, last - first)
        def _(f):
            at = pl.ds(pl.multiple_of(f * cols, cols), cols)
            whole = pl.ds(pl.multiple_of(base + f * cols, cols), cols)
            pre = pre_loc[row, whole]
            if halos:
                pre += shift_right(taps[0, at]) + taps[1, at] + shift_left(taps[2, at])
            sig = 1.0 / (1.0 + jnp.exp(-pre))
            act = pre * sig
            acts[row][at] = act.astype(BF16)
            grad = act_grad[row, whole].astype(F32) * sig * (1.0 + pre - act)
            grad16 = grad.astype(BF16)
            pgs[row][at] = grad16
            grad = grad16.astype(F32)
            spread[row, at, :chans] = shift_left(grad).astype(BF16)
            spread[row, at, chans : 2 * chans] = grad16
            spread[row, at, 2 * chans :] = shift_right(grad).astype(BF16)

        for k in range(3):
            skip = k * shift // cols
            there = min(last + skip, planes) - (first + skip)
            if there > 0:
                cots[row, : there * cols, k * chans : (k + 1) * chans] = row_of(cot, row, first + skip, first + skip + there)
            there = max(there, 0) * cols
            if there < cells:
                cots[row, there:, k * chans : (k + 1) * chans] = jnp.zeros((cells - there, chans), BF16)
    wide = rows * cells
    target = total if final else outs[0]
    for n in range(4):
        if n < 3:
            out = outer(ext[n : n + rows].reshape(wide, chans), spread[...].reshape(wide, 3 * chans))
        else:
            out = outer(jnp.concatenate([a[...] for a in acts], 0), cots[...].reshape(wide, 3 * chans))
        at = slice(n * chans, (n + 1) * chans)
        target[at] = out if before is None else before[at] + out
    if final:
        size = 2 * chans // ends
        for half in range(2):
            for slot in range(ends):
                at = (half ^ code[0]) * 2 * chans + (slot ^ code[1]) * size
                out = total[pl.ds(pl.multiple_of(at, size), size)] * scale
                outs[half][slot * size : (slot + 1) * size] = out.astype(BF16)


def out_kernel(shift, rows, parts, lat, *refs):
    acts, (wt, block_out, act_pad) = refs[:-3], refs[-3:]
    planes, rows, cols, chans = lat.shape
    cells = planes * cols
    for row in range(rows):
        act_pad[: 2 * shift] = jnp.zeros((2 * shift, chans), BF16)
        for n, (first, last) in enumerate(parts):
            act_pad[2 * shift + first * cols : 2 * shift + last * cols] = acts[n * rows + row][...]
        mixed = mm(act_pad[pl.ds(2 * shift, cells)], wt[0])
        mixed += mm(act_pad[pl.ds(shift, cells)], wt[1])
        mixed += mm(act_pad[:cells], wt[2])
        mixed = mixed.astype(BF16).astype(F32).reshape(planes, cols, chans)
        block_out[:, row] = (lat[:, row].astype(F32) + mixed).astype(BF16)


def back_kernel(rows, parts, cot, *refs):
    pgs, (ws, back_loc, taps) = refs[:-3], refs[-3:]
    _, _, cols, chans = cot.shape
    for row in range(rows):
        for n, (first, last) in enumerate(parts):
            at = slice(first * cols, last * cols)
            for b in range(3):
                total = None
                for a in range(3):
                    if 0 <= row - a + 1 < rows:
                        out = mm_t(pgs[n * rows + row - a + 1][...], ws[a, b])
                        total = out if total is None else total + out
                taps[b, at] = total

        @pl.loop(0, cot.shape[0])
        def _(f):
            at = pl.ds(pl.multiple_of(f * cols, cols), cols)
            back = shift_left(taps[0, at]) + taps[1, at] + shift_right(taps[2, at])
            back_loc[row, at] = cot[f, row].astype(F32) + back


def last_kernel(parts, back_loc, ws, *refs):
    aboves, belows = refs[: len(parts)], refs[len(parts) : 2 * len(parts)]
    latents_grad, taps = refs[2 * len(parts) :]
    planes, rows, cols, chans = latents_grad.shape
    for row in range(rows):
        halos = []
        if row == 0:
            halos.append((2, aboves))
        if row == rows - 1:
            halos.append((0, belows))
        for b in range(3):
            for n, (a, pieces) in enumerate(halos):
                for (first, last), piece in zip(parts, pieces):
                    at = slice(first * cols, last * cols)
                    out = mm_t(piece[...], ws[a, b])
                    taps[b, at] = out if n == 0 else taps[b, at] + out

        @pl.loop(0, planes)
        def _(f):
            at = pl.ds(pl.multiple_of(f * cols, cols), cols)
            back = back_loc[row, at]
            if halos:
                back += shift_left(taps[0, at]) + taps[1, at] + shift_right(taps[2, at])
            latents_grad[f, row] = back.astype(BF16)


def order_kernel(ends, code, mine, other, spatial, temporal, total):
    chans = spatial.shape[-1]
    size = 2 * chans // ends
    for half, sums in enumerate((mine, other)):
        for slot in range(ends):
            at = (half ^ code[0]) * 2 * chans + (slot ^ code[1]) * size
            total[pl.ds(pl.multiple_of(at, size), size)] = sums[slot * size : (slot + 1) * size].astype(F32)
    for a in range(3):
        for b in range(3):
            spatial[a, b] = total[a * chans : (a + 1) * chans, b * chans : (b + 1) * chans]
    for k in range(3):
        temporal[k] = total[3 * chans :, k * chans : (k + 1) * chans]


def bits_of(axis):
    count = lax.axis_size(axis)
    return [(axis, 1 << n) for n in range(count.bit_length()) if 1 << n < count]


def send(x, steps):
    wide, tall = lax.axis_size("dp"), lax.axis_size("tm")
    mask = sum(bit * tall if axis == "dp" else bit for axis, bit in steps)
    return lax.ppermute(x, ("dp", "tm"), [(i, i ^ mask) for i in range(wide * tall)])


def plus(x, *others):
    total = x.astype(F32)
    for other in others:
        total = total + other.astype(F32)
    return total.astype(BF16)


def groups_of(rows):
    wide, tall = bits_of("dp")[1:], bits_of("tm")
    order = [x for pair in zip(wide, tall[1:]) for x in pair]
    order += wide[len(tall) - 1 :] + tall[1 + len(wide) :] + tall[:1]
    groups, ends = [], 1
    while order:
        group, order = order[:2], order[2:]
        split = rows % (TILE_ROWS * ends << len(group)) == 0
        ends = ends << len(group) if split else ends
        groups.append((group, split))
    return groups, ends


def codes(groups):
    def bit_at(step):
        return (lax.axis_index(step[0]) // step[1]) % 2

    word = 0
    for group, split in groups:
        for step in group if split else ():
            word = 2 * word + bit_at(step)
    return jnp.stack([jnp.asarray(x, jnp.int32) for x in (bit_at(("dp", 1)), word)])


def subsets(group):
    return [[s for n, s in enumerate(group) if k >> (len(group) - 1 - n) & 1] for k in range(1, 1 << len(group))]


def add_up(mine, other, groups, beside, there, last):
    core = [("dp", 1)]
    mine = plus(mine, send(other, core))
    plan = [(group, split, True) for group, split in groups]
    plan += [(group, split, False) for group, split in reversed(groups) if split]
    for n, (group, split, down) in enumerate(plan):
        others = subsets(group)
        size = mine.shape[0] // (len(others) + 1) if split and down else 0
        got = [send(mine[(k + 1) * size : (k + 2) * size] if size else mine, steps) for k, steps in enumerate(others)]
        if n < len(plan) - 1:
            got, also = lax.optimization_barrier((got, beside[n]() if n < len(beside) else ()))
            there += [also] if also else []
        else:
            there += [run() for run in beside[n:]]
            got, end = lax.optimization_barrier((got, last()))
        mine = plus(mine[:size] if size else mine, *got) if down else jnp.concatenate([mine, *got], axis=0)
    return mine, send(mine, core), end


def halo(first, last):
    ends = lax.axis_size("tm") - 1
    above = lax.ppermute(last, "tm", [(i, i + 1) for i in range(ends)])
    below = lax.ppermute(first, "tm", [(i + 1, i) for i in range(ends)])
    return above, below


def body(latents, cotangent, spatial_weight, temporal_weight):
    clips, frames, rows, cols, chans = latents.shape
    planes, shift = frames * clips, clips * cols
    cells = planes * cols
    lat = jnp.swapaxes(latents, 0, 1).reshape(planes, rows, cols, chans)
    cot = jnp.swapaxes(cotangent, 0, 1).reshape(planes, rows, cols, chans)
    scale = (clips * lax.axis_size("dp") * frames * rows * lax.axis_size("tm") * cols) ** (-0.5)
    groups, ends = groups_of(2 * chans)
    code = codes(groups)
    unit = 2 * cells * chans * chans
    def cut(places):
        cuts = [0] + [round(planes * place) for place in places] + [planes]
        return list(zip(cuts[:-1], cuts[1:]))

    parts = cut(LATENT_PARTS)
    def ends_of(x, i, j):
        return x[i:j, 0].reshape(-1, chans), x[i:j, rows - 1].reshape(-1, chans)

    halos = [halo(*ends_of(lat, *parts[0]))]
    taps = pltpu.VMEM((3, cells, chans), F32)
    padded = pltpu.VMEM((cells + 2 * shift, chans), BF16)
    pre_loc, act_grad = call(
        functools.partial(first_kernel, shift),
        [pltpu.VMEM((rows, cells, chans), F32), pltpu.VMEM((rows, cells, chans), BF16)],
        [taps, padded], 28, (9 * rows - 6 + 3 * rows) * unit,
        [lat, cot, spatial_weight, temporal_weight],
    )
    rest, act_grad = lax.optimization_barrier((lat, act_grad))
    halos += [halo(*ends_of(rest, *part)) for part in parts[1:]]
    acts, pgs, total = [], [], None
    for n, (i, j) in enumerate(parts):
        final = n == len(parts) - 1
        size = (j - i) * cols
        narrow = jax.ShapeDtypeStruct((size, chans), BF16)
        if final:
            outs = [jax.ShapeDtypeStruct((2 * chans, 3 * chans), BF16)] * 2
        else:
            outs = [pltpu.VMEM((4 * chans, 3 * chans), F32)]
        args = [code] if final else []
        args += [keep(lat), keep(cot), keep(halos[n][0]), keep(halos[n][1]), keep(pre_loc), keep(act_grad)]
        args += [keep(spatial_weight)] + ([keep(total)] if n else [])
        done = call(
            functools.partial(grads_kernel, (i, j, final), rows, shift, ends, scale),
            [narrow] * (2 * rows) + outs,
            [
                pltpu.VMEM((3, size, chans), F32),
                pltpu.VMEM((rows + 2, size, chans), BF16),
                pltpu.VMEM((rows, size, 3 * chans), BF16),
                pltpu.VMEM((rows, size, 3 * chans), BF16),
                pltpu.VMEM((4 * chans, 3 * chans), F32),
            ],
            28, (6 + 12 * rows) * unit * (j - i) // planes, args,
        )
        acts += done[:rows]
        pgs += done[rows : 2 * rows]
        total = done[2 * rows]
    image = jax.ShapeDtypeStruct(lat.shape, BF16)
    grad_parts = cut(GRAD_PARTS)

    def grad_halo(i, j):
        def piece(row):
            found = [
                pgs[n * rows + row][(max(i, first) - first) * cols : (min(j, last) - first) * cols]
                for n, (first, last) in enumerate(parts)
                if max(i, first) < min(j, last)
            ]
            return found[0] if len(found) == 1 else jnp.concatenate(found, axis=0)

        return halo(piece(0), piece(rows - 1))

    def out():
        return call(
            functools.partial(out_kernel, shift, rows, parts), [image], [padded], 28, 3 * rows * unit,
            [lat, *acts, temporal_weight],
        )[0]

    def back():
        return call(
            functools.partial(back_kernel, rows, parts), [jax.ShapeDtypeStruct((rows, cells, chans), F32)], [taps], 28,
            (9 * rows - 6) * unit, [cot, *pgs, spatial_weight],
        )[0]

    works = [out, back]
    beside = [
        lambda part=part, work=work: (grad_halo(*part), work and work())
        for part, work in itertools.zip_longest(grad_parts, works)
    ]
    there = []

    def last():
        pg_halos = [pair for pair, _ in there]
        return call(
            functools.partial(last_kernel, grad_parts), [image], [taps], 28, 6 * unit,
            [there[1][1], spatial_weight, *(h[0] for h in pg_halos), *(h[1] for h in pg_halos)],
        )[0]

    mine, other, latents_grad = add_up(done[2 * rows], done[2 * rows + 1], groups, beside, there, last)
    block_out = there[0][1]
    spatial_grad, temporal_grad = call(
        functools.partial(order_kernel, ends),
        [jax.ShapeDtypeStruct((3, 3, chans, chans), F32), jax.ShapeDtypeStruct((3, chans, chans), F32)],
        [pltpu.VMEM((4 * chans, 3 * chans), F32)], 28, 0, [code, mine, other],
    )

    def home(x):
        return jnp.swapaxes(x.reshape(frames, clips, rows, cols, chans), 0, 1)

    return home(block_out), home(latents_grad), spatial_grad, temporal_grad


def solution(mesh):
    in_specs = (P("dp", None, "tm", None, None), P("dp", None, "tm", None, None), P(), P())
    out_specs = (P("dp", None, "tm", None, None), P("dp", None, "tm", None, None), P(), P())
    return jax.shard_map(body, mesh=mesh, in_specs=in_specs, out_specs=out_specs, check_vma=False)
```

time: 139 us -> 102 us (0.73)
  waiting for transfers between devices: 65.6 us -> 11.2 us
  starting transfers between devices: 30.3 us -> 51.9 us
  Pallas kernels: 36.4 us -> 26.2 us
  local copies, waits for them, and re-layouts: 4.69 us -> 10.9 us
    ppermute x10 -> x14, waiting for transfers between devices: 37.5 us -> 10.3 us  [send(): lax.ppermute(x, ('dp', 'tm'), [(i, i ^ mask) for i in range(wide * tall)])]
    ppermute x2 -> x5, waiting for transfers between devices: 25.6 us -> 0.9 us  [halo(): above = lax.ppermute(last, 'tm', [(i, i + 1) for i in range(ends)])]
    ppermute x2 -> x5, starting transfers between devices: 9.67 us -> 25.1 us  [halo(): above = lax.ppermute(last, 'tm', [(i, i + 1) for i in range(ends)])]
    pallas_call x5 -> x7, Pallas kernels: 36.4 us -> 26.2 us  [call(): pl.pallas_call(kernel, out_shape=outs, in_specs=[SMEM if a.dtype == jnp.i...]
    unnamed x16 -> x31, local copies, waits for them, and re-layouts: 1.85 us -> 7.8 us
    ppermute x2 -> x5, starting transfers between devices: 2.58 us -> 6.43 us  [halo(): below = lax.ppermute(first, 'tm', [(i + 1, i) for i in range(ends)])]
    ppermute x2 -> x5, waiting for transfers between devices: 2.48 us -> 0.01 us  [halo(): below = lax.ppermute(first, 'tm', [(i + 1, i) for i in range(ends)])]
    ppermute x10 -> x14, starting transfers between devices: 18.1 us -> 20.3 us  [send(): lax.ppermute(x, ('dp', 'tm'), [(i, i ^ mask) for i in range(wide * tall)])]
  transfers between devices with their start and end apart: 14 -> 24, of which waited for: 12 -> 7; matrix products, arithmetic and copies ran while one was open for 0% -> 1% of each run, Pallas kernels for 16% -> 19%
where the time goes in v2:
time: 102 us
  starting transfers between devices  51.9 us (51%)
  Pallas kernels  26.2 us (26%)
  waiting for transfers between devices  11.2 us (11%)
  local copies, waits for them, and re-layouts  10.9 us (11%)
  between operations  1.11 us (1%)
    pallas_call x7, Pallas kernels, call(): pl.pallas_call(kernel, out_shape=outs, in_specs=[SMEM if a.dtype == jnp.i...  26.2 us
    ppermute x5, starting transfers between devices, halo(): above = lax.ppermute(last, 'tm', [(i, i + 1) for i in range(ends)])  25.1 us
    ppermute x14, starting transfers between devices, send(): lax.ppermute(x, ('dp', 'tm'), [(i, i ^ mask) for i in range(wide * tall)])  20.3 us
    ppermute x14, waiting for transfers between devices, send(): lax.ppermute(x, ('dp', 'tm'), [(i, i ^ mask) for i in range(wide * tall)])  10.3 us
    unnamed x31, local copies, waits for them, and re-layouts  7.8 us
    ppermute x5, starting transfers between devices, halo(): below = lax.ppermute(first, 'tm', [(i + 1, i) for i in range(ends)])  6.43 us
    slice x2, local copies, waits for them, and re-layouts, ends_of(): return (x[i:j, 0].reshape(-1, chans), x[i:j, rows - 1].reshape(-1, chans))  2.92 us
  transfers between devices with their start and end apart: 24, of which 7 were waited for; matrix products, arithmetic and copies ran while one was open for 1% of the time, Pallas kernels for 19%

profile of v2, /device:TPU:0, one launch (start us, length us, event | category | flops | bytes accessed | tf_op | source)
XLA Modules:
  0.0 101.7 jit_solution(6235642303202843567)
XLA Ops:
  0.6 0.0 copy-start.11
  0.7 2.2 %fusion = (bf16[12,1,64,256]{3,2,1,0:T(8,128)(2,1)}, bf16[12,1,64,256]{3,2,1,0:T(8,128)(2,1)}) fusion(bf16[17,2,64,256]{3,2,1,0:T(8,128)(2,1)} %bitcast.10), kind=kLoop, calls=%fused_computation.12 | loop fusion | bytes 1572864 | tf_op jit(solution)/shard_map/slice | solution.py:327
  2.8 5.6 %collective-permute-start.2 = (bf16[768,256]{1,0:T(8,128)(2,1)}, bf16[768,256]{1,0:T(8,128)(2,1)}, u32[]{:S(2)}, u32[]{:S(2)}) collective-permute-start(bf16[768,256]{1,0:T(8,128)(2,1)} %bitcast.6), channel_id=1, source_target_pairs={{0,1},{1,2},{2,3},{3,4},{4,5},{5,6},{6,7},{8,9},{9,10},{10,11},{11... | collective-permute-start | bytes 1179656 | tf_op jit(solution)/shard_map/ppermute | solution.py:306
  8.4 1.3 %collective-permute-start.3 = (bf16[768,256]{1,0:T(8,128)(2,1)}, bf16[768,256]{1,0:T(8,128)(2,1)}, u32[]{:S(2)}, u32[]{:S(2)}) collective-permute-start(bf16[768,256]{1,0:T(8,128)(2,1)} %bitcast.7), channel_id=1, source_target_pairs={{1,0},{2,1},{3,2},{4,3},{5,4},{6,5},{7,6},{9,8},{10,9},{11,10},{12... | collective-permute-start | bytes 1179656 | tf_op jit(solution)/shard_map/ppermute | solution.py:307
  9.8 0.0 copy-start.1
  9.8 1.3 %copy-done.1 = bf16[3,3,256,256]{3,2,1,0:T(8,128)(2,1)S(1)} copy-done((bf16[3,3,256,256]{3,2,1,0:T(8,128)(2,1)S(1)}, bf16[3,3,256,256]{3,2,1,0:T(8,128)(2,1)}, u32[]{:S(2)}) %copy-start.1) | copy-done | bytes 1179672
  11.0 1.2 %copy-done.6 = bf16[1,17,2,64,256]{4,3,2,1,0:T(8,128)(2,1)S(1)} copy-done((bf16[1,17,2,64,256]{4,3,2,1,0:T(8,128)(2,1)S(1)}, bf16[1,17,2,64,256]{4,3,2,1,0:T(8,128)(2,1)}, u32[]{:S(2)}) %copy-start.6) | copy-done | bytes 1114136
  12.3 4.9 %shard_map.75 = (f32[2,1088,256]{2,1,0:T(8,128)S(1)}, bf16[2,1088,256]{2,1,0:T(8,128)(2,1)S(1)}) custom-call(bf16[17,2,64,256]{3,2,1,0:T(8,128)(2,1)S(1)} %bitcast.11, bf16[17,2,64,256]{3,2,1,0:T(8,128)(2,1)S(1)} %bitcast.16, bf16[3,3,256,256]{3,2,1,0:T(8,128)(2,1)S(1)} %copy-done.1, bf16[3,256,256]{2,1,0:T(8,128)(2,1)S(1)} %copy-done.11), custom_call_target="tpu_custom_call" | custom-call | flops 2566914048 | bytes 7143424 | tf_op jit(solution)/shard_map/pallas_call | solution.py:40
  17.2 0.0 copy-start.3
  17.2 1.4 %copy-done.3 = f32[2,1088,256]{2,1,0:T(8,128)} copy-done((f32[2,1088,256]{2,1,0:T(8,128)}, f32[2,1088,256]{2,1,0:T(8,128)S(1)}, u32[]{:S(2)}) %copy-start.3) | copy-done | bytes 2228248
  18.5 1.0 copy-done.8
  19.5 0.7 fusion.1
  20.3 5.2 %collective-permute-start = (bf16[320,256]{1,0:T(8,128)(2,1)}, bf16[320,256]{1,0:T(8,128)(2,1)}, u32[]{:S(2)}, u32[]{:S(2)}) collective-permute-start(bf16[320,256]{1,0:T(8,128)(2,1)} %bitcast.4), channel_id=1, source_target_pairs={{0,1},{1,2},{2,3},{3,4},{4,5},{5,6},{6,7},{8,9},{9,10},{10,11},{11... | collective-permute-start | bytes 491528 | tf_op jit(solution)/shard_map/ppermute | solution.py:306
  25.5 1.3 %collective-permute-start.1 = (bf16[320,256]{1,0:T(8,128)(2,1)}, bf16[320,256]{1,0:T(8,128)(2,1)}, u32[]{:S(2)}, u32[]{:S(2)}) collective-permute-start(bf16[320,256]{1,0:T(8,128)(2,1)} %bitcast.5), channel_id=1, source_target_pairs={{1,0},{2,1},{3,2},{4,3},{5,4},{6,5},{7,6},{9,8},{10,9},{11,10},{12... | collective-permute-start | bytes 491528 | tf_op jit(solution)/shard_map/ppermute | solution.py:307
  26.9 0.1 pad_add_fusion.refs_0_.code
  26.9 0.0 collective-permute-done.2.refs_2_
  26.9 0.0 collective-permute-done.3.refs_3_
  27.0 0.0 copy-start.4
  27.0 1.6 %copy-done.4 = f32[2,1088,256]{2,1,0:T(8,128)S(1)} copy-done((f32[2,1088,256]{2,1,0:T(8,128)S(1)}, f32[2,1088,256]{2,1,0:T(8,128)}, u32[]{:S(2)}) %copy-start.4) | copy-done | bytes 2228248
  28.6 1.2 %copy-done.9 = bf16[2,1088,256]{2,1,0:T(8,128)(2,1)S(1)} copy-done((bf16[2,1088,256]{2,1,0:T(8,128)(2,1)S(1)}, bf16[2,1088,256]{2,1,0:T(8,128)(2,1)}, u32[]{:S(2)}) %copy-start.9) | copy-done | bytes 1114136
  29.8 6.5 %shard_map.76 = (bf16[768,256]{1,0:T(8,128)(2,1)S(1)}, bf16[768,256]{1,0:T(8,128)(2,1)S(1)}, bf16[768,256]{1,0:T(8,128)(2,1)S(1)}, bf16[768,256]{1,0:T(8,128)(2,1)S(1)}, f32[1024,768]{1,0:T(8,128)S(1)}) custom-call(bf16[17,2,64,256]{3,2,1,0:T(8,128)(2,1)S(1)} %bitcast.13, bf16[17,2,64,256]{3,2,1,0:T(8,128)(2,1)S(1)} %bitcast.17, ...), custom_call_target="tpu_custom_call" | custom-call | flops 3019898880 | bytes 12255232 | tf_op jit(solution)/shard_map/pallas_call | solution.py:40
  36.4 0.0 collective-permute-done.refs_3_
  36.4 0.0 collective-permute-done.1.refs_4_
  36.4 4.0 %shard_map.77 = (bf16[320,256]{1,0:T(8,128)(2,1)S(1)}, bf16[320,256]{1,0:T(8,128)(2,1)S(1)}, bf16[320,256]{1,0:T(8,128)(2,1)S(1)}, bf16[320,256]{1,0:T(8,128)(2,...) custom-call(s32[2]{0:T(128)S(1)} %pad_add_fusion.refs_0_.code, bf16[17,2,64,256]{3,2,1,0:T(8,128)(2,1)S(1)} %bitcast.14, ...), custom_call_target="tpu_custom_call" | custom-call | flops 1258291200 | bytes 12451848 | tf_op jit(solution)/shard_map/pallas_call | solution.py:40
  40.4 0.1 collective-permute-start.4
  40.5 1.3 %collective-permute-start.9 = (bf16[448,256]{1,0:T(8,128)(2,1)S(1)}, bf16[448,256]{1,0:T(8,128)(2,1)S(1)}, u32[]{:S(2)}, u32[]{:S(2)}) collective-permute-start(bf16[448,256]{1,0:T(8,128)(2,1)S(1)} %slice.56), channel_id=1, source_target_pairs={{1,0},{2,1},{3,2},{4,3},{5,4},{6,5},{7,6},{9,8},{10,9},{11,10},{12... | collective-permute-start | bytes 688136 | tf_op jit(solution)/shard_map/ppermute | solution.py:307
  41.8 5.2 %collective-permute-start.8 = (bf16[448,256]{1,0:T(8,128)(2,1)S(1)}, bf16[448,256]{1,0:T(8,128)(2,1)S(1)}, u32[]{:S(2)}, u32[]{:S(2)}) collective-permute-start(bf16[448,256]{1,0:T(8,128)(2,1)S(1)} %slice.55), channel_id=1, source_target_pairs={{0,1},{1,2},{2,3},{3,4},{4,5},{5,6},{6,7},{8,9},{9,10},{10,11},{11... | collective-permute-start | bytes 688136 | tf_op jit(solution)/shard_map/ppermute | solution.py:306
  47.0 0.0 collective-permute-done.4
  47.0 0.2 add_convert_fusion
  47.2 0.0 copy-start.12
  47.3 5.2 %collective-permute-start.7 = (bf16[128,768]{1,0:T(8,128)(2,1)S(1)}, bf16[128,768]{1,0:T(8,128)(2,1)S(1)}, u32[]{:S(2)}, u32[]{:S(2)}) collective-permute-start(bf16[128,768]{1,0:T(8,128)(2,1)S(1)} %get-tuple-element.86), channel_id=1, source_target_pairs={{0,18},{1,19},{2,16},{3,17},{4,22},{5,23},{6,20},{7,21},{8,26},{9,... | collective-permute-start | bytes 589832 | tf_op jit(solution)/shard_map/ppermute | solution.py:247
  52.5 0.5 collective-permute-start.6
  53.0 0.1 collective-permute-start.5
  53.1 2.1 %shard_map.78 = bf16[17,2,64,256]{3,2,1,0:T(8,128)(2,1)} custom-call(bf16[17,2,64,256]{3,2,1,0:T(8,128)(2,1)S(1)} %bitcast.15, bf16[768,256]{1,0:T(8,128)(2,1)S(1)} %get-tuple-element.51.refs_0_, bf16[768,256]{1,0:T(8,128)(2,1)S(1)} %get-tuple-element.52.refs_1_, bf16[320,256]{1,0:T(8,128)(2,1)S(1)} %get-tuple-element.53.refs_2_, ...), custom_call_target="tpu_custom_call" | custom-call | flops 855638016 | bytes 3735552 | tf_op jit(solution)/shard_map/pallas_call | solution.py:40
  55.2 0.0 collective-permute-done.9.refs_3_
  55.2 1.3 %collective-permute-start.14 = (bf16[320,256]{1,0:T(8,128)(2,1)S(1)}, bf16[320,256]{1,0:T(8,128)(2,1)S(1)}, u32[]{:S(2)}, u32[]{:S(2)}) collective-permute-start(bf16[320,256]{1,0:T(8,128)(2,1)S(1)} %slice.63), channel_id=1, source_target_pairs={{1,0},{2,1},{3,2},{4,3},{5,4},{6,5},{7,6},{9,8},{10,9},{11,10},{12... | collective-permute-start | bytes 491528 | tf_op jit(solution)/shard_map/ppermute | solution.py:307
  56.5 0.9 collective-permute-done.8.refs_0_
  57.4 4.5 %collective-permute-start.13 = (bf16[320,256]{1,0:T(8,128)(2,1)S(1)}, bf16[320,256]{1,0:T(8,128)(2,1)S(1)}, u32[]{:S(2)}, u32[]{:S(2)}) collective-permute-start(bf16[320,256]{1,0:T(8,128)(2,1)S(1)} %slice.62), channel_id=1, source_target_pairs={{0,1},{1,2},{2,3},{3,4},{4,5},{5,6},{6,7},{8,9},{9,10},{10,11},{11... | collective-permute-start | bytes 491528 | tf_op jit(solution)/shard_map/ppermute | solution.py:306
  61.9 0.9 collective-permute-done.6
  62.9 0.0 collective-permute-done.5
  62.9 0.1 add_convert_fusion.1
  63.0 4.9 %collective-permute-start.12 = (bf16[32,768]{1,0:T(8,128)(2,1)S(1)}, bf16[32,768]{1,0:T(8,128)(2,1)S(1)}, u32[]{:S(2)}, u32[]{:S(2)}) collective-permute-start(bf16[32,768]{1,0:T(8,128)(2,1)S(1)} %get-tuple-element.89), channel_id=1, source_target_pairs={{0,5},{1,4},{2,7},{3,6},{4,1},{5,0},{6,3},{7,2},{8,13},{9,12},{10,... | collective-permute-start | bytes 147464 | tf_op jit(solution)/shard_map/ppermute | solution.py:247
  67.8 0.3 collective-permute-start.11
  68.2 0.7 collective-permute-start.10
  68.9 3.1 %shard_map.79.back_loc = f32[2,1088,256]{2,1,0:T(8,128)S(1)} custom-call(bf16[17,2,64,256]{3,2,1,0:T(8,128)(2,1)S(1)} %bitcast.19, bf16[768,256]{1,0:T(8,128)(2,1)S(1)} %get-tuple-element.50.refs_0_, bf16[768,256]{1,0:T(8,128)(2,1)S(1)} %get-tuple-element.49.refs_1_, bf16[320,256]{1,0:T(8,128)(2,1)S(1)} %get-tuple-element.59.refs_2_, ...), custom_call_target="tpu_custom_call" | custom-call | flops 1711276032 | bytes 5636096 | tf_op jit(solution)/shard_map/pallas_call | solution.py:40
  72.0 0.0 collective-permute-done.14.refs_4_
  72.0 1.3 %collective-permute-start.19 = (bf16[320,256]{1,0:T(8,128)(2,1)S(1)}, bf16[320,256]{1,0:T(8,128)(2,1)S(1)}, u32[]{:S(2)}, u32[]{:S(2)}) collective-permute-start(bf16[320,256]{1,0:T(8,128)(2,1)S(1)} %get-tuple-element.59.refs_2_), channel_id=1, source_target_pairs={{1,0},{2,1},{3,2},{4,3},{5,4},{6,5},{7,6},{9,8},{10,9},{11,10},{12... | collective-permute-start | bytes 491528 | tf_op jit(solution)/shard_map/ppermute | solution.py:307
  73.3 4.6 %collective-permute-start.18 = (bf16[320,256]{1,0:T(8,128)(2,1)S(1)}, bf16[320,256]{1,0:T(8,128)(2,1)S(1)}, u32[]{:S(2)}, u32[]{:S(2)}) collective-permute-start(bf16[320,256]{1,0:T(8,128)(2,1)S(1)} %get-tuple-element.60.refs_3_), channel_id=1, source_target_pairs={{0,1},{1,2},{2,3},{3,4},{4,5},{5,6},{6,7},{8,9},{9,10},{10,11},{11... | collective-permute-start | bytes 491528 | tf_op jit(solution)/shard_map/ppermute | solution.py:306
  77.9 0.0 collective-permute-done.12
  77.9 0.0 collective-permute-done.11
  78.0 4.3 %collective-permute-start.17 = (bf16[32,768]{1,0:T(8,128)(2,1)S(1)}, bf16[32,768]{1,0:T(8,128)(2,1)S(1)}, u32[]{:S(2)}, u32[]{:S(2)}) collective-permute-start(bf16[32,768]{1,0:T(8,128)(2,1)S(1)} %get-tuple-element.81), channel_id=1, source_target_pairs={{0,5},{1,4},{2,7},{3,6},{4,1},{5,0},{6,3},{7,2},{8,13},{9,12},{10,... | collective-permute-start | bytes 147464 | tf_op jit(solution)/shard_map/ppermute | solution.py:247
  82.3 0.3 collective-permute-start.16
  82.6 0.3 collective-permute-start.15
  82.9 2.5 %collective-permute-done.17 = bf16[32,768]{1,0:T(8,128)(2,1)S(1)} collective-permute-done((bf16[32,768]{1,0:T(8,128)(2,1)S(1)}, bf16[32,768]{1,0:T(8,128)(2,1)S(1)}, u32[]{:S(2)}, u32[]{:S(2)}) %collective-permute-start.17) | collective-permute-done | bytes 49184 | tf_op jit(solution)/shard_map/ppermute | solution.py:247
  85.4 1.9 %collective-permute-done.16 = bf16[32,768]{1,0:T(8,128)(2,1)S(1)} collective-permute-done((bf16[32,768]{1,0:T(8,128)(2,1)S(1)}, bf16[32,768]{1,0:T(8,128)(2,1)S(1)}, u32[]{:S(2)}, u32[]{:S(2)}) %collective-permute-start.16) | collective-permute-done | bytes 49184 | tf_op jit(solution)/shard_map/ppermute | solution.py:247
  87.3 2.0 %collective-permute-start.22 = (bf16[128,768]{1,0:T(8,128)(2,1)S(1)}, bf16[128,768]{1,0:T(8,128)(2,1)S(1)}, u32[]{:S(2)}, u32[]{:S(2)}) collective-permute-start(bf16[128,768]{1,0:T(8,128)(2,1)S(1)} %pad_maximum_fusion), channel_id=1, source_target_pairs={{0,18},{1,19},{2,16},{3,17},{4,22},{5,23},{6,20},{7,21},{8,26},{9,... | collective-permute-start | bytes 589832 | tf_op jit(solution)/shard_map/ppermute | solution.py:247
  89.3 0.5 collective-permute-start.21
  89.8 1.0 collective-permute-start.20
  90.9 3.1 %shard_map.80 = bf16[17,2,64,256]{3,2,1,0:T(8,128)(2,1)} custom-call(f32[2,1088,256]{2,1,0:T(8,128)S(1)} %shard_map.79.back_loc, bf16[3,3,256,256]{3,2,1,0:T(8,128)(2,1)S(1)} %copy-done.2, bf16[448,256]{1,0:T(8,128)(2,1)S(1)} %collective-permute-done.8.refs_0_, bf16[320,256]{1,0:T(8,128)(2,1)S(1)} %collective-permute-done.13.refs_1_, ...), custom_call_target="tpu_custom_call" | custom-call | flops 855638016 | bytes 5636096 | tf_op jit(solution)/shard_map/pallas_call | solution.py:40
  94.0 1.2 %collective-permute-done.22 = bf16[128,768]{1,0:T(8,128)(2,1)S(1)} collective-permute-done((bf16[128,768]{1,0:T(8,128)(2,1)S(1)}, bf16[128,768]{1,0:T(8,128)(2,1)S(1)}, u32[]{:S(2)}, u32[]{:S(2)}) %collective-permute-start.22) | collective-permute-done | bytes 196640 | tf_op jit(solution)/shard_map/ppermute | solution.py:247
  95.2 1.5 %collective-permute-done.21 = bf16[128,768]{1,0:T(8,128)(2,1)S(1)} collective-permute-done((bf16[128,768]{1,0:T(8,128)(2,1)S(1)}, bf16[128,768]{1,0:T(8,128)(2,1)S(1)}, u32[]{:S(2)}, u32[]{:S(2)}) %collective-permute-start.21) | collective-permute-done | bytes 196640 | tf_op jit(solution)/shard_map/ppermute | solution.py:247
  96.8 0.1 collective-permute-start.23
  96.9 2.3 %collective-permute-done.23.other = bf16[512,768]{1,0:T(8,128)(2,1)S(1)} collective-permute-done((bf16[512,768]{1,0:T(8,128)(2,1)S(1)}, bf16[512,768]{1,0:T(8,128)(2,1)S(1)}, u32[]{:S(2)}, u32[]{:S(2)}) %collective-permute-start.23) | collective-permute-done | bytes 786464 | tf_op jit(solution)/shard_map/ppermute | solution.py:247
  99.2 2.6 %shard_map.81 = (f32[3,3,256,256]{3,2,1,0:T(8,128)}, f32[3,256,256]{2,1,0:T(8,128)}) custom-call(s32[2]{0:T(128)S(1)} %pad_add_fusion.refs_0_.code, bf16[512,768]{1,0:T(8,128)(2,1)S(1)} %constant_dynamic-update-slice_fusion.mine, bf16[512,768]{1,0:T(8,128)(2,1)S(1)} %collective-permute-done.23.other), custom_call_target="tpu_custom_call" | custom-call | bytes 4718600 | tf_op jit(solution)/shard_map/pallas_call | solution.py:40
  (36 shorter events, 0.3 us)
Async XLA Ops:
  0.6 9.1 %copy-start = (bf16[1,17,2,64,256]{4,3,2,1,0:T(8,128)(2,1)S(1)}, bf16[1,17,2,64,256]{4,3,2,1,0:T(8,128)(2,1)}, u32[]{:S(2)}) copy-start(bf16[1,17,2,64,256]{4,3,2,1,0:T(8,128)(2,1)} %param.4) | copy-start | bytes 3342340
  0.6 9.1 %copy-start.11 = (bf16[3,256,256]{2,1,0:T(8,128)(2,1)S(1)}, bf16[3,256,256]{2,1,0:T(8,128)(2,1)}, u32[]{:S(2)}) copy-start(bf16[3,256,256]{2,1,0:T(8,128)(2,1)} %refs_4_.2) | copy-start | bytes 1179652
  2.8 24.1 %collective-permute-start.2 = (bf16[768,256]{1,0:T(8,128)(2,1)}, bf16[768,256]{1,0:T(8,128)(2,1)}, u32[]{:S(2)}, u32[]{:S(2)}) collective-permute-start(bf16[768,256]{1,0:T(8,128)(2,1)} %bitcast.6), channel_id=1, source_target_pairs={{0,1},{1,2},{2,3},{3,4},{4,5},{5,6},{6,7},{8,9},{9,10},{10,11},{11... | collective-permute-start | bytes 1179656 | tf_op jit(solution)/shard_map/ppermute | solution.py:306
  8.4 18.5 %collective-permute-start.3 = (bf16[768,256]{1,0:T(8,128)(2,1)}, bf16[768,256]{1,0:T(8,128)(2,1)}, u32[]{:S(2)}, u32[]{:S(2)}) collective-permute-start(bf16[768,256]{1,0:T(8,128)(2,1)} %bitcast.7), channel_id=1, source_target_pairs={{1,0},{2,1},{3,2},{4,3},{5,4},{6,5},{7,6},{9,8},{10,9},{11,10},{12... | collective-permute-start | bytes 1179656 | tf_op jit(solution)/shard_map/ppermute | solution.py:307
  9.8 1.3 %copy-start.1 = (bf16[3,3,256,256]{3,2,1,0:T(8,128)(2,1)S(1)}, bf16[3,3,256,256]{3,2,1,0:T(8,128)(2,1)}, u32[]{:S(2)}) copy-start(bf16[3,3,256,256]{3,2,1,0:T(8,128)(2,1)} %ws.3) | copy-start | bytes 3538948
  11.0 1.2 %copy-start.6 = (bf16[1,17,2,64,256]{4,3,2,1,0:T(8,128)(2,1)S(1)}, bf16[1,17,2,64,256]{4,3,2,1,0:T(8,128)(2,1)}, u32[]{:S(2)}) copy-start(bf16[1,17,2,64,256]{4,3,2,1,0:T(8,128)(2,1)} %param.5) | copy-start | bytes 3342340
  12.3 14.7 %copy-start.2 = (bf16[3,3,256,256]{3,2,1,0:T(8,128)(2,1)S(1)}, bf16[3,3,256,256]{3,2,1,0:T(8,128)(2,1)}, u32[]{:S(2)}) copy-start(bf16[3,3,256,256]{3,2,1,0:T(8,128)(2,1)} %ws.3) | copy-start | bytes 3538948
  12.3 14.7 %copy-start.7 = (bf16[1,17,2,64,256]{4,3,2,1,0:T(8,128)(2,1)S(1)}, bf16[1,17,2,64,256]{4,3,2,1,0:T(8,128)(2,1)}, u32[]{:S(2)}) copy-start(bf16[1,17,2,64,256]{4,3,2,1,0:T(8,128)(2,1)} %param.5) | copy-start | bytes 3342340
  17.2 1.4 %copy-start.3 = (f32[2,1088,256]{2,1,0:T(8,128)}, f32[2,1088,256]{2,1,0:T(8,128)S(1)}, u32[]{:S(2)}) copy-start(f32[2,1088,256]{2,1,0:T(8,128)S(1)} %get-tuple-element.44.refs_4_.refs_5_) | copy-start | bytes 6684676
  18.5 1.0 copy-start.8
  20.3 16.1 %collective-permute-start = (bf16[320,256]{1,0:T(8,128)(2,1)}, bf16[320,256]{1,0:T(8,128)(2,1)}, u32[]{:S(2)}, u32[]{:S(2)}) collective-permute-start(bf16[320,256]{1,0:T(8,128)(2,1)} %bitcast.4), channel_id=1, source_target_pairs={{0,1},{1,2},{2,3},{3,4},{4,5},{5,6},{6,7},{8,9},{9,10},{10,11},{11... | collective-permute-start | bytes 491528 | tf_op jit(solution)/shard_map/ppermute | solution.py:306
  25.5 10.9 %collective-permute-start.1 = (bf16[320,256]{1,0:T(8,128)(2,1)}, bf16[320,256]{1,0:T(8,128)(2,1)}, u32[]{:S(2)}, u32[]{:S(2)}) collective-permute-start(bf16[320,256]{1,0:T(8,128)(2,1)} %bitcast.5), channel_id=1, source_target_pairs={{1,0},{2,1},{3,2},{4,3},{5,4},{6,5},{7,6},{9,8},{10,9},{11,10},{12... | collective-permute-start | bytes 491528 | tf_op jit(solution)/shard_map/ppermute | solution.py:307
  27.0 1.6 %copy-start.4 = (f32[2,1088,256]{2,1,0:T(8,128)S(1)}, f32[2,1088,256]{2,1,0:T(8,128)}, u32[]{:S(2)}) copy-start(f32[2,1088,256]{2,1,0:T(8,128)} %copy-done.3) | copy-start | bytes 6684676
  28.6 1.2 %copy-start.9 = (bf16[2,1088,256]{2,1,0:T(8,128)(2,1)S(1)}, bf16[2,1088,256]{2,1,0:T(8,128)(2,1)}, u32[]{:S(2)}) copy-start(bf16[2,1088,256]{2,1,0:T(8,128)(2,1)} %copy-done.8) | copy-start | bytes 3342340
  29.8 6.6 %copy-start.5 = (f32[2,1088,256]{2,1,0:T(8,128)S(1)}, f32[2,1088,256]{2,1,0:T(8,128)}, u32[]{:S(2)}) copy-start(f32[2,1088,256]{2,1,0:T(8,128)} %copy-done.3) | copy-start | bytes 6684676
  29.8 6.6 %copy-start.10 = (bf16[2,1088,256]{2,1,0:T(8,128)(2,1)S(1)}, bf16[2,1088,256]{2,1,0:T(8,128)(2,1)}, u32[]{:S(2)}) copy-start(bf16[2,1088,256]{2,1,0:T(8,128)(2,1)} %copy-done.8) | copy-start | bytes 3342340
  40.4 6.6 %collective-permute-start.4 = (bf16[512,768]{1,0:T(8,128)(2,1)S(1)}, bf16[512,768]{1,0:T(8,128)(2,1)S(1)}, u32[]{:S(2)}, u32[]{:S(2)}) collective-permute-start(bf16[512,768]{1,0:T(8,128)(2,1)S(1)} %get-tuple-element.48), channel_id=1, source_target_pairs={{0,8},{1,9},{2,10},{3,11},{4,12},{5,13},{6,14},{7,15},{8,0},{9,1},... | collective-permute-start | bytes 2359304 | tf_op jit(solution)/shard_map/ppermute | solution.py:247
  40.5 14.7 %collective-permute-start.9 = (bf16[448,256]{1,0:T(8,128)(2,1)S(1)}, bf16[448,256]{1,0:T(8,128)(2,1)S(1)}, u32[]{:S(2)}, u32[]{:S(2)}) collective-permute-start(bf16[448,256]{1,0:T(8,128)(2,1)S(1)} %slice.56), channel_id=1, source_target_pairs={{1,0},{2,1},{3,2},{4,3},{5,4},{6,5},{7,6},{9,8},{10,9},{11,10},{12... | collective-permute-start | bytes 688136 | tf_op jit(solution)/shard_map/ppermute | solution.py:307
  41.8 15.6 %collective-permute-start.8 = (bf16[448,256]{1,0:T(8,128)(2,1)S(1)}, bf16[448,256]{1,0:T(8,128)(2,1)S(1)}, u32[]{:S(2)}, u32[]{:S(2)}) collective-permute-start(bf16[448,256]{1,0:T(8,128)(2,1)S(1)} %slice.55), channel_id=1, source_target_pairs={{0,1},{1,2},{2,3},{3,4},{4,5},{5,6},{6,7},{8,9},{9,10},{10,11},{11... | collective-permute-start | bytes 688136 | tf_op jit(solution)/shard_map/ppermute | solution.py:306
  47.2 5.9 %copy-start.12 = (bf16[3,256,256]{2,1,0:T(8,128)(2,1)S(1)}, bf16[3,256,256]{2,1,0:T(8,128)(2,1)}, u32[]{:S(2)}) copy-start(bf16[3,256,256]{2,1,0:T(8,128)(2,1)} %refs_4_.2) | copy-start | bytes 1179652
  47.3 14.6 %collective-permute-start.7 = (bf16[128,768]{1,0:T(8,128)(2,1)S(1)}, bf16[128,768]{1,0:T(8,128)(2,1)S(1)}, u32[]{:S(2)}, u32[]{:S(2)}) collective-permute-start(bf16[128,768]{1,0:T(8,128)(2,1)S(1)} %get-tuple-element.86), channel_id=1, source_target_pairs={{0,18},{1,19},{2,16},{3,17},{4,22},{5,23},{6,20},{7,21},{8,26},{9,... | collective-permute-start | bytes 589832 | tf_op jit(solution)/shard_map/ppermute | solution.py:247
  52.5 10.4 %collective-permute-start.6 = (bf16[128,768]{1,0:T(8,128)(2,1)S(1)}, bf16[128,768]{1,0:T(8,128)(2,1)S(1)}, u32[]{:S(2)}, u32[]{:S(2)}) collective-permute-start(bf16[128,768]{1,0:T(8,128)(2,1)S(1)} %get-tuple-element.87), channel_id=1, source_target_pairs={{0,16},{1,17},{2,18},{3,19},{4,20},{5,21},{6,22},{7,23},{8,24},{9,... | collective-permute-start | bytes 589832 | tf_op jit(solution)/shard_map/ppermute | solution.py:247
  53.0 9.9 %collective-permute-start.5 = (bf16[128,768]{1,0:T(8,128)(2,1)S(1)}, bf16[128,768]{1,0:T(8,128)(2,1)S(1)}, u32[]{:S(2)}, u32[]{:S(2)}) collective-permute-start(bf16[128,768]{1,0:T(8,128)(2,1)S(1)} %get-tuple-element.88), channel_id=1, source_target_pairs={{0,2},{1,3},{2,0},{3,1},{4,6},{5,7},{6,4},{7,5},{8,10},{9,11},{10,... | collective-permute-start | bytes 589832 | tf_op jit(solution)/shard_map/ppermute | solution.py:247
  55.2 16.8 %collective-permute-start.14 = (bf16[320,256]{1,0:T(8,128)(2,1)S(1)}, bf16[320,256]{1,0:T(8,128)(2,1)S(1)}, u32[]{:S(2)}, u32[]{:S(2)}) collective-permute-start(bf16[320,256]{1,0:T(8,128)(2,1)S(1)} %slice.63), channel_id=1, source_target_pairs={{1,0},{2,1},{3,2},{4,3},{5,4},{6,5},{7,6},{9,8},{10,9},{11,10},{12... | collective-permute-start | bytes 491528 | tf_op jit(solution)/shard_map/ppermute | solution.py:307
  57.4 15.9 %collective-permute-start.13 = (bf16[320,256]{1,0:T(8,128)(2,1)S(1)}, bf16[320,256]{1,0:T(8,128)(2,1)S(1)}, u32[]{:S(2)}, u32[]{:S(2)}) collective-permute-start(bf16[320,256]{1,0:T(8,128)(2,1)S(1)} %slice.62), channel_id=1, source_target_pairs={{0,1},{1,2},{2,3},{3,4},{4,5},{5,6},{6,7},{8,9},{9,10},{10,11},{11... | collective-permute-start | bytes 491528 | tf_op jit(solution)/shard_map/ppermute | solution.py:306
  63.0 14.9 %collective-permute-start.12 = (bf16[32,768]{1,0:T(8,128)(2,1)S(1)}, bf16[32,768]{1,0:T(8,128)(2,1)S(1)}, u32[]{:S(2)}, u32[]{:S(2)}) collective-permute-start(bf16[32,768]{1,0:T(8,128)(2,1)S(1)} %get-tuple-element.89), channel_id=1, source_target_pairs={{0,5},{1,4},{2,7},{3,6},{4,1},{5,0},{6,3},{7,2},{8,13},{9,12},{10,... | collective-permute-start | bytes 147464 | tf_op jit(solution)/shard_map/ppermute | solution.py:247
  67.8 10.0 %collective-permute-start.11 = (bf16[32,768]{1,0:T(8,128)(2,1)S(1)}, bf16[32,768]{1,0:T(8,128)(2,1)S(1)}, u32[]{:S(2)}, u32[]{:S(2)}) collective-permute-start(bf16[32,768]{1,0:T(8,128)(2,1)S(1)} %get-tuple-element.90), channel_id=1, source_target_pairs={{0,4},{1,5},{2,6},{3,7},{4,0},{5,1},{6,2},{7,3},{8,12},{9,13},{10,... | collective-permute-start | bytes 147464 | tf_op jit(solution)/shard_map/ppermute | solution.py:247
  68.2 9.7 %collective-permute-start.10 = (bf16[32,768]{1,0:T(8,128)(2,1)S(1)}, bf16[32,768]{1,0:T(8,128)(2,1)S(1)}, u32[]{:S(2)}, u32[]{:S(2)}) collective-permute-start(bf16[32,768]{1,0:T(8,128)(2,1)S(1)} %get-tuple-element.91), channel_id=1, source_target_pairs={{0,1},{1,0},{2,3},{3,2},{4,5},{5,4},{6,7},{7,6},{8,9},{9,8},{10,11... | collective-permute-start | bytes 147464 | tf_op jit(solution)/shard_map/ppermute | solution.py:247
  72.0 10.9 %collective-permute-start.19 = (bf16[320,256]{1,0:T(8,128)(2,1)S(1)}, bf16[320,256]{1,0:T(8,128)(2,1)S(1)}, u32[]{:S(2)}, u32[]{:S(2)}) collective-permute-start(bf16[320,256]{1,0:T(8,128)(2,1)S(1)} %get-tuple-element.59.refs_2_), channel_id=1, source_target_pairs={{1,0},{2,1},{3,2},{4,3},{5,4},{6,5},{7,6},{9,8},{10,9},{11,10},{12... | collective-permute-start | bytes 491528 | tf_op jit(solution)/shard_map/ppermute | solution.py:307
  73.3 9.6 %collective-permute-start.18 = (bf16[320,256]{1,0:T(8,128)(2,1)S(1)}, bf16[320,256]{1,0:T(8,128)(2,1)S(1)}, u32[]{:S(2)}, u32[]{:S(2)}) collective-permute-start(bf16[320,256]{1,0:T(8,128)(2,1)S(1)} %get-tuple-element.60.refs_3_), channel_id=1, source_target_pairs={{0,1},{1,2},{2,3},{3,4},{4,5},{5,6},{6,7},{8,9},{9,10},{10,11},{11... | collective-permute-start | bytes 491528 | tf_op jit(solution)/shard_map/ppermute | solution.py:306
  78.0 7.4 %collective-permute-start.17 = (bf16[32,768]{1,0:T(8,128)(2,1)S(1)}, bf16[32,768]{1,0:T(8,128)(2,1)S(1)}, u32[]{:S(2)}, u32[]{:S(2)}) collective-permute-start(bf16[32,768]{1,0:T(8,128)(2,1)S(1)} %get-tuple-element.81), channel_id=1, source_target_pairs={{0,5},{1,4},{2,7},{3,6},{4,1},{5,0},{6,3},{7,2},{8,13},{9,12},{10,... | collective-permute-start | bytes 147464 | tf_op jit(solution)/shard_map/ppermute | solution.py:247
  82.3 5.0 %collective-permute-start.16 = (bf16[32,768]{1,0:T(8,128)(2,1)S(1)}, bf16[32,768]{1,0:T(8,128)(2,1)S(1)}, u32[]{:S(2)}, u32[]{:S(2)}) collective-permute-start(bf16[32,768]{1,0:T(8,128)(2,1)S(1)} %get-tuple-element.81), channel_id=1, source_target_pairs={{0,4},{1,5},{2,6},{3,7},{4,0},{5,1},{6,2},{7,3},{8,12},{9,13},{10,... | collective-permute-start | bytes 147464 | tf_op jit(solution)/shard_map/ppermute | solution.py:247
  82.6 4.7 %collective-permute-start.15 = (bf16[32,768]{1,0:T(8,128)(2,1)S(1)}, bf16[32,768]{1,0:T(8,128)(2,1)S(1)}, u32[]{:S(2)}, u32[]{:S(2)}) collective-permute-start(bf16[32,768]{1,0:T(8,128)(2,1)S(1)} %get-tuple-element.81), channel_id=1, source_target_pairs={{0,1},{1,0},{2,3},{3,2},{4,5},{5,4},{6,7},{7,6},{8,9},{9,8},{10,11... | collective-permute-start | bytes 147464 | tf_op jit(solution)/shard_map/ppermute | solution.py:247
  87.3 7.9 %collective-permute-start.22 = (bf16[128,768]{1,0:T(8,128)(2,1)S(1)}, bf16[128,768]{1,0:T(8,128)(2,1)S(1)}, u32[]{:S(2)}, u32[]{:S(2)}) collective-permute-start(bf16[128,768]{1,0:T(8,128)(2,1)S(1)} %pad_maximum_fusion), channel_id=1, source_target_pairs={{0,18},{1,19},{2,16},{3,17},{4,22},{5,23},{6,20},{7,21},{8,26},{9,... | collective-permute-start | bytes 589832 | tf_op jit(solution)/shard_map/ppermute | solution.py:247
  89.3 7.4 %collective-permute-start.21 = (bf16[128,768]{1,0:T(8,128)(2,1)S(1)}, bf16[128,768]{1,0:T(8,128)(2,1)S(1)}, u32[]{:S(2)}, u32[]{:S(2)}) collective-permute-start(bf16[128,768]{1,0:T(8,128)(2,1)S(1)} %pad_maximum_fusion), channel_id=1, source_target_pairs={{0,16},{1,17},{2,18},{3,19},{4,20},{5,21},{6,22},{7,23},{8,24},{9,... | collective-permute-start | bytes 589832 | tf_op jit(solution)/shard_map/ppermute | solution.py:247
  89.8 6.9 %collective-permute-start.20 = (bf16[128,768]{1,0:T(8,128)(2,1)S(1)}, bf16[128,768]{1,0:T(8,128)(2,1)S(1)}, u32[]{:S(2)}, u32[]{:S(2)}) collective-permute-start(bf16[128,768]{1,0:T(8,128)(2,1)S(1)} %pad_maximum_fusion), channel_id=1, source_target_pairs={{0,2},{1,3},{2,0},{3,1},{4,6},{5,7},{6,4},{7,5},{8,10},{9,11},{10,... | collective-permute-start | bytes 589832 | tf_op jit(solution)/shard_map/ppermute | solution.py:247
  96.8 2.4 %collective-permute-start.23 = (bf16[512,768]{1,0:T(8,128)(2,1)S(1)}, bf16[512,768]{1,0:T(8,128)(2,1)S(1)}, u32[]{:S(2)}, u32[]{:S(2)}) collective-permute-start(bf16[512,768]{1,0:T(8,128)(2,1)S(1)} %constant_dynamic-update-slice_fusion.mine), channel_id=1, source_target_pairs={{0,8},{1,9},{2,10},{3,11},{4,12},{5,13},{6,14},{7,15},{8,0},{9,1},... | collective-permute-start | bytes 2359304 | tf_op jit(solution)/shard_map/ppermute | solution.py:247

commit v3 on v0

v3 whole, which is shorter than its diff:
```python
import functools
import itertools
import math

import jax
import jax.numpy as jnp
from jax import lax
from jax.experimental import pallas as pl
from jax.experimental.pallas import tpu as pltpu
from jax.sharding import PartitionSpec as P

BF16 = jnp.bfloat16
F32 = jnp.float32
TILE_ROWS = 16
PIECE_ROWS = 128
VMEM = pl.BlockSpec(memory_space=pltpu.VMEM)
SMEM = pl.BlockSpec(memory_space=pltpu.SMEM)
ANY = pl.BlockSpec(memory_space=pl.ANY)


def mm(a, b):
    return jnp.dot(a, b, preferred_element_type=F32)


def mm_t(a, b):
    return lax.dot_general(a, b, (((1,), (1,)), ((), ())), preferred_element_type=F32)


def outer(a, b):
    return lax.dot_general(a, b, (((0,), (0,)), ((), ())), preferred_element_type=F32)


def keep(x):
    return pltpu.with_memory_space_constraint(x, pltpu.VMEM)


def away(x):
    return pltpu.with_memory_space_constraint(x, pltpu.HBM)


def call(kernel, outs, scratch, vmem_mb, flops, args, far=(), out_far=False, aliases=None):
    size = sum(a.size * a.dtype.itemsize for a in args)
    size += sum(math.prod(o.shape) * jnp.dtype(o.dtype).itemsize for o in outs)
    args = [away(a) if n in far else a for n, a in enumerate(args)]
    specs = [SMEM if a.dtype == jnp.int32 else ANY if n in far else VMEM for n, a in enumerate(args)]
    return pl.pallas_call(
        kernel,
        out_shape=outs,
        in_specs=specs,
        out_specs=[ANY if out_far else VMEM] * len(outs),
        scratch_shapes=scratch,
        input_output_aliases=aliases or {},
        compiler_params=pltpu.CompilerParams(vmem_limit_bytes=vmem_mb << 20),
        cost_estimate=pl.CostEstimate(flops=flops, bytes_accessed=size, transcendentals=0),
    )(*args)


def start(src, dst, sem):
    copy = pltpu.make_async_copy(src, dst, sem)
    copy.start()
    return copy


def row_at(code, place, rows):
    return jnp.where(code[0] == 0, place, rows - 1 - place)


def tap_at(code, step):
    return jnp.where(code[0] == 0, 1 + step, 1 - step)


def shift_right(tile):
    w = lax.broadcasted_iota(jnp.int32, tile.shape, 0)
    return jnp.where(w == 0, 0.0, pltpu.roll(tile, 1, 0))


def shift_left(tile):
    w = lax.broadcasted_iota(jnp.int32, tile.shape, 0)
    last = tile.shape[0] - 1
    return jnp.where(w == last, 0.0, pltpu.roll(tile, last, 0))


def act_grad_kernel(shift, code, cot, wt, act_grad, cot_pad):
    planes, rows, cols, chans = cot.shape
    cells = planes * cols
    for place in range(rows):
        cot_pad[:cells] = cot[:, row_at(code, place, rows)].reshape(cells, chans)
        cot_pad[cells:] = jnp.zeros((2 * shift, chans), BF16)
        total = mm_t(cot_pad[:cells], wt[0])
        total += mm_t(cot_pad[pl.ds(shift, cells)], wt[1])
        total += mm_t(cot_pad[pl.ds(2 * shift, cells)], wt[2])
        act_grad[place] = total.astype(BF16)


def pre_kernel(code, lat, ws, pre_loc, taps):
    planes, rows, cols, chans = lat.shape
    cells = planes * cols
    for place in range(rows):
        for b in range(3):
            total = None
            for step in (-1, 0, 1):
                if 0 <= place + step < rows:
                    cells_in = lat[:, row_at(code, place + step, rows)].reshape(cells, chans)
                    part = mm(cells_in, ws[tap_at(code, step), b])
                    total = part if total is None else total + part
            taps[b] = total

        @pl.loop(0, planes)
        def _(f):
            at = pl.ds(pl.multiple_of(f * cols, cols), cols)
            pre_loc[place, at] = shift_right(taps[0, at]) + taps[1, at] + shift_left(taps[2, at])


def fetch(place, shift, code, lat, cot, pre_loc, act_grad, pres, grads, cots, sems):
    planes, rows, cols, chans = lat.shape
    row = row_at(code, place, rows)
    early = [start(pre_loc.at[place], pres, sems.at[0]), start(act_grad.at[place], grads, sems.at[1])]
    late = []
    for k in range(3):
        there, lanes = planes - k * shift // cols, slice(k * chans, (k + 1) * chans)
        src = cot.at[pl.ds(planes - there, there), row]
        late.append(start(src, cots.at[pl.ds(0, there), :, lanes], sems.at[2 + k]))
        if there < planes:
            cots[there:, :, lanes] = jnp.zeros((planes - there, cols, chans), BF16)
    return early, late


def point_grads(halo_taps, cols, taps, pres, grads, act_ref, pg_ref, spread):
    chans = pres.shape[-1]

    @pl.loop(0, pres.shape[0] // cols)
    def _(f):
        at = pl.ds(pl.multiple_of(f * cols, cols), cols)
        pre = pres[at]
        if halo_taps:
            pre += shift_right(taps[0, at]) + taps[1, at] + shift_left(taps[2, at])
        sig = 0.5 + 0.5 * jnp.tanh(0.5 * pre)
        act = pre * sig
        act_ref[at] = act.astype(BF16)
        grad = grads[at].astype(F32) * sig * (1.0 + pre - act)
        grad16 = grad.astype(BF16)
        pg_ref[at] = grad16
        spread[at, :chans] = shift_left(grad).astype(BF16)
        spread[at, chans : 2 * chans] = grad16
        spread[at, 2 * chans :] = shift_right(grad).astype(BF16)


def early_kernel(shift, code, lat, cot, halo, pre_loc, act_grad, ws, *refs):
    planes, rows, cols, chans = lat.shape
    cells, count = planes * cols, rows - 1
    acts, pgs, refs = refs[:count], refs[count : 2 * count], refs[2 * count :]
    sums, next_pres, next_grads, next_cots, next_ext, taps, ext, spread, cots, pres, grads, sems, next_sems = refs
    copies = []
    for n in range(count):
        copies.append(fetch(n, shift, code, lat, cot, pre_loc, act_grad, pres.at[n], grads.at[n], cots.at[n], sems.at[n]))
    rows_in = [start(lat.at[:, row_at(code, n, rows)], ext.at[n], sems.at[n, 5]) for n in range(rows)]
    ahead = sum(fetch(count, shift, code, lat, cot, pre_loc, act_grad, next_pres, next_grads, next_cots, next_sems), [])
    for n in range(2):
        ahead.append(start(lat.at[:, row_at(code, count - 1 + n, rows)], next_ext.at[n], next_sems.at[5 + n]))
    for b in range(3):
        taps[b] = mm(halo[...], ws[tap_at(code, -1), b])
    for n in range(count):
        for copy in copies[n][0]:
            copy.wait()
        point_grads(n == 0, cols, taps, pres.at[n], grads.at[n], acts[n], pgs[n], spread.at[n])
    for copy in rows_in + [copy for _, late in copies for copy in late]:
        copy.wait()
    for kind in range(4):
        out = None
        for n in range(count):
            if kind == 3:
                part = outer(acts[n][...], cots[n].reshape(cells, 3 * chans))
            elif kind + n == 0:
                part = outer(halo[...], spread[n])
            else:
                part = outer(ext[n + kind - 1].reshape(cells, chans), spread[n])
            out = part if out is None else out + part
        block = 3 if kind == 3 else tap_at(code, kind - 1)
        sums[pl.ds(pl.multiple_of(block * chans, chans), chans)] = out
    for copy in ahead:
        copy.wait()


def late_kernel(ends, scale, code, halo, ws, before, pres, grads, cots, ext, act, pg, sums, taps, spread):
    _, planes, cols, chans = ext.shape
    cells = planes * cols
    for b in range(3):
        taps[b] = mm(halo[...], ws[tap_at(code, 1), b])
    point_grads(True, cols, taps, pres, grads, act, pg, spread)
    size = 2 * chans // ends
    for kind in range(4):
        if kind == 3:
            out = outer(act[...], cots[...].reshape(cells, 3 * chans))
        elif kind == 2:
            out = outer(halo[...], spread[...])
        else:
            out = outer(ext[kind].reshape(cells, chans), spread[...])
        block = 3 if kind == 3 else tap_at(code, kind - 1)
        out = (before[pl.ds(pl.multiple_of(block * chans, chans), chans)] + out) * scale
        for n in range(chans // size):
            half, piece = lax.div(block, 2), lax.rem(block, 2) * (chans // size) + n
            here = pl.multiple_of((piece ^ code[2]) * size, size)
            sums[half ^ code[1], pl.ds(here, size)] = out[n * size : (n + 1) * size].astype(BF16)


def out_kernel(shift, code, lat, *refs):
    acts, (wt, block_out, act_pad) = refs[:-3], refs[-3:]
    planes, rows, cols, chans = lat.shape
    cells = planes * cols
    for place in range(rows):
        row = row_at(code, place, rows)
        act_pad[: 2 * shift] = jnp.zeros((2 * shift, chans), BF16)
        act_pad[2 * shift :] = acts[place][...]
        mixed = mm(act_pad[pl.ds(2 * shift, cells)], wt[0])
        mixed += mm(act_pad[pl.ds(shift, cells)], wt[1])
        mixed += mm(act_pad[:cells], wt[2])
        mixed = mixed.astype(BF16).astype(F32).reshape(planes, cols, chans)
        block_out[:, row] = (lat[:, row].astype(F32) + mixed).astype(BF16)


def back_kernel(code, cot, *refs):
    pgs, (ws, back_loc, taps) = refs[:-3], refs[-3:]
    planes, rows, cols, _ = cot.shape
    for place in range(rows):
        row = row_at(code, place, rows)
        for b in range(3):
            total = None
            for step in (-1, 0, 1):
                if 0 <= place - step < rows:
                    out = mm_t(pgs[place - step][...], ws[tap_at(code, step), b])
                    total = out if total is None else total + out
            taps[b] = total

        @pl.loop(0, planes)
        def _(f):
            at = pl.ds(pl.multiple_of(f * cols, cols), cols)
            back = shift_left(taps[0, at]) + taps[1, at] + shift_right(taps[2, at])
            back_loc[place, at] = cot[f, row].astype(F32) + back


def last_kernel(code, back_loc, ws, far, near, latents_grad, taps):
    planes, rows, cols, chans = latents_grad.shape
    for place in range(rows):
        row = row_at(code, place, rows)
        halos = [(1, far)] if place == 0 else []
        halos += [(-1, near)] if place == rows - 1 else []
        for n, (step, halo) in enumerate(halos):
            for b in range(3):
                out = mm_t(halo[...], ws[tap_at(code, step), b])
                taps[b] = out if n == 0 else taps[b] + out

        @pl.loop(0, planes)
        def _(f):
            at = pl.ds(pl.multiple_of(f * cols, cols), cols)
            back = back_loc[place, at]
            if halos:
                back += shift_left(taps[0, at]) + taps[1, at] + shift_right(taps[2, at])
            latents_grad[f, row] = back.astype(BF16)


def order_kernel(ends, own, code, sums, *refs):
    spatial, temporal, blocks, sems = refs[-4:]
    chans = spatial.shape[-1]
    size = 2 * chans // ends
    for slot in range(ends):
        piece = slot ^ code[2]
        block, at = lax.div(piece, chans // size), lax.rem(piece, chans // size) * size
        for b in range(3):
            found = sums[slot * size : (slot + 1) * size, b * chans : (b + 1) * chans]
            blocks[block, b, pl.ds(pl.multiple_of(at, size), size)] = found.astype(F32)
    half = code[1] if own else 1 - code[1]

    @pl.when(half == 0)
    def _():
        copies = [start(blocks.at[n], spatial.at[n], sems.at[n]) for n in range(2)]
        for copy in copies:
            copy.wait()

    @pl.when(half != 0)
    def _():
        copies = [start(blocks.at[0], spatial.at[2], sems.at[0]), start(blocks.at[1], temporal, sems.at[1])]
        for copy in copies:
            copy.wait()


def bits_of(axis):
    count = lax.axis_size(axis)
    return [(axis, 1 << n) for n in range(count.bit_length()) if 1 << n < count]


def send(x, steps):
    wide, tall = lax.axis_size("dp"), lax.axis_size("tm")
    mask = sum(bit * tall if axis == "dp" else bit for axis, bit in steps)
    return lax.ppermute(x, ("dp", "tm"), [(i, i ^ mask) for i in range(wide * tall)])


def send_pieces(x, steps):
    rows = x.shape[0]
    pieces = [send(x[n : min(n + PIECE_ROWS, rows)], steps) for n in range(0, rows, PIECE_ROWS)]
    return jnp.concatenate(pieces, axis=0) if len(pieces) > 1 else pieces[0]


def plus(x, *others):
    total = x.astype(F32)
    for other in others:
        total = total + other.astype(F32)
    return total.astype(BF16)


def groups_of(rows):
    wide, tall = bits_of("dp")[1:], bits_of("tm")
    groups, ends, split = [], 1, True
    for order, shared in ((wide, True), (tall[1:], True), (tall[:1], False)):
        while order:
            group, order = order[:2], order[2:]
            split = split and shared and rows % (TILE_ROWS * ends << len(group)) == 0
            ends = ends << len(group) if split else ends
            groups.append((group, split))
    return groups, ends


def codes(groups):
    def bit_at(step):
        return (lax.axis_index(step[0]) // step[1]) % 2

    word = 0
    for group, split in groups:
        for step in group if split else ():
            word = 2 * word + bit_at(step)
    return jnp.stack([jnp.asarray(x, jnp.int32) for x in (bit_at(("tm", 1)), bit_at(("dp", 1)), word)])


def subsets(group):
    return [[s for n, s in enumerate(group) if k >> (len(group) - 1 - n) & 1] for k in range(1, 1 << len(group))]


def add_up(mine, other, groups, beside, there):
    core = [("dp", 1)]
    mine = plus(mine, send_pieces(other, core))
    plan = [(group, split, True) for group, split in groups]
    shared = [step for group, split in groups if split for step in group]
    while shared:
        count = 2 - len(shared) % 2
        plan.append((shared[-count:], True, False))
        shared = shared[:-count]
    works = beside[: len(plan)]
    works[-1:] = [dict(itertools.chain.from_iterable(work.items() for work in beside[len(works) - 1 :]))]
    for n, (group, split, down) in enumerate(plan):
        others = subsets(group)
        size = mine.shape[0] // (len(others) + 1) if split and down else 0
        move = send_pieces if down else send
        got = [move(mine[(k + 1) * size : (k + 2) * size] if size else mine, steps) for k, steps in enumerate(others)]
        if n < len(works):
            got, also = lax.optimization_barrier((got, {name: run(mine) for name, run in works[n].items()}))
            there |= also
        mine = plus(mine[:size] if size else mine, *got) if down else jnp.concatenate([mine, *got], axis=0)
    return mine, send(mine, core)


def from_near(x):
    count = lax.axis_size("tm")
    return lax.ppermute(x, "tm", [(i, i ^ 1) for i in range(count) if i ^ 1 < count])


def from_far(x):
    count = lax.axis_size("tm")
    return lax.ppermute(x, "tm", [(i, j) for i in range(count) if 0 <= (j := ((i - 1) ^ 1) + 1) < count])


def after(x, *others):
    return lax.optimization_barrier((x, others))[0]


def body(latents, cotangent, spatial_weight, temporal_weight):
    clips, frames, rows, cols, chans = latents.shape
    planes, shift = frames * clips, clips * cols
    cells = planes * cols
    lat = jnp.swapaxes(latents, 0, 1).reshape(planes, rows, cols, chans)
    cot = jnp.swapaxes(cotangent, 0, 1).reshape(planes, rows, cols, chans)
    scale = (clips * lax.axis_size("dp") * frames * rows * lax.axis_size("tm") * cols) ** (-0.5)
    groups, ends = groups_of(2 * chans)
    code = codes(groups)
    unit = 2 * cells * chans * chans

    def lat_row(source, place):
        row = lax.axis_index("tm") % 2 * (rows - 1 - 2 * place) + place
        return lax.dynamic_index_in_dim(source, row, 1, keepdims=False).reshape(cells, chans)

    there = {}
    lat_far = from_far(lat_row(lat, 0))
    taps = pltpu.VMEM((3, cells, chans), F32)
    padded = pltpu.VMEM((cells + 2 * shift, chans), BF16)
    (act_grad,) = call(
        functools.partial(act_grad_kernel, shift), [pltpu.HBM((rows, cells, chans), BF16)], [padded], 10,
        3 * rows * unit, [code, cot, temporal_weight],
    )
    lat_near = from_near(lat_row(after(lat, act_grad), rows - 1))
    (pre_loc,) = call(
        pre_kernel, [pltpu.HBM((rows, cells, chans), F32)], [taps], 10, (9 * rows - 6) * unit,
        [code, after(lat, act_grad), spatial_weight],
    )
    narrow = jax.ShapeDtypeStruct((cells, chans), BF16)
    count = rows - 1
    early = call(
        functools.partial(early_kernel, shift),
        [narrow] * (2 * count)
        + [
            pltpu.VMEM((4 * chans, 3 * chans), F32),
            pltpu.VMEM((cells, chans), F32),
            pltpu.VMEM((cells, chans), BF16),
            pltpu.VMEM((planes, cols, 3 * chans), BF16),
            pltpu.VMEM((2, planes, cols, chans), BF16),
        ],
        [
            taps,
            pltpu.VMEM((rows, planes, cols, chans), BF16),
            pltpu.VMEM((count, cells, 3 * chans), BF16),
            pltpu.VMEM((count, planes, cols, 3 * chans), BF16),
            pltpu.VMEM((count, cells, chans), F32),
            pltpu.VMEM((count, cells, chans), BF16),
            pltpu.SemaphoreType.DMA((rows, 6)),
            pltpu.SemaphoreType.DMA((7,)),
        ],
        16, (3 + 12 * count) * unit, [code, lat, cot, keep(lat_far), pre_loc, act_grad, keep(spatial_weight)],
        far=(1, 2, 4, 5),
    )
    acts, pgs = list(early[:count]), list(early[count : 2 * count])
    there["far"] = from_far(after(pgs[0], lat_near))
    act, pg, sums = call(
        functools.partial(late_kernel, ends, scale),
        [narrow, narrow, jax.ShapeDtypeStruct((2, 2 * chans, 3 * chans), BF16)],
        [taps, pltpu.VMEM((cells, 3 * chans), BF16)], 12, 15 * unit,
        [code, *map(keep, (lat_near, spatial_weight, *early[2 * count :]))],
    )
    acts, pgs = acts + [act], pgs + [pg]
    image = jax.ShapeDtypeStruct(lat.shape, BF16)

    def out(_):
        return call(
            functools.partial(out_kernel, shift), [image], [padded], 12, 3 * rows * unit,
            [code, lat, *acts, temporal_weight],
        )[0]

    def back(_):
        return call(
            back_kernel, [jax.ShapeDtypeStruct((rows, cells, chans), F32)], [taps], 12,
            (9 * rows - 6) * unit, [code, cot, *pgs, spatial_weight],
        )[0]

    def last(_):
        return call(
            last_kernel, [image], [taps], 12, 6 * unit,
            [code, there["back"], keep(spatial_weight), keep(there["far"]), keep(there["near"])],
        )[0]

    def ordered(sums, *given):
        return call(
            functools.partial(order_kernel, ends, not given),
            [jax.ShapeDtypeStruct((3, 3, chans, chans), F32), jax.ShapeDtypeStruct((3, chans, chans), F32)],
            [pltpu.VMEM((2, 3, chans, chans), F32), pltpu.SemaphoreType.DMA((2,))],
            8, 0, [code, keep(sums), *given],
            far=(2, 3), out_far=True, aliases={2: 0, 3: 1} if given else None,
        )

    beside = [
        {"far": lambda _: there["far"], "out": out},
        {"near": lambda gate: from_near(after(pgs[-1], gate)), "back": back},
        {},
        {},
        {"last": last},
    ]
    mine, other = add_up(sums[0], sums[1], groups, beside, there)
    latents_grad, block_out = there["last"], there["out"]
    spatial_grad, temporal_grad = ordered(other, *ordered(mine))

    def home(x):
        return jnp.swapaxes(x.reshape(frames, clips, rows, cols, chans), 0, 1)

    return home(block_out), home(latents_grad), spatial_grad, temporal_grad


def solution(mesh):
    in_specs = (P("dp", None, "tm", None, None), P("dp", None, "tm", None, None), P(), P())
    out_specs = (P("dp", None, "tm", None, None), P("dp", None, "tm", None, None), P(), P())
    return jax.shard_map(body, mesh=mesh, in_specs=in_specs, out_specs=out_specs, check_vma=False)
```

time: 222 us -> 94.5 us (0.43)
  waiting for transfers between devices: 147 us -> 27.1 us
  Pallas kernels: 0 us -> 31.9 us
  matrix products: 23.6 us -> 0 us
  starting transfers between devices: 13.6 us -> 30.1 us
  between operations: 14.3 us -> 1.1 us
  local copies, waits for them, and re-layouts: 15.4 us -> 3.55 us
  other arithmetic: 8.18 us -> 0.5 us
    psum x1 -> x0, waiting for transfers between devices: 111 us -> none  [body(): lax.psum((spatial_local, temporal_local), ('dp', 'tm'))]
    pallas_call x0 -> x9, Pallas kernels: none -> 31.9 us  [call(): pl.pallas_call(kernel, out_shape=outs, in_specs=specs, out_specs=[ANY if...]
    dot_general x12 -> x0, matrix products: 23.6 us -> none  [the longest x3 6.78 us: causal_mix(): jnp.dot(earlier, weight[tap], preferred_element_type=jnp.float32)]
    ppermute x4 -> x19, starting transfers between devices: 13.6 us -> 30.1 us  [the longest x15 15.4 us: send(): lax.ppermute(x, ('dp', 'tm'), [(i, i ^ mask) for i in range(wide * tall)])]
    ppermute x4 -> x19, waiting for transfers between devices: 35.9 us -> 27.1 us  [the longest x15 19.8 us: send(): lax.ppermute(x, ('dp', 'tm'), [(i, i ^ mask) for i in range(wide * tall)])]
    unnamed x37 -> x17, local copies, waits for them, and re-layouts: 10.1 us -> 2.3 us
    mul x2 -> x0, other arithmetic: 4.3 us -> none  [the longest x1 3.35 us: body(): spatial_sum * scale]
    slice x4 -> x3, local copies, waits for them, and re-layouts: 3.99 us -> 0.1 us  [the longest x2 0.08 us: send_pieces(): x[n:min(n + PIECE_ROWS, rows)]]
  transfers between devices with their start and end apart: 5 -> 19, of which waited for: 3 -> 10; matrix products, arithmetic and copies ran while one was open for 10% -> 0% of each run, Pallas kernels for 0% -> 27%
where the time goes in v3:
time: 94.5 us; the launch traced here: 94.2 us
  Pallas kernels  31.9 us (34%)
  starting transfers between devices  30.1 us (32%)
  waiting for transfers between devices  27.1 us (29%)
  local copies, waits for them, and re-layouts  3.55 us (4%)
  between operations  1.1 us (1%)
    pallas_call x9, Pallas kernels, call(): pl.pallas_call(kernel, out_shape=outs, in_specs=specs, out_specs=[ANY if...  31.9 us
    ppermute x15, waiting for transfers between devices, send(): lax.ppermute(x, ('dp', 'tm'), [(i, i ^ mask) for i in range(wide * tall)])  19.8 us
    ppermute x15, starting transfers between devices, send(): lax.ppermute(x, ('dp', 'tm'), [(i, i ^ mask) for i in range(wide * tall)])  15.4 us
    ppermute x2, starting transfers between devices, from_near(): lax.ppermute(x, 'tm', [(i, i ^ 1) for i in range(count) if i ^ 1 < count])  13 us
    ppermute x2, waiting for transfers between devices, from_near(): lax.ppermute(x, 'tm', [(i, i ^ 1) for i in range(count) if i ^ 1 < count])  7.35 us
    unnamed x17, local copies, waits for them, and re-layouts  2.3 us
  transfers between devices with their start and end apart: 19, of which 10 were waited for; matrix products, arithmetic and copies ran while one was open for 0% of the time, Pallas kernels for 27%

profile of v3, /device:TPU:0, one launch (start us, length us, event | category | flops | bytes accessed | tf_op | source)
XLA Modules:
  0.0 94.2 jit_solution(7401923655204916340)
XLA Ops:
  0.6 1.1 %constant_dynamic-slice_fusion = bf16[1,17,1,64,256]{4,3,2,1,0:T(8,128)(2,1)S(1)} fusion(bf16[1,17,2,64,256]{4,3,2,1,0:T(8,128)(2,1)} %param.4, s32[]{:T(128)S(6)} %select_n.55), kind=kLoop, calls=%fused_computation.17 | loop fusion | bytes 1114116 | tf_op jit(solution)/shard_map/jit(dynamic_index_in_dim)/dynamic_slice | solution.py:387
  1.8 0.7 collective-permute-start.1
  2.5 0.1 pad_add_fusion.code
  2.6 0.0 copy-start.3
  2.6 1.0 %copy-done.3 = bf16[3,256,256]{2,1,0:T(8,128)(2,1)S(1)} copy-done((bf16[3,256,256]{2,1,0:T(8,128)(2,1)S(1)}, bf16[3,256,256]{2,1,0:T(8,128)(2,1)}, u32[]{:S(2)}) %copy-start.3) | copy-done | bytes 393240
  3.6 0.0 copy-start.5
  3.6 1.2 %copy-done.5 = bf16[1,17,2,64,256]{4,3,2,1,0:T(8,128)(2,1)S(1)} copy-done((bf16[1,17,2,64,256]{4,3,2,1,0:T(8,128)(2,1)S(1)}, bf16[1,17,2,64,256]{4,3,2,1,0:T(8,128)(2,1)}, u32[]{:S(2)}) %copy-start.5) | copy-done | bytes 1114136
  4.9 0.0 copy-start.1
  4.9 0.0 copy-start
  4.9 2.6 %shard_map.75.act_grad = bf16[2,1088,256]{2,1,0:T(8,128)(2,1)} custom-call(s32[3]{0:T(128)S(1)} %pad_add_fusion.code, bf16[17,2,64,256]{3,2,1,0:T(8,128)(2,1)S(1)} %bitcast.25, bf16[3,256,256]{2,1,0:T(8,128)(2,1)S(1)} %copy-done.3), custom_call_target="tpu_custom_call" | custom-call | flops 855638016 | bytes 2621452 | tf_op jit(solution)/shard_map/pallas_call | solution.py:46
  7.5 0.0 copy-done.1
  7.5 5.8 %collective-permute-start = (bf16[1088,256]{1,0:T(8,128)(2,1)S(1)}, bf16[1088,256]{1,0:T(8,128)(2,1)S(1)}, u32[]{:S(2)}, u32[]{:S(2)}) collective-permute-start(bf16[1088,256]{1,0:T(8,128)(2,1)S(1)} %bitcast.30), channel_id=1, source_target_pairs={{0,1},{1,0},{2,3},{3,2},{4,5},{5,4},{6,7},{7,6},{8,9},{9,8},{10,11... | collective-permute-start | bytes 1671176 | tf_op jit(solution)/shard_map/ppermute | solution.py:362
  13.3 0.0 copy-done
  13.3 5.2 %shard_map.76.pre_loc = f32[2,1088,256]{2,1,0:T(8,128)} custom-call(s32[3]{0:T(128)S(1)} %pad_add_fusion.code, bf16[17,2,64,256]{3,2,1,0:T(8,128)(2,1)S(1)} %bitcast.22, bf16[3,3,256,256]{3,2,1,0:T(8,128)(2,1)S(1)} %copy-done), custom_call_target="tpu_custom_call" | custom-call | flops 1711276032 | bytes 4521996 | tf_op jit(solution)/shard_map/pallas_call | solution.py:46
  18.5 0.0 collective-permute-done.1.halo
  18.5 5.5 %shard_map.77 = (bf16[1088,256]{1,0:T(8,128)(2,1)S(1)}, bf16[1088,256]{1,0:T(8,128)(2,1)S(1)}, f32[1024,768]{1,0:T(8,128)S(1)}, f32[1088,256]{1,0:T(8,128)S(1)},...) custom-call(s32[3]{0:T(128)S(1)} %pad_add_fusion.code, ...), custom_call_target="tpu_custom_call" | custom-call | flops 2139095040 | bytes 16023564 | tf_op jit(solution)/shard_map/pallas_call | solution.py:46
  24.0 7.3 %collective-permute-done.halo = bf16[1088,256]{1,0:T(8,128)(2,1)S(1)} collective-permute-done((bf16[1088,256]{1,0:T(8,128)(2,1)S(1)}, bf16[1088,256]{1,0:T(8,128)(2,1)S(1)}, u32[]{:S(2)}, u32[]{:S(2)}) %collective-permute-start) | collective-permute-done | bytes 557088 | tf_op jit(solution)/shard_map/ppermute | solution.py:362
  31.3 4.4 %shard_map.78 = (bf16[1088,256]{1,0:T(8,128)(2,1)S(1)}, bf16[1088,256]{1,0:T(8,128)(2,1)S(1)}, bf16[2,512,768]{2,1,0:T(8,128)(2,1)S(1)}) custom-call(s32[3]{0:T(128)S(1)} %pad_add_fusion.code, bf16[1088,256]{1,0:T(8,128)(2,1)S(1)} %collective-permute-done.halo, bf16[3,3,256,256]{3,2,1,0:T(8,128)(2,1)S(1)} %copy-done, ...), custom_call_target="tpu_custom_call" | custom-call | flops 2139095040 | bytes 12025868 | tf_op jit(solution)/shard_map/pallas_call | solution.py:46
  35.7 0.1 slice_bitcast_fusion.3
  35.8 0.1 collective-permute-start.2
  35.9 0.5 collective-permute-start.3
  36.4 0.1 collective-permute-start.4
  36.4 0.4 collective-permute-start.5
  36.9 1.0 %collective-permute-start.8 = (bf16[1088,256]{1,0:T(8,128)(2,1)S(1)}, bf16[1088,256]{1,0:T(8,128)(2,1)S(1)}, u32[]{:S(2)}, u32[]{:S(2)}) collective-permute-start(bf16[1088,256]{1,0:T(8,128)(2,1)S(1)} %get-tuple-element.41.refs_0_), channel_id=1, source_target_pairs={{1,2},{2,1},{3,4},{4,3},{5,6},{6,5},{9,10},{10,9},{11,12},{12,11},... | collective-permute-start | bytes 1671176 | tf_op jit(solution)/shard_map/ppermute | solution.py:367
  37.9 0.0 collective-permute-done.2
  37.9 0.0 collective-permute-done.3
  37.9 0.0 collective-permute-done.4
  37.9 0.2 collective-permute-done.5
  38.1 0.2 fusion
  38.4 1.6 %collective-permute-start.6 = (bf16[128,768]{1,0:T(8,128)(2,1)S(1)}, bf16[128,768]{1,0:T(8,128)(2,1)S(1)}, u32[]{:S(2)}, u32[]{:S(2)}) collective-permute-start(bf16[128,768]{1,0:T(8,128)(2,1)S(1)} %get-tuple-element.68), channel_id=1, source_target_pairs={{0,16},{1,17},{2,18},{3,19},{4,20},{5,21},{6,22},{7,23},{8,24},{9,... | collective-permute-start | bytes 589832 | tf_op jit(solution)/shard_map/ppermute | solution.py:294
  39.9 0.5 collective-permute-start.7
  40.5 0.0 copy-done.2
  40.5 0.0 copy-done.4
  40.5 2.6 %shard_map.79 = bf16[17,2,64,256]{3,2,1,0:T(8,128)(2,1)} custom-call(s32[3]{0:T(128)S(1)} %pad_add_fusion.code, bf16[17,2,64,256]{3,2,1,0:T(8,128)(2,1)S(1)} %bitcast.23, bf16[1088,256]{1,0:T(8,128)(2,1)S(1)} %get-tuple-element.42.refs_0_, bf16[1088,256]{1,0:T(8,128)(2,1)S(1)} %get-tuple-element.43.refs_1_, bf16[3,256,256]{2,1,0:T(8,128)(2,1)S(1)} %copy-done.4), custom_call_target="tpu_custom_call" | custom-call | flops 855638016 | bytes 3735564 | tf_op jit(solution)/shard_map/pallas_call | solution.py:46
  43.1 3.1 %collective-permute-done.6 = bf16[128,768]{1,0:T(8,128)(2,1)S(1)} collective-permute-done((bf16[128,768]{1,0:T(8,128)(2,1)S(1)}, bf16[128,768]{1,0:T(8,128)(2,1)S(1)}, u32[]{:S(2)}, u32[]{:S(2)}) %collective-permute-start.6) | collective-permute-done | bytes 196640 | tf_op jit(solution)/shard_map/ppermute | solution.py:294
  46.2 3.5 %collective-permute-done.7 = bf16[128,768]{1,0:T(8,128)(2,1)S(1)} collective-permute-done((bf16[128,768]{1,0:T(8,128)(2,1)S(1)}, bf16[128,768]{1,0:T(8,128)(2,1)S(1)}, u32[]{:S(2)}, u32[]{:S(2)}) %collective-permute-start.7) | collective-permute-done | bytes 196640 | tf_op jit(solution)/shard_map/ppermute | solution.py:294
  49.7 0.0 collective-permute-done.8.far
  49.7 0.1 add_convert_fusion
  49.8 7.2 %collective-permute-start.12 = (bf16[1088,256]{1,0:T(8,128)(2,1)S(1)}, bf16[1088,256]{1,0:T(8,128)(2,1)S(1)}, u32[]{:S(2)}, u32[]{:S(2)}) collective-permute-start(bf16[1088,256]{1,0:T(8,128)(2,1)S(1)} %get-tuple-element.47.refs_1_), channel_id=1, source_target_pairs={{0,1},{1,0},{2,3},{3,2},{4,5},{5,4},{6,7},{7,6},{8,9},{9,8},{10,11... | collective-permute-start | bytes 1671176 | tf_op jit(solution)/shard_map/ppermute | solution.py:362
  57.1 1.6 %collective-permute-start.10 = (bf16[64,768]{1,0:T(8,128)(2,1)S(1)}, bf16[64,768]{1,0:T(8,128)(2,1)S(1)}, u32[]{:S(2)}, u32[]{:S(2)}) collective-permute-start(bf16[64,768]{1,0:T(8,128)(2,1)S(1)} %get-tuple-element.71), channel_id=1, source_target_pairs={{0,2},{1,3},{2,0},{3,1},{4,6},{5,7},{6,4},{7,5},{8,10},{9,11},{10,... | collective-permute-start | bytes 294920 | tf_op jit(solution)/shard_map/ppermute | solution.py:294
  58.7 2.5 %collective-permute-start.11 = (bf16[64,768]{1,0:T(8,128)(2,1)S(1)}, bf16[64,768]{1,0:T(8,128)(2,1)S(1)}, u32[]{:S(2)}, u32[]{:S(2)}) collective-permute-start(bf16[64,768]{1,0:T(8,128)(2,1)S(1)} %get-tuple-element.70), channel_id=1, source_target_pairs={{0,6},{1,7},{2,4},{3,5},{4,2},{5,3},{6,0},{7,1},{8,14},{9,15},{10,... | collective-permute-start | bytes 294920 | tf_op jit(solution)/shard_map/ppermute | solution.py:294
  61.2 0.0 collective-permute-start.9
  61.2 0.0 copy-done.6
  61.2 4.0 %shard_map.80.back_loc = f32[2,1088,256]{2,1,0:T(8,128)S(1)} custom-call(s32[3]{0:T(128)S(1)} %pad_add_fusion.code, bf16[17,2,64,256]{3,2,1,0:T(8,128)(2,1)S(1)} %bitcast.26, bf16[1088,256]{1,0:T(8,128)(2,1)S(1)} %get-tuple-element.41.refs_0_, bf16[1088,256]{1,0:T(8,128)(2,1)S(1)} %get-tuple-element.47.refs_1_, bf16[3,3,256,256]{3,2,1,0:T(8,128)(2,1)S(1)} %copy-done), custom_call_target="tpu_custom_call" | custom-call | flops 1711276032 | bytes 5636108 | tf_op jit(solution)/shard_map/pallas_call | solution.py:46
  65.2 0.0 collective-permute-done.10
  65.2 0.8 collective-permute-done.11
  66.0 3.2 %collective-permute-done.9 = bf16[64,768]{1,0:T(8,128)(2,1)S(1)} collective-permute-done((bf16[64,768]{1,0:T(8,128)(2,1)S(1)}, bf16[64,768]{1,0:T(8,128)(2,1)S(1)}, u32[]{:S(2)}, u32[]{:S(2)}) %collective-permute-start.9) | collective-permute-done | bytes 98336 | tf_op jit(solution)/shard_map/ppermute | solution.py:294
  69.1 0.0 collective-permute-done.12.near
  69.1 0.1 add_convert_fusion.2
  69.2 1.7 %collective-permute-start.13 = (bf16[64,768]{1,0:T(8,128)(2,1)S(1)}, bf16[64,768]{1,0:T(8,128)(2,1)S(1)}, u32[]{:S(2)}, u32[]{:S(2)}) collective-permute-start(bf16[64,768]{1,0:T(8,128)(2,1)S(1)} %add_convert_fusion.2), channel_id=1, source_target_pairs={{0,1},{1,0},{2,3},{3,2},{4,5},{5,4},{6,7},{7,6},{8,9},{9,8},{10,11... | collective-permute-start | bytes 294920 | tf_op jit(solution)/shard_map/ppermute | solution.py:294
  70.9 3.0 %collective-permute-done.13 = bf16[64,768]{1,0:T(8,128)(2,1)S(1)} collective-permute-done((bf16[64,768]{1,0:T(8,128)(2,1)S(1)}, bf16[64,768]{1,0:T(8,128)(2,1)S(1)}, u32[]{:S(2)}, u32[]{:S(2)}) %collective-permute-start.13) | collective-permute-done | bytes 98336 | tf_op jit(solution)/shard_map/ppermute | solution.py:294
  73.9 2.8 %collective-permute-start.14 = (bf16[64,768]{1,0:T(8,128)(2,1)S(1)}, bf16[64,768]{1,0:T(8,128)(2,1)S(1)}, u32[]{:S(2)}, u32[]{:S(2)}) collective-permute-start(bf16[64,768]{1,0:T(8,128)(2,1)S(1)} %get-tuple-element.63), channel_id=1, source_target_pairs={{0,4},{1,5},{2,6},{3,7},{4,0},{5,1},{6,2},{7,3},{8,12},{9,13},{10,... | collective-permute-start | bytes 294920 | tf_op jit(solution)/shard_map/ppermute | solution.py:294
  76.7 3.0 %collective-permute-done.14 = bf16[64,768]{1,0:T(8,128)(2,1)S(1)} collective-permute-done((bf16[64,768]{1,0:T(8,128)(2,1)S(1)}, bf16[64,768]{1,0:T(8,128)(2,1)S(1)}, u32[]{:S(2)}, u32[]{:S(2)}) %collective-permute-start.14) | collective-permute-done | bytes 98336 | tf_op jit(solution)/shard_map/ppermute | solution.py:294
  79.7 1.7 %collective-permute-start.15 = (bf16[128,768]{1,0:T(8,128)(2,1)S(1)}, bf16[128,768]{1,0:T(8,128)(2,1)S(1)}, u32[]{:S(2)}, u32[]{:S(2)}) collective-permute-start(bf16[128,768]{1,0:T(8,128)(2,1)S(1)} %pad_maximum_fusion.1), channel_id=1, source_target_pairs={{0,2},{1,3},{2,0},{3,1},{4,6},{5,7},{6,4},{7,5},{8,10},{9,11},{10,... | collective-permute-start | bytes 589832 | tf_op jit(solution)/shard_map/ppermute | solution.py:294
  81.5 1.5 %collective-permute-start.16 = (bf16[128,768]{1,0:T(8,128)(2,1)S(1)}, bf16[128,768]{1,0:T(8,128)(2,1)S(1)}, u32[]{:S(2)}, u32[]{:S(2)}) collective-permute-start(bf16[128,768]{1,0:T(8,128)(2,1)S(1)} %pad_maximum_fusion.1), channel_id=1, source_target_pairs={{0,16},{1,17},{2,18},{3,19},{4,20},{5,21},{6,22},{7,23},{8,24},{9,... | collective-permute-start | bytes 589832 | tf_op jit(solution)/shard_map/ppermute | solution.py:294
  83.0 0.3 collective-permute-start.17
  83.3 4.0 %shard_map.81 = bf16[17,2,64,256]{3,2,1,0:T(8,128)(2,1)} custom-call(s32[3]{0:T(128)S(1)} %pad_add_fusion.code, f32[2,1088,256]{2,1,0:T(8,128)S(1)} %shard_map.80.back_loc, bf16[3,3,256,256]{3,2,1,0:T(8,128)(2,1)S(1)} %copy-done, bf16[1088,256]{1,0:T(8,128)(2,1)S(1)} %collective-permute-done.8.far, bf16[1088,256]{1,0:T(8,128)(2,1)S(1)} %collective-permute-done.12.near), custom_call_target="tpu_custom_call" | custom-call | flops 855638016 | bytes 5636108 | tf_op jit(solution)/shard_map/pallas_call | solution.py:46
  87.2 0.0 collective-permute-done.15
  87.3 2.6 %collective-permute-done.16 = bf16[128,768]{1,0:T(8,128)(2,1)S(1)} collective-permute-done((bf16[128,768]{1,0:T(8,128)(2,1)S(1)}, bf16[128,768]{1,0:T(8,128)(2,1)S(1)}, u32[]{:S(2)}, u32[]{:S(2)}) %collective-permute-start.16) | collective-permute-done | bytes 196640 | tf_op jit(solution)/shard_map/ppermute | solution.py:294
  89.9 0.0 collective-permute-done.17
  89.9 0.1 collective-permute-start.18
  90.0 1.8 %shard_map.82 = (f32[3,3,256,256]{3,2,1,0:T(8,128)}, f32[3,256,256]{2,1,0:T(8,128)}) custom-call(s32[3]{0:T(128)S(1)} %pad_add_fusion.code, bf16[512,768]{1,0:T(8,128)(2,1)S(1)} %constant_dynamic-update-slice_fusion.sums), custom_call_target="tpu_custom_call" | custom-call | bytes 3932172 | tf_op jit(solution)/shard_map/pallas_call | solution.py:46
  91.8 0.5 collective-permute-done.18.sums
  92.3 1.8 %shard_map.83 = (f32[3,3,256,256]{3,2,1,0:T(8,128)}, f32[3,256,256]{2,1,0:T(8,128)}) custom-call(s32[3]{0:T(128)S(1)} %pad_add_fusion.code, bf16[512,768]{1,0:T(8,128)(2,1)S(1)} %collective-permute-done.18.sums, f32[3,3,256,256]{3,2,1,0:T(8,128)} %get-tuple-element.58.refs_0_, ...), custom_call_target="tpu_custom_call", output_to_operand_aliasing={{0}: (2, {}), {1}: (3, {})} | custom-call | bytes 7077900 | tf_op jit(solution)/shard_map/pallas_call | solution.py:46
  (13 shorter events, 0.2 us)
Async XLA Ops:
  1.8 16.7 %collective-permute-start.1 = (bf16[1088,256]{1,0:T(8,128)(2,1)S(1)}, bf16[1088,256]{1,0:T(8,128)(2,1)S(1)}, u32[]{:S(2)}, u32[]{:S(2)}) collective-permute-start(bf16[1088,256]{1,0:T(8,128)(2,1)S(1)} %bitcast.29), channel_id=1, source_target_pairs={{1,2},{2,1},{3,4},{4,3},{5,6},{6,5},{9,10},{10,9},{11,12},{12,11},... | collective-permute-start | bytes 1671176 | tf_op jit(solution)/shard_map/ppermute | solution.py:367
  2.6 1.0 %copy-start.3 = (bf16[3,256,256]{2,1,0:T(8,128)(2,1)S(1)}, bf16[3,256,256]{2,1,0:T(8,128)(2,1)}, u32[]{:S(2)}) copy-start(bf16[3,256,256]{2,1,0:T(8,128)(2,1)} %refs_2_.2) | copy-start | bytes 1179652
  3.6 1.2 %copy-start.5 = (bf16[1,17,2,64,256]{4,3,2,1,0:T(8,128)(2,1)S(1)}, bf16[1,17,2,64,256]{4,3,2,1,0:T(8,128)(2,1)}, u32[]{:S(2)}) copy-start(bf16[1,17,2,64,256]{4,3,2,1,0:T(8,128)(2,1)} %param.5) | copy-start | bytes 3342340
  4.9 2.6 %copy-start.1 = (bf16[1,17,2,64,256]{4,3,2,1,0:T(8,128)(2,1)S(1)}, bf16[1,17,2,64,256]{4,3,2,1,0:T(8,128)(2,1)}, u32[]{:S(2)}) copy-start(bf16[1,17,2,64,256]{4,3,2,1,0:T(8,128)(2,1)} %param.4) | copy-start | bytes 3342340
  4.9 8.4 %copy-start = (bf16[3,3,256,256]{3,2,1,0:T(8,128)(2,1)S(1)}, bf16[3,3,256,256]{3,2,1,0:T(8,128)(2,1)}, u32[]{:S(2)}) copy-start(bf16[3,3,256,256]{3,2,1,0:T(8,128)(2,1)} %ws.7) | copy-start | bytes 3538948
  7.5 23.8 %collective-permute-start = (bf16[1088,256]{1,0:T(8,128)(2,1)S(1)}, bf16[1088,256]{1,0:T(8,128)(2,1)S(1)}, u32[]{:S(2)}, u32[]{:S(2)}) collective-permute-start(bf16[1088,256]{1,0:T(8,128)(2,1)S(1)} %bitcast.30), channel_id=1, source_target_pairs={{0,1},{1,0},{2,3},{3,2},{4,5},{5,4},{6,7},{7,6},{8,9},{9,8},{10,11... | collective-permute-start | bytes 1671176 | tf_op jit(solution)/shard_map/ppermute | solution.py:362
  35.8 2.1 %collective-permute-start.2 = (bf16[128,768]{1,0:T(8,128)(2,1)S(1)}, bf16[128,768]{1,0:T(8,128)(2,1)S(1)}, u32[]{:S(2)}, u32[]{:S(2)}) collective-permute-start(bf16[128,768]{1,0:T(8,128)(2,1)S(1)} %get-tuple-element.64), channel_id=1, source_target_pairs={{0,8},{1,9},{2,10},{3,11},{4,12},{5,13},{6,14},{7,15},{8,0},{9,1},... | collective-permute-start | bytes 589832 | tf_op jit(solution)/shard_map/ppermute | solution.py:294
  35.9 2.0 %collective-permute-start.3 = (bf16[128,768]{1,0:T(8,128)(2,1)S(1)}, bf16[128,768]{1,0:T(8,128)(2,1)S(1)}, u32[]{:S(2)}, u32[]{:S(2)}) collective-permute-start(bf16[128,768]{1,0:T(8,128)(2,1)S(1)} %get-tuple-element.67), channel_id=1, source_target_pairs={{0,8},{1,9},{2,10},{3,11},{4,12},{5,13},{6,14},{7,15},{8,0},{9,1},... | collective-permute-start | bytes 589832 | tf_op jit(solution)/shard_map/ppermute | solution.py:294
  36.4 1.5 %collective-permute-start.4 = (bf16[128,768]{1,0:T(8,128)(2,1)S(1)}, bf16[128,768]{1,0:T(8,128)(2,1)S(1)}, u32[]{:S(2)}, u32[]{:S(2)}) collective-permute-start(bf16[128,768]{1,0:T(8,128)(2,1)S(1)} %get-tuple-element.66), channel_id=1, source_target_pairs={{0,8},{1,9},{2,10},{3,11},{4,12},{5,13},{6,14},{7,15},{8,0},{9,1},... | collective-permute-start | bytes 589832 | tf_op jit(solution)/shard_map/ppermute | solution.py:294
  36.4 1.7 %collective-permute-start.5 = (bf16[128,768]{1,0:T(8,128)(2,1)S(1)}, bf16[128,768]{1,0:T(8,128)(2,1)S(1)}, u32[]{:S(2)}, u32[]{:S(2)}) collective-permute-start(bf16[128,768]{1,0:T(8,128)(2,1)S(1)} %get-tuple-element.65), channel_id=1, source_target_pairs={{0,8},{1,9},{2,10},{3,11},{4,12},{5,13},{6,14},{7,15},{8,0},{9,1},... | collective-permute-start | bytes 589832 | tf_op jit(solution)/shard_map/ppermute | solution.py:294
  36.9 3.6 %copy-start.2 = (bf16[1,17,2,64,256]{4,3,2,1,0:T(8,128)(2,1)S(1)}, bf16[1,17,2,64,256]{4,3,2,1,0:T(8,128)(2,1)}, u32[]{:S(2)}) copy-start(bf16[1,17,2,64,256]{4,3,2,1,0:T(8,128)(2,1)} %param.4) | copy-start | bytes 3342340
  36.9 3.6 %copy-start.4 = (bf16[3,256,256]{2,1,0:T(8,128)(2,1)S(1)}, bf16[3,256,256]{2,1,0:T(8,128)(2,1)}, u32[]{:S(2)}) copy-start(bf16[3,256,256]{2,1,0:T(8,128)(2,1)} %refs_2_.2) | copy-start | bytes 1179652
  36.9 12.9 %collective-permute-start.8 = (bf16[1088,256]{1,0:T(8,128)(2,1)S(1)}, bf16[1088,256]{1,0:T(8,128)(2,1)S(1)}, u32[]{:S(2)}, u32[]{:S(2)}) collective-permute-start(bf16[1088,256]{1,0:T(8,128)(2,1)S(1)} %get-tuple-element.41.refs_0_), channel_id=1, source_target_pairs={{1,2},{2,1},{3,4},{4,3},{5,6},{6,5},{9,10},{10,9},{11,12},{12,11},... | collective-permute-start | bytes 1671176 | tf_op jit(solution)/shard_map/ppermute | solution.py:367
  38.4 7.8 %collective-permute-start.6 = (bf16[128,768]{1,0:T(8,128)(2,1)S(1)}, bf16[128,768]{1,0:T(8,128)(2,1)S(1)}, u32[]{:S(2)}, u32[]{:S(2)}) collective-permute-start(bf16[128,768]{1,0:T(8,128)(2,1)S(1)} %get-tuple-element.68), channel_id=1, source_target_pairs={{0,16},{1,17},{2,18},{3,19},{4,20},{5,21},{6,22},{7,23},{8,24},{9,... | collective-permute-start | bytes 589832 | tf_op jit(solution)/shard_map/ppermute | solution.py:294
  39.9 9.8 %collective-permute-start.7 = (bf16[128,768]{1,0:T(8,128)(2,1)S(1)}, bf16[128,768]{1,0:T(8,128)(2,1)S(1)}, u32[]{:S(2)}, u32[]{:S(2)}) collective-permute-start(bf16[128,768]{1,0:T(8,128)(2,1)S(1)} %get-tuple-element.69), channel_id=1, source_target_pairs={{0,16},{1,17},{2,18},{3,19},{4,20},{5,21},{6,22},{7,23},{8,24},{9,... | collective-permute-start | bytes 589832 | tf_op jit(solution)/shard_map/ppermute | solution.py:294
  43.1 18.1 %copy-start.6 = (bf16[1,17,2,64,256]{4,3,2,1,0:T(8,128)(2,1)S(1)}, bf16[1,17,2,64,256]{4,3,2,1,0:T(8,128)(2,1)}, u32[]{:S(2)}) copy-start(bf16[1,17,2,64,256]{4,3,2,1,0:T(8,128)(2,1)} %param.5) | copy-start | bytes 3342340
  49.8 19.3 %collective-permute-start.12 = (bf16[1088,256]{1,0:T(8,128)(2,1)S(1)}, bf16[1088,256]{1,0:T(8,128)(2,1)S(1)}, u32[]{:S(2)}, u32[]{:S(2)}) collective-permute-start(bf16[1088,256]{1,0:T(8,128)(2,1)S(1)} %get-tuple-element.47.refs_1_), channel_id=1, source_target_pairs={{0,1},{1,0},{2,3},{3,2},{4,5},{5,4},{6,7},{7,6},{8,9},{9,8},{10,11... | collective-permute-start | bytes 1671176 | tf_op jit(solution)/shard_map/ppermute | solution.py:362
  57.1 8.2 %collective-permute-start.10 = (bf16[64,768]{1,0:T(8,128)(2,1)S(1)}, bf16[64,768]{1,0:T(8,128)(2,1)S(1)}, u32[]{:S(2)}, u32[]{:S(2)}) collective-permute-start(bf16[64,768]{1,0:T(8,128)(2,1)S(1)} %get-tuple-element.71), channel_id=1, source_target_pairs={{0,2},{1,3},{2,0},{3,1},{4,6},{5,7},{6,4},{7,5},{8,10},{9,11},{10,... | collective-permute-start | bytes 294920 | tf_op jit(solution)/shard_map/ppermute | solution.py:294
  58.7 7.3 %collective-permute-start.11 = (bf16[64,768]{1,0:T(8,128)(2,1)S(1)}, bf16[64,768]{1,0:T(8,128)(2,1)S(1)}, u32[]{:S(2)}, u32[]{:S(2)}) collective-permute-start(bf16[64,768]{1,0:T(8,128)(2,1)S(1)} %get-tuple-element.70), channel_id=1, source_target_pairs={{0,6},{1,7},{2,4},{3,5},{4,2},{5,3},{6,0},{7,1},{8,14},{9,15},{10,... | collective-permute-start | bytes 294920 | tf_op jit(solution)/shard_map/ppermute | solution.py:294
  61.2 8.0 %collective-permute-start.9 = (bf16[64,768]{1,0:T(8,128)(2,1)S(1)}, bf16[64,768]{1,0:T(8,128)(2,1)S(1)}, u32[]{:S(2)}, u32[]{:S(2)}) collective-permute-start(bf16[64,768]{1,0:T(8,128)(2,1)S(1)} %get-tuple-element.72), channel_id=1, source_target_pairs={{0,4},{1,5},{2,6},{3,7},{4,0},{5,1},{6,2},{7,3},{8,12},{9,13},{10,... | collective-permute-start | bytes 294920 | tf_op jit(solution)/shard_map/ppermute | solution.py:294
  69.2 4.7 %collective-permute-start.13 = (bf16[64,768]{1,0:T(8,128)(2,1)S(1)}, bf16[64,768]{1,0:T(8,128)(2,1)S(1)}, u32[]{:S(2)}, u32[]{:S(2)}) collective-permute-start(bf16[64,768]{1,0:T(8,128)(2,1)S(1)} %add_convert_fusion.2), channel_id=1, source_target_pairs={{0,1},{1,0},{2,3},{3,2},{4,5},{5,4},{6,7},{7,6},{8,9},{9,8},{10,11... | collective-permute-start | bytes 294920 | tf_op jit(solution)/shard_map/ppermute | solution.py:294
  73.9 5.8 %collective-permute-start.14 = (bf16[64,768]{1,0:T(8,128)(2,1)S(1)}, bf16[64,768]{1,0:T(8,128)(2,1)S(1)}, u32[]{:S(2)}, u32[]{:S(2)}) collective-permute-start(bf16[64,768]{1,0:T(8,128)(2,1)S(1)} %get-tuple-element.63), channel_id=1, source_target_pairs={{0,4},{1,5},{2,6},{3,7},{4,0},{5,1},{6,2},{7,3},{8,12},{9,13},{10,... | collective-permute-start | bytes 294920 | tf_op jit(solution)/shard_map/ppermute | solution.py:294
  79.7 7.5 %collective-permute-start.15 = (bf16[128,768]{1,0:T(8,128)(2,1)S(1)}, bf16[128,768]{1,0:T(8,128)(2,1)S(1)}, u32[]{:S(2)}, u32[]{:S(2)}) collective-permute-start(bf16[128,768]{1,0:T(8,128)(2,1)S(1)} %pad_maximum_fusion.1), channel_id=1, source_target_pairs={{0,2},{1,3},{2,0},{3,1},{4,6},{5,7},{6,4},{7,5},{8,10},{9,11},{10,... | collective-permute-start | bytes 589832 | tf_op jit(solution)/shard_map/ppermute | solution.py:294
  81.5 8.4 %collective-permute-start.16 = (bf16[128,768]{1,0:T(8,128)(2,1)S(1)}, bf16[128,768]{1,0:T(8,128)(2,1)S(1)}, u32[]{:S(2)}, u32[]{:S(2)}) collective-permute-start(bf16[128,768]{1,0:T(8,128)(2,1)S(1)} %pad_maximum_fusion.1), channel_id=1, source_target_pairs={{0,16},{1,17},{2,18},{3,19},{4,20},{5,21},{6,22},{7,23},{8,24},{9,... | collective-permute-start | bytes 589832 | tf_op jit(solution)/shard_map/ppermute | solution.py:294
  83.0 6.9 %collective-permute-start.17 = (bf16[128,768]{1,0:T(8,128)(2,1)S(1)}, bf16[128,768]{1,0:T(8,128)(2,1)S(1)}, u32[]{:S(2)}, u32[]{:S(2)}) collective-permute-start(bf16[128,768]{1,0:T(8,128)(2,1)S(1)} %pad_maximum_fusion.1), channel_id=1, source_target_pairs={{0,18},{1,19},{2,16},{3,17},{4,22},{5,23},{6,20},{7,21},{8,26},{9,... | collective-permute-start | bytes 589832 | tf_op jit(solution)/shard_map/ppermute | solution.py:294
  89.9 2.4 %collective-permute-start.18 = (bf16[512,768]{1,0:T(8,128)(2,1)S(1)}, bf16[512,768]{1,0:T(8,128)(2,1)S(1)}, u32[]{:S(2)}, u32[]{:S(2)}) collective-permute-start(bf16[512,768]{1,0:T(8,128)(2,1)S(1)} %constant_dynamic-update-slice_fusion.sums), channel_id=1, source_target_pairs={{0,8},{1,9},{2,10},{3,11},{4,12},{5,13},{6,14},{7,15},{8,0},{9,1},... | collective-permute-start | bytes 2359304 | tf_op jit(solution)/shard_map/ppermute | solution.py:294

commit v4 on v3

--- a/solution.py
+++ b/solution.py
@@ -1,5 +1,4 @@
 import functools
-import itertools
 import math
 
 import jax
@@ -69,6 +68,10 @@
     return jnp.where(code[0] == 0, 1 + step, 1 - step)
 
 
+def if_far(code, x):
+    return x * code[3].astype(F32)
+
+
 def shift_right(tile):
     w = lax.broadcasted_iota(jnp.int32, tile.shape, 0)
     return jnp.where(w == 0, 0.0, pltpu.roll(tile, 1, 0))
@@ -158,7 +161,7 @@
     for n in range(2):
         ahead.append(start(lat.at[:, row_at(code, count - 1 + n, rows)], next_ext.at[n], next_sems.at[5 + n]))
     for b in range(3):
-        taps[b] = mm(halo[...], ws[tap_at(code, -1), b])
+        taps[b] = if_far(code, mm(halo[...], ws[tap_at(code, -1), b]))
     for n in range(count):
         for copy in copies[n][0]:
             copy.wait()
@@ -171,7 +174,7 @@
             if kind == 3:
                 part = outer(acts[n][...], cots[n].reshape(cells, 3 * chans))
             elif kind + n == 0:
-                part = outer(halo[...], spread[n])
+                part = if_far(code, outer(halo[...], spread[n]))
             else:
                 part = outer(ext[n + kind - 1].reshape(cells, chans), spread[n])
             out = part if out is None else out + part
@@ -247,6 +250,7 @@
         for n, (step, halo) in enumerate(halos):
             for b in range(3):
                 out = mm_t(halo[...], ws[tap_at(code, step), b])
+                out = if_far(code, out) if halo is far else out
                 taps[b] = out if n == 0 else taps[b] + out
 
         @pl.loop(0, planes)
@@ -327,7 +331,9 @@
     for group, split in groups:
         for step in group if split else ():
             word = 2 * word + bit_at(step)
-    return jnp.stack([jnp.asarray(x, jnp.int32) for x in (bit_at(("tm", 1)), bit_at(("dp", 1)), word)])
+    band = lax.axis_index("tm")
+    has_far = jnp.where((band == 0) | (band == lax.axis_size("tm") - 1), 0, 1)
+    return jnp.stack([jnp.asarray(x, jnp.int32) for x in (bit_at(("tm", 1)), bit_at(("dp", 1)), word, has_far)])
 
 
 def subsets(group):
@@ -343,15 +349,13 @@
         count = 2 - len(shared) % 2
         plan.append((shared[-count:], True, False))
         shared = shared[:-count]
-    works = beside[: len(plan)]
-    works[-1:] = [dict(itertools.chain.from_iterable(work.items() for work in beside[len(works) - 1 :]))]
     for n, (group, split, down) in enumerate(plan):
         others = subsets(group)
         size = mine.shape[0] // (len(others) + 1) if split and down else 0
         move = send_pieces if down else send
         got = [move(mine[(k + 1) * size : (k + 2) * size] if size else mine, steps) for k, steps in enumerate(others)]
-        if n < len(works):
-            got, also = lax.optimization_barrier((got, {name: run(mine) for name, run in works[n].items()}))
+        for run in beside[n : None if n == len(plan) - 1 else n + 1]:
+            got, also = lax.optimization_barrier((got, run(mine)))
             there |= also
         mine = plus(mine[:size] if size else mine, *got) if down else jnp.concatenate([mine, *got], axis=0)
     return mine, send(mine, core)
@@ -363,8 +367,13 @@
 
 
 def from_far(x):
-    count = lax.axis_size("tm")
-    return lax.ppermute(x, "tm", [(i, j) for i in range(count) if 0 <= (j := ((i - 1) ^ 1) + 1) < count])
+    wide, tall = lax.axis_size("dp"), lax.axis_size("tm")
+    pairs = []
+    for d in range(wide):
+        for i in range(tall):
+            j = ((i - 1) ^ 1) + 1
+            pairs.append((d * tall + i, d * tall + j if 0 <= j < tall else (d ^ 1) * tall + i))
+    return lax.ppermute(x, ("dp", "tm"), pairs)
 
 
 def after(x, *others):
@@ -435,23 +444,27 @@
     acts, pgs = acts + [act], pgs + [pg]
     image = jax.ShapeDtypeStruct(lat.shape, BF16)
 
-    def out(_):
-        return call(
+    def beside_first(gate):
+        (block_out,) = call(
             functools.partial(out_kernel, shift), [image], [padded], 12, 3 * rows * unit,
             [code, lat, *acts, temporal_weight],
-        )[0]
-
-    def back(_):
-        return call(
+        )
+        later.append(from_near(after(pgs[-1], gate)))
+        return {"far": there["far"], "out": block_out}
+
+    def beside_second(_):
+        (back_loc,) = call(
             back_kernel, [jax.ShapeDtypeStruct((rows, cells, chans), F32)], [taps], 12,
             (9 * rows - 6) * unit, [code, cot, *pgs, spatial_weight],
-        )[0]
-
-    def last(_):
-        return call(
+        )
+        return {"near": later[0], "back": back_loc}
+
+    def beside_last(_):
+        (latents_grad,) = call(
             last_kernel, [image], [taps], 12, 6 * unit,
-            [code, there["back"], keep(spatial_weight), keep(there["far"]), keep(there["near"])],
-        )[0]
+            [code, there["back"], *map(keep, (spatial_weight, there["far"], there["near"]))],
+        )
+        return {"grad": latents_grad}
 
     def ordered(sums, *given):
         return call(
@@ -462,15 +475,10 @@
             far=(2, 3), out_far=True, aliases={2: 0, 3: 1} if given else None,
         )
 
-    beside = [
-        {"far": lambda _: there["far"], "out": out},
-        {"near": lambda gate: from_near(after(pgs[-1], gate)), "back": back},
-        {},
-        {},
-        {"last": last},
-    ]
+    later = []
+    beside = [beside_first, beside_second, lambda _: {}, lambda _: {}, beside_last]
     mine, other = add_up(sums[0], sums[1], groups, beside, there)
-    latents_grad, block_out = there["last"], there["out"]
+    block_out, latents_grad = there["out"], there["grad"]
     spatial_grad, temporal_grad = ordered(other, *ordered(mine))
 
     def home(x):

time: 94.5 us -> 90.1 us (0.953)
  starting transfers between devices: 30.1 us -> 25.7 us
    ppermute x2, starting transfers between devices: 13 us -> 6.87 us  [from_near(): lax.ppermute(x, 'tm', [(i, i ^ 1) for i in range(count) if i ^ 1 < count])]
    ppermute x15, starting transfers between devices: 15.4 us -> 18.3 us  [send(): lax.ppermute(x, ('dp', 'tm'), [(i, i ^ mask) for i in range(wide * tall)])]
    ppermute x2, starting transfers between devices: 1.69 us -> 0.6 us  [from_far(): return lax.ppermute(x, ('dp', 'tm'), pairs)]
  transfers between devices with their start and end apart: 19 -> 19, of which waited for: 10 -> 14; matrix products, arithmetic and copies ran while one was open for 0% -> 1% of each run, Pallas kernels for 27% -> 29%
where the time goes in v4:
time: 90.1 us; the launch traced here: 89 us
  Pallas kernels  31.9 us (35%)
  waiting for transfers between devices  26.5 us (29%)
  starting transfers between devices  25.7 us (29%)
  local copies, waits for them, and re-layouts  3.55 us (4%)
    pallas_call x9, Pallas kernels, call(): pl.pallas_call(kernel, out_shape=outs, in_specs=specs, out_specs=[ANY if...  31.9 us
    ppermute x15, waiting for transfers between devices, send(): lax.ppermute(x, ('dp', 'tm'), [(i, i ^ mask) for i in range(wide * tall)])  19.1 us
    ppermute x15, starting transfers between devices, send(): lax.ppermute(x, ('dp', 'tm'), [(i, i ^ mask) for i in range(wide * tall)])  18.3 us
    ppermute x2, waiting for transfers between devices, from_near(): lax.ppermute(x, 'tm', [(i, i ^ 1) for i in range(count) if i ^ 1 < count])  7.47 us
    ppermute x2, starting transfers between devices, from_near(): lax.ppermute(x, 'tm', [(i, i ^ 1) for i in range(count) if i ^ 1 < count])  6.87 us
    unnamed x17, local copies, waits for them, and re-layouts  2.3 us
  transfers between devices with their start and end apart: 19, of which 14 were waited for; matrix products, arithmetic and copies ran while one was open for 1% of the time, Pallas kernels for 29%

profile of v4, /device:TPU:0, one launch (start us, length us, event | category | flops | bytes accessed | tf_op | source)
XLA Modules:
  0.0 89.0 jit_solution(11187720752428242487)
XLA Ops:
  0.6 1.1 %constant_dynamic-slice_fusion = bf16[1,17,1,64,256]{4,3,2,1,0:T(8,128)(2,1)S(1)} fusion(bf16[1,17,2,64,256]{4,3,2,1,0:T(8,128)(2,1)} %param.4, s32[]{:T(128)S(6)} %select_n.60), kind=kLoop, calls=%fused_computation.17 | loop fusion | bytes 1114116 | tf_op jit(solution)/shard_map/jit(dynamic_index_in_dim)/dynamic_slice | solution.py:396
  1.8 0.5 collective-permute-start.1
  2.3 0.1 pad_add_fusion.code
  2.3 0.0 copy-start.3
  2.3 1.0 %copy-done.3 = bf16[3,256,256]{2,1,0:T(8,128)(2,1)S(1)} copy-done((bf16[3,256,256]{2,1,0:T(8,128)(2,1)S(1)}, bf16[3,256,256]{2,1,0:T(8,128)(2,1)}, u32[]{:S(2)}) %copy-start.3) | copy-done | bytes 393240
  3.3 0.0 copy-start.5
  3.3 1.2 %copy-done.5 = bf16[1,17,2,64,256]{4,3,2,1,0:T(8,128)(2,1)S(1)} copy-done((bf16[1,17,2,64,256]{4,3,2,1,0:T(8,128)(2,1)S(1)}, bf16[1,17,2,64,256]{4,3,2,1,0:T(8,128)(2,1)}, u32[]{:S(2)}) %copy-start.5) | copy-done | bytes 1114136
  4.6 0.0 copy-start.1
  4.6 0.0 copy-start
  4.6 2.6 %shard_map.75.act_grad = bf16[2,1088,256]{2,1,0:T(8,128)(2,1)} custom-call(s32[4]{0:T(128)S(1)} %pad_add_fusion.code, bf16[17,2,64,256]{3,2,1,0:T(8,128)(2,1)S(1)} %bitcast.26, bf16[3,256,256]{2,1,0:T(8,128)(2,1)S(1)} %copy-done.3), custom_call_target="tpu_custom_call" | custom-call | flops 855638016 | bytes 2621456 | tf_op jit(solution)/shard_map/pallas_call | solution.py:45
  7.2 0.0 copy-done.1
  7.2 4.1 %collective-permute-start = (bf16[1088,256]{1,0:T(8,128)(2,1)S(1)}, bf16[1088,256]{1,0:T(8,128)(2,1)S(1)}, u32[]{:S(2)}, u32[]{:S(2)}) collective-permute-start(bf16[1088,256]{1,0:T(8,128)(2,1)S(1)} %bitcast.31), channel_id=1, source_target_pairs={{0,1},{1,0},{2,3},{3,2},{4,5},{5,4},{6,7},{7,6},{8,9},{9,8},{10,11... | collective-permute-start | bytes 1671176 | tf_op jit(solution)/shard_map/ppermute | solution.py:366
  11.3 0.0 copy-done
  11.3 5.2 %shard_map.76.pre_loc = f32[2,1088,256]{2,1,0:T(8,128)} custom-call(s32[4]{0:T(128)S(1)} %pad_add_fusion.code, bf16[17,2,64,256]{3,2,1,0:T(8,128)(2,1)S(1)} %bitcast.23, bf16[3,3,256,256]{3,2,1,0:T(8,128)(2,1)S(1)} %copy-done), custom_call_target="tpu_custom_call" | custom-call | flops 1711276032 | bytes 4522000 | tf_op jit(solution)/shard_map/pallas_call | solution.py:45
  16.5 0.0 collective-permute-done.1.halo
  16.5 5.5 %shard_map.77 = (bf16[1088,256]{1,0:T(8,128)(2,1)S(1)}, bf16[1088,256]{1,0:T(8,128)(2,1)S(1)}, f32[1024,768]{1,0:T(8,128)S(1)}, f32[1088,256]{1,0:T(8,128)S(1)},...) custom-call(s32[4]{0:T(128)S(1)} %pad_add_fusion.code, ...), custom_call_target="tpu_custom_call" | custom-call | flops 2139095040 | bytes 16023568 | tf_op jit(solution)/shard_map/pallas_call | solution.py:45
  22.0 7.5 %collective-permute-done.halo = bf16[1088,256]{1,0:T(8,128)(2,1)S(1)} collective-permute-done((bf16[1088,256]{1,0:T(8,128)(2,1)S(1)}, bf16[1088,256]{1,0:T(8,128)(2,1)S(1)}, u32[]{:S(2)}, u32[]{:S(2)}) %collective-permute-start) | collective-permute-done | bytes 557088 | tf_op jit(solution)/shard_map/ppermute | solution.py:366
  29.5 4.4 %shard_map.78 = (bf16[1088,256]{1,0:T(8,128)(2,1)S(1)}, bf16[1088,256]{1,0:T(8,128)(2,1)S(1)}, bf16[2,512,768]{2,1,0:T(8,128)(2,1)S(1)}) custom-call(s32[4]{0:T(128)S(1)} %pad_add_fusion.code, bf16[1088,256]{1,0:T(8,128)(2,1)S(1)} %collective-permute-done.halo, bf16[3,3,256,256]{3,2,1,0:T(8,128)(2,1)S(1)} %copy-done, ...), custom_call_target="tpu_custom_call" | custom-call | flops 2139095040 | bytes 12025872 | tf_op jit(solution)/shard_map/pallas_call | solution.py:45
  33.9 0.1 slice_bitcast_fusion.3
  34.0 0.1 collective-permute-start.2
  34.0 0.5 collective-permute-start.3
  34.5 0.1 collective-permute-start.4
  34.6 0.4 collective-permute-start.5
  35.0 0.1 collective-permute-start.8
  35.1 0.3 collective-permute-done.2
  35.5 0.3 collective-permute-done.3
  35.7 0.3 collective-permute-done.4
  36.0 0.3 collective-permute-done.5
  36.3 0.2 fusion
  36.6 1.6 %collective-permute-start.6 = (bf16[128,768]{1,0:T(8,128)(2,1)S(1)}, bf16[128,768]{1,0:T(8,128)(2,1)S(1)}, u32[]{:S(2)}, u32[]{:S(2)}) collective-permute-start(bf16[128,768]{1,0:T(8,128)(2,1)S(1)} %get-tuple-element.68), channel_id=1, source_target_pairs={{0,16},{1,17},{2,18},{3,19},{4,20},{5,21},{6,22},{7,23},{8,24},{9,... | collective-permute-start | bytes 589832 | tf_op jit(solution)/shard_map/ppermute | solution.py:298
  38.1 0.5 collective-permute-start.7
  38.6 0.0 copy-done.2
  38.7 0.0 copy-done.4
  38.7 2.6 %shard_map.79 = bf16[17,2,64,256]{3,2,1,0:T(8,128)(2,1)} custom-call(s32[4]{0:T(128)S(1)} %pad_add_fusion.code, bf16[17,2,64,256]{3,2,1,0:T(8,128)(2,1)S(1)} %bitcast.24, bf16[1088,256]{1,0:T(8,128)(2,1)S(1)} %get-tuple-element.42.refs_0_, bf16[1088,256]{1,0:T(8,128)(2,1)S(1)} %get-tuple-element.43.refs_1_, bf16[3,256,256]{2,1,0:T(8,128)(2,1)S(1)} %copy-done.4), custom_call_target="tpu_custom_call" | custom-call | flops 855638016 | bytes 3735568 | tf_op jit(solution)/shard_map/pallas_call | solution.py:45
  41.3 2.8 %collective-permute-start.12 = (bf16[1088,256]{1,0:T(8,128)(2,1)S(1)}, bf16[1088,256]{1,0:T(8,128)(2,1)S(1)}, u32[]{:S(2)}, u32[]{:S(2)}) collective-permute-start(bf16[1088,256]{1,0:T(8,128)(2,1)S(1)} %get-tuple-element.47.refs_1_), channel_id=1, source_target_pairs={{0,1},{1,0},{2,3},{3,2},{4,5},{5,4},{6,7},{7,6},{8,9},{9,8},{10,11... | collective-permute-start | bytes 1671176 | tf_op jit(solution)/shard_map/ppermute | solution.py:366
  44.0 0.3 collective-permute-done.6
  44.4 3.5 %collective-permute-done.7 = bf16[128,768]{1,0:T(8,128)(2,1)S(1)} collective-permute-done((bf16[128,768]{1,0:T(8,128)(2,1)S(1)}, bf16[128,768]{1,0:T(8,128)(2,1)S(1)}, u32[]{:S(2)}, u32[]{:S(2)}) %collective-permute-start.7) | collective-permute-done | bytes 196640 | tf_op jit(solution)/shard_map/ppermute | solution.py:298
  47.9 0.0 collective-permute-done.8.far
  47.9 0.1 add_convert_fusion
  48.1 5.3 %collective-permute-start.10 = (bf16[64,768]{1,0:T(8,128)(2,1)S(1)}, bf16[64,768]{1,0:T(8,128)(2,1)S(1)}, u32[]{:S(2)}, u32[]{:S(2)}) collective-permute-start(bf16[64,768]{1,0:T(8,128)(2,1)S(1)} %get-tuple-element.71), channel_id=1, source_target_pairs={{0,2},{1,3},{2,0},{3,1},{4,6},{5,7},{6,4},{7,5},{8,10},{9,11},{10,... | collective-permute-start | bytes 294920 | tf_op jit(solution)/shard_map/ppermute | solution.py:298
  53.4 2.5 %collective-permute-start.11 = (bf16[64,768]{1,0:T(8,128)(2,1)S(1)}, bf16[64,768]{1,0:T(8,128)(2,1)S(1)}, u32[]{:S(2)}, u32[]{:S(2)}) collective-permute-start(bf16[64,768]{1,0:T(8,128)(2,1)S(1)} %get-tuple-element.70), channel_id=1, source_target_pairs={{0,6},{1,7},{2,4},{3,5},{4,2},{5,3},{6,0},{7,1},{8,14},{9,15},{10,... | collective-permute-start | bytes 294920 | tf_op jit(solution)/shard_map/ppermute | solution.py:298
  55.9 0.1 collective-permute-start.9
  56.0 0.0 copy-done.6
  56.0 4.0 %shard_map.80.back_loc = f32[2,1088,256]{2,1,0:T(8,128)S(1)} custom-call(s32[4]{0:T(128)S(1)} %pad_add_fusion.code, bf16[17,2,64,256]{3,2,1,0:T(8,128)(2,1)S(1)} %bitcast.27, bf16[1088,256]{1,0:T(8,128)(2,1)S(1)} %get-tuple-element.41.refs_0_, bf16[1088,256]{1,0:T(8,128)(2,1)S(1)} %get-tuple-element.47.refs_1_, bf16[3,3,256,256]{3,2,1,0:T(8,128)(2,1)S(1)} %copy-done), custom_call_target="tpu_custom_call" | custom-call | flops 1711276032 | bytes 5636112 | tf_op jit(solution)/shard_map/pallas_call | solution.py:45
  60.0 0.0 collective-permute-done.10
  60.0 0.9 collective-permute-done.11
  60.9 3.3 %collective-permute-done.9 = bf16[64,768]{1,0:T(8,128)(2,1)S(1)} collective-permute-done((bf16[64,768]{1,0:T(8,128)(2,1)S(1)}, bf16[64,768]{1,0:T(8,128)(2,1)S(1)}, u32[]{:S(2)}, u32[]{:S(2)}) %collective-permute-start.9) | collective-permute-done | bytes 98336 | tf_op jit(solution)/shard_map/ppermute | solution.py:298
  64.2 0.0 collective-permute-done.12.near
  64.2 0.1 add_convert_fusion.2
  64.2 1.5 %collective-permute-start.13 = (bf16[64,768]{1,0:T(8,128)(2,1)S(1)}, bf16[64,768]{1,0:T(8,128)(2,1)S(1)}, u32[]{:S(2)}, u32[]{:S(2)}) collective-permute-start(bf16[64,768]{1,0:T(8,128)(2,1)S(1)} %add_convert_fusion.2), channel_id=1, source_target_pairs={{0,1},{1,0},{2,3},{3,2},{4,5},{5,4},{6,7},{7,6},{8,9},{9,8},{10,11... | collective-permute-start | bytes 294920 | tf_op jit(solution)/shard_map/ppermute | solution.py:298
  65.7 3.2 %collective-permute-done.13 = bf16[64,768]{1,0:T(8,128)(2,1)S(1)} collective-permute-done((bf16[64,768]{1,0:T(8,128)(2,1)S(1)}, bf16[64,768]{1,0:T(8,128)(2,1)S(1)}, u32[]{:S(2)}, u32[]{:S(2)}) %collective-permute-start.13) | collective-permute-done | bytes 98336 | tf_op jit(solution)/shard_map/ppermute | solution.py:298
  68.9 2.0 %collective-permute-start.14 = (bf16[64,768]{1,0:T(8,128)(2,1)S(1)}, bf16[64,768]{1,0:T(8,128)(2,1)S(1)}, u32[]{:S(2)}, u32[]{:S(2)}) collective-permute-start(bf16[64,768]{1,0:T(8,128)(2,1)S(1)} %get-tuple-element.63), channel_id=1, source_target_pairs={{0,4},{1,5},{2,6},{3,7},{4,0},{5,1},{6,2},{7,3},{8,12},{9,13},{10,... | collective-permute-start | bytes 294920 | tf_op jit(solution)/shard_map/ppermute | solution.py:298
  71.0 4.7 %collective-permute-done.14 = bf16[64,768]{1,0:T(8,128)(2,1)S(1)} collective-permute-done((bf16[64,768]{1,0:T(8,128)(2,1)S(1)}, bf16[64,768]{1,0:T(8,128)(2,1)S(1)}, u32[]{:S(2)}, u32[]{:S(2)}) %collective-permute-start.14) | collective-permute-done | bytes 98336 | tf_op jit(solution)/shard_map/ppermute | solution.py:298
  75.7 0.3 collective-permute-start.15
  76.0 1.5 %collective-permute-start.16 = (bf16[128,768]{1,0:T(8,128)(2,1)S(1)}, bf16[128,768]{1,0:T(8,128)(2,1)S(1)}, u32[]{:S(2)}, u32[]{:S(2)}) collective-permute-start(bf16[128,768]{1,0:T(8,128)(2,1)S(1)} %pad_maximum_fusion.1), channel_id=1, source_target_pairs={{0,16},{1,17},{2,18},{3,19},{4,20},{5,21},{6,22},{7,23},{8,24},{9,... | collective-permute-start | bytes 589832 | tf_op jit(solution)/shard_map/ppermute | solution.py:298
  77.5 1.7 %collective-permute-start.17 = (bf16[128,768]{1,0:T(8,128)(2,1)S(1)}, bf16[128,768]{1,0:T(8,128)(2,1)S(1)}, u32[]{:S(2)}, u32[]{:S(2)}) collective-permute-start(bf16[128,768]{1,0:T(8,128)(2,1)S(1)} %pad_maximum_fusion.1), channel_id=1, source_target_pairs={{0,18},{1,19},{2,16},{3,17},{4,22},{5,23},{6,20},{7,21},{8,26},{9,... | collective-permute-start | bytes 589832 | tf_op jit(solution)/shard_map/ppermute | solution.py:298
  79.2 3.9 %shard_map.81 = bf16[17,2,64,256]{3,2,1,0:T(8,128)(2,1)} custom-call(s32[4]{0:T(128)S(1)} %pad_add_fusion.code, f32[2,1088,256]{2,1,0:T(8,128)S(1)} %shard_map.80.back_loc, bf16[3,3,256,256]{3,2,1,0:T(8,128)(2,1)S(1)} %copy-done, bf16[1088,256]{1,0:T(8,128)(2,1)S(1)} %collective-permute-done.8.far, bf16[1088,256]{1,0:T(8,128)(2,1)S(1)} %collective-permute-done.12.near), custom_call_target="tpu_custom_call" | custom-call | flops 855638016 | bytes 5636112 | tf_op jit(solution)/shard_map/pallas_call | solution.py:45
  83.2 0.0 collective-permute-done.15
  83.2 0.6 collective-permute-done.16
  83.8 1.0 %collective-permute-done.17 = bf16[128,768]{1,0:T(8,128)(2,1)S(1)} collective-permute-done((bf16[128,768]{1,0:T(8,128)(2,1)S(1)}, bf16[128,768]{1,0:T(8,128)(2,1)S(1)}, u32[]{:S(2)}, u32[]{:S(2)}) %collective-permute-start.17) | collective-permute-done | bytes 196640 | tf_op jit(solution)/shard_map/ppermute | solution.py:298
  84.8 0.1 collective-permute-start.18
  84.9 1.8 %shard_map.82 = (f32[3,3,256,256]{3,2,1,0:T(8,128)}, f32[3,256,256]{2,1,0:T(8,128)}) custom-call(s32[4]{0:T(128)S(1)} %pad_add_fusion.code, bf16[512,768]{1,0:T(8,128)(2,1)S(1)} %constant_dynamic-update-slice_fusion.sums), custom_call_target="tpu_custom_call" | custom-call | bytes 3932176 | tf_op jit(solution)/shard_map/pallas_call | solution.py:45
  86.7 0.5 collective-permute-done.18.sums
  87.2 1.8 %shard_map.83 = (f32[3,3,256,256]{3,2,1,0:T(8,128)}, f32[3,256,256]{2,1,0:T(8,128)}) custom-call(s32[4]{0:T(128)S(1)} %pad_add_fusion.code, bf16[512,768]{1,0:T(8,128)(2,1)S(1)} %collective-permute-done.18.sums, f32[3,3,256,256]{3,2,1,0:T(8,128)} %get-tuple-element.58.refs_0_, ...), custom_call_target="tpu_custom_call", output_to_operand_aliasing={{0}: (2, {}), {1}: (3, {})} | custom-call | bytes 7077904 | tf_op jit(solution)/shard_map/pallas_call | solution.py:45
  (13 shorter events, 0.2 us)
Async XLA Ops:
  1.8 14.8 %collective-permute-start.1 = (bf16[1088,256]{1,0:T(8,128)(2,1)S(1)}, bf16[1088,256]{1,0:T(8,128)(2,1)S(1)}, u32[]{:S(2)}, u32[]{:S(2)}) collective-permute-start(bf16[1088,256]{1,0:T(8,128)(2,1)S(1)} %bitcast.30), channel_id=1, source_target_pairs={{0,8},{1,2},{2,1},{3,4},{4,3},{5,6},{6,5},{7,15},{8,0},{9,10},{10,... | collective-permute-start | bytes 1671176 | tf_op jit(solution)/shard_map/ppermute | solution.py:376
  2.3 1.0 %copy-start.3 = (bf16[3,256,256]{2,1,0:T(8,128)(2,1)S(1)}, bf16[3,256,256]{2,1,0:T(8,128)(2,1)}, u32[]{:S(2)}) copy-start(bf16[3,256,256]{2,1,0:T(8,128)(2,1)} %refs_2_.2) | copy-start | bytes 1179652
  3.3 1.2 %copy-start.5 = (bf16[1,17,2,64,256]{4,3,2,1,0:T(8,128)(2,1)S(1)}, bf16[1,17,2,64,256]{4,3,2,1,0:T(8,128)(2,1)}, u32[]{:S(2)}) copy-start(bf16[1,17,2,64,256]{4,3,2,1,0:T(8,128)(2,1)} %param.5) | copy-start | bytes 3342340
  4.6 2.6 %copy-start.1 = (bf16[1,17,2,64,256]{4,3,2,1,0:T(8,128)(2,1)S(1)}, bf16[1,17,2,64,256]{4,3,2,1,0:T(8,128)(2,1)}, u32[]{:S(2)}) copy-start(bf16[1,17,2,64,256]{4,3,2,1,0:T(8,128)(2,1)} %param.4) | copy-start | bytes 3342340
  4.6 6.8 %copy-start = (bf16[3,3,256,256]{3,2,1,0:T(8,128)(2,1)S(1)}, bf16[3,3,256,256]{3,2,1,0:T(8,128)(2,1)}, u32[]{:S(2)}) copy-start(bf16[3,3,256,256]{3,2,1,0:T(8,128)(2,1)} %ws.7) | copy-start | bytes 3538948
  7.2 22.3 %collective-permute-start = (bf16[1088,256]{1,0:T(8,128)(2,1)S(1)}, bf16[1088,256]{1,0:T(8,128)(2,1)S(1)}, u32[]{:S(2)}, u32[]{:S(2)}) collective-permute-start(bf16[1088,256]{1,0:T(8,128)(2,1)S(1)} %bitcast.31), channel_id=1, source_target_pairs={{0,1},{1,0},{2,3},{3,2},{4,5},{5,4},{6,7},{7,6},{8,9},{9,8},{10,11... | collective-permute-start | bytes 1671176 | tf_op jit(solution)/shard_map/ppermute | solution.py:366
  34.0 1.5 %collective-permute-start.2 = (bf16[128,768]{1,0:T(8,128)(2,1)S(1)}, bf16[128,768]{1,0:T(8,128)(2,1)S(1)}, u32[]{:S(2)}, u32[]{:S(2)}) collective-permute-start(bf16[128,768]{1,0:T(8,128)(2,1)S(1)} %get-tuple-element.64), channel_id=1, source_target_pairs={{0,8},{1,9},{2,10},{3,11},{4,12},{5,13},{6,14},{7,15},{8,0},{9,1},... | collective-permute-start | bytes 589832 | tf_op jit(solution)/shard_map/ppermute | solution.py:298
  34.0 1.7 %collective-permute-start.3 = (bf16[128,768]{1,0:T(8,128)(2,1)S(1)}, bf16[128,768]{1,0:T(8,128)(2,1)S(1)}, u32[]{:S(2)}, u32[]{:S(2)}) collective-permute-start(bf16[128,768]{1,0:T(8,128)(2,1)S(1)} %get-tuple-element.67), channel_id=1, source_target_pairs={{0,8},{1,9},{2,10},{3,11},{4,12},{5,13},{6,14},{7,15},{8,0},{9,1},... | collective-permute-start | bytes 589832 | tf_op jit(solution)/shard_map/ppermute | solution.py:298
  34.5 1.5 %collective-permute-start.4 = (bf16[128,768]{1,0:T(8,128)(2,1)S(1)}, bf16[128,768]{1,0:T(8,128)(2,1)S(1)}, u32[]{:S(2)}, u32[]{:S(2)}) collective-permute-start(bf16[128,768]{1,0:T(8,128)(2,1)S(1)} %get-tuple-element.66), channel_id=1, source_target_pairs={{0,8},{1,9},{2,10},{3,11},{4,12},{5,13},{6,14},{7,15},{8,0},{9,1},... | collective-permute-start | bytes 589832 | tf_op jit(solution)/shard_map/ppermute | solution.py:298
  34.6 1.7 %collective-permute-start.5 = (bf16[128,768]{1,0:T(8,128)(2,1)S(1)}, bf16[128,768]{1,0:T(8,128)(2,1)S(1)}, u32[]{:S(2)}, u32[]{:S(2)}) collective-permute-start(bf16[128,768]{1,0:T(8,128)(2,1)S(1)} %get-tuple-element.65), channel_id=1, source_target_pairs={{0,8},{1,9},{2,10},{3,11},{4,12},{5,13},{6,14},{7,15},{8,0},{9,1},... | collective-permute-start | bytes 589832 | tf_op jit(solution)/shard_map/ppermute | solution.py:298
  35.0 3.6 %copy-start.2 = (bf16[1,17,2,64,256]{4,3,2,1,0:T(8,128)(2,1)S(1)}, bf16[1,17,2,64,256]{4,3,2,1,0:T(8,128)(2,1)}, u32[]{:S(2)}) copy-start(bf16[1,17,2,64,256]{4,3,2,1,0:T(8,128)(2,1)} %param.4) | copy-start | bytes 3342340
  35.0 3.6 %copy-start.4 = (bf16[3,256,256]{2,1,0:T(8,128)(2,1)S(1)}, bf16[3,256,256]{2,1,0:T(8,128)(2,1)}, u32[]{:S(2)}) copy-start(bf16[3,256,256]{2,1,0:T(8,128)(2,1)} %refs_2_.2) | copy-start | bytes 1179652
  35.0 12.9 %collective-permute-start.8 = (bf16[1088,256]{1,0:T(8,128)(2,1)S(1)}, bf16[1088,256]{1,0:T(8,128)(2,1)S(1)}, u32[]{:S(2)}, u32[]{:S(2)}) collective-permute-start(bf16[1088,256]{1,0:T(8,128)(2,1)S(1)} %get-tuple-element.41.refs_0_), channel_id=1, source_target_pairs={{0,8},{1,2},{2,1},{3,4},{4,3},{5,6},{6,5},{7,15},{8,0},{9,10},{10,... | collective-permute-start | bytes 1671176 | tf_op jit(solution)/shard_map/ppermute | solution.py:376
  36.6 7.8 %collective-permute-start.6 = (bf16[128,768]{1,0:T(8,128)(2,1)S(1)}, bf16[128,768]{1,0:T(8,128)(2,1)S(1)}, u32[]{:S(2)}, u32[]{:S(2)}) collective-permute-start(bf16[128,768]{1,0:T(8,128)(2,1)S(1)} %get-tuple-element.68), channel_id=1, source_target_pairs={{0,16},{1,17},{2,18},{3,19},{4,20},{5,21},{6,22},{7,23},{8,24},{9,... | collective-permute-start | bytes 589832 | tf_op jit(solution)/shard_map/ppermute | solution.py:298
  38.1 9.8 %collective-permute-start.7 = (bf16[128,768]{1,0:T(8,128)(2,1)S(1)}, bf16[128,768]{1,0:T(8,128)(2,1)S(1)}, u32[]{:S(2)}, u32[]{:S(2)}) collective-permute-start(bf16[128,768]{1,0:T(8,128)(2,1)S(1)} %get-tuple-element.69), channel_id=1, source_target_pairs={{0,16},{1,17},{2,18},{3,19},{4,20},{5,21},{6,22},{7,23},{8,24},{9,... | collective-permute-start | bytes 589832 | tf_op jit(solution)/shard_map/ppermute | solution.py:298
  41.3 14.7 %copy-start.6 = (bf16[1,17,2,64,256]{4,3,2,1,0:T(8,128)(2,1)S(1)}, bf16[1,17,2,64,256]{4,3,2,1,0:T(8,128)(2,1)}, u32[]{:S(2)}) copy-start(bf16[1,17,2,64,256]{4,3,2,1,0:T(8,128)(2,1)} %param.5) | copy-start | bytes 3342340
  41.3 22.9 %collective-permute-start.12 = (bf16[1088,256]{1,0:T(8,128)(2,1)S(1)}, bf16[1088,256]{1,0:T(8,128)(2,1)S(1)}, u32[]{:S(2)}, u32[]{:S(2)}) collective-permute-start(bf16[1088,256]{1,0:T(8,128)(2,1)S(1)} %get-tuple-element.47.refs_1_), channel_id=1, source_target_pairs={{0,1},{1,0},{2,3},{3,2},{4,5},{5,4},{6,7},{7,6},{8,9},{9,8},{10,11... | collective-permute-start | bytes 1671176 | tf_op jit(solution)/shard_map/ppermute | solution.py:366
  48.1 12.0 %collective-permute-start.10 = (bf16[64,768]{1,0:T(8,128)(2,1)S(1)}, bf16[64,768]{1,0:T(8,128)(2,1)S(1)}, u32[]{:S(2)}, u32[]{:S(2)}) collective-permute-start(bf16[64,768]{1,0:T(8,128)(2,1)S(1)} %get-tuple-element.71), channel_id=1, source_target_pairs={{0,2},{1,3},{2,0},{3,1},{4,6},{5,7},{6,4},{7,5},{8,10},{9,11},{10,... | collective-permute-start | bytes 294920 | tf_op jit(solution)/shard_map/ppermute | solution.py:298
  53.4 7.5 %collective-permute-start.11 = (bf16[64,768]{1,0:T(8,128)(2,1)S(1)}, bf16[64,768]{1,0:T(8,128)(2,1)S(1)}, u32[]{:S(2)}, u32[]{:S(2)}) collective-permute-start(bf16[64,768]{1,0:T(8,128)(2,1)S(1)} %get-tuple-element.70), channel_id=1, source_target_pairs={{0,6},{1,7},{2,4},{3,5},{4,2},{5,3},{6,0},{7,1},{8,14},{9,15},{10,... | collective-permute-start | bytes 294920 | tf_op jit(solution)/shard_map/ppermute | solution.py:298
  55.9 8.3 %collective-permute-start.9 = (bf16[64,768]{1,0:T(8,128)(2,1)S(1)}, bf16[64,768]{1,0:T(8,128)(2,1)S(1)}, u32[]{:S(2)}, u32[]{:S(2)}) collective-permute-start(bf16[64,768]{1,0:T(8,128)(2,1)S(1)} %get-tuple-element.72), channel_id=1, source_target_pairs={{0,4},{1,5},{2,6},{3,7},{4,0},{5,1},{6,2},{7,3},{8,12},{9,13},{10,... | collective-permute-start | bytes 294920 | tf_op jit(solution)/shard_map/ppermute | solution.py:298
  64.2 4.7 %collective-permute-start.13 = (bf16[64,768]{1,0:T(8,128)(2,1)S(1)}, bf16[64,768]{1,0:T(8,128)(2,1)S(1)}, u32[]{:S(2)}, u32[]{:S(2)}) collective-permute-start(bf16[64,768]{1,0:T(8,128)(2,1)S(1)} %add_convert_fusion.2), channel_id=1, source_target_pairs={{0,1},{1,0},{2,3},{3,2},{4,5},{5,4},{6,7},{7,6},{8,9},{9,8},{10,11... | collective-permute-start | bytes 294920 | tf_op jit(solution)/shard_map/ppermute | solution.py:298
  68.9 6.7 %collective-permute-start.14 = (bf16[64,768]{1,0:T(8,128)(2,1)S(1)}, bf16[64,768]{1,0:T(8,128)(2,1)S(1)}, u32[]{:S(2)}, u32[]{:S(2)}) collective-permute-start(bf16[64,768]{1,0:T(8,128)(2,1)S(1)} %get-tuple-element.63), channel_id=1, source_target_pairs={{0,4},{1,5},{2,6},{3,7},{4,0},{5,1},{6,2},{7,3},{8,12},{9,13},{10,... | collective-permute-start | bytes 294920 | tf_op jit(solution)/shard_map/ppermute | solution.py:298
  75.7 7.5 %collective-permute-start.15 = (bf16[128,768]{1,0:T(8,128)(2,1)S(1)}, bf16[128,768]{1,0:T(8,128)(2,1)S(1)}, u32[]{:S(2)}, u32[]{:S(2)}) collective-permute-start(bf16[128,768]{1,0:T(8,128)(2,1)S(1)} %pad_maximum_fusion.1), channel_id=1, source_target_pairs={{0,2},{1,3},{2,0},{3,1},{4,6},{5,7},{6,4},{7,5},{8,10},{9,11},{10,... | collective-permute-start | bytes 589832 | tf_op jit(solution)/shard_map/ppermute | solution.py:298
  76.0 7.8 %collective-permute-start.16 = (bf16[128,768]{1,0:T(8,128)(2,1)S(1)}, bf16[128,768]{1,0:T(8,128)(2,1)S(1)}, u32[]{:S(2)}, u32[]{:S(2)}) collective-permute-start(bf16[128,768]{1,0:T(8,128)(2,1)S(1)} %pad_maximum_fusion.1), channel_id=1, source_target_pairs={{0,16},{1,17},{2,18},{3,19},{4,20},{5,21},{6,22},{7,23},{8,24},{9,... | collective-permute-start | bytes 589832 | tf_op jit(solution)/shard_map/ppermute | solution.py:298
  77.5 7.3 %collective-permute-start.17 = (bf16[128,768]{1,0:T(8,128)(2,1)S(1)}, bf16[128,768]{1,0:T(8,128)(2,1)S(1)}, u32[]{:S(2)}, u32[]{:S(2)}) collective-permute-start(bf16[128,768]{1,0:T(8,128)(2,1)S(1)} %pad_maximum_fusion.1), channel_id=1, source_target_pairs={{0,18},{1,19},{2,16},{3,17},{4,22},{5,23},{6,20},{7,21},{8,26},{9,... | collective-permute-start | bytes 589832 | tf_op jit(solution)/shard_map/ppermute | solution.py:298
  84.8 2.4 %collective-permute-start.18 = (bf16[512,768]{1,0:T(8,128)(2,1)S(1)}, bf16[512,768]{1,0:T(8,128)(2,1)S(1)}, u32[]{:S(2)}, u32[]{:S(2)}) collective-permute-start(bf16[512,768]{1,0:T(8,128)(2,1)S(1)} %constant_dynamic-update-slice_fusion.sums), channel_id=1, source_target_pairs={{0,8},{1,9},{2,10},{3,11},{4,12},{5,13},{6,14},{7,15},{8,0},{9,1},... | collective-permute-start | bytes 2359304 | tf_op jit(solution)/shard_map/ppermute | solution.py:298

commit v5 on v4

--- a/solution.py
+++ b/solution.py
@@ -11,7 +11,7 @@
 BF16 = jnp.bfloat16
 F32 = jnp.float32
 TILE_ROWS = 16
-PIECE_ROWS = 128
+PIECE_ROWS = 512
 VMEM = pl.BlockSpec(memory_space=pltpu.VMEM)
 SMEM = pl.BlockSpec(memory_space=pltpu.SMEM)
 ANY = pl.BlockSpec(memory_space=pl.ANY)
@@ -184,26 +184,41 @@
         copy.wait()
 
 
-def late_kernel(ends, scale, code, halo, ws, before, pres, grads, cots, ext, act, pg, sums, taps, spread):
-    _, planes, cols, chans = ext.shape
-    cells = planes * cols
+def late_kernel(ends, scale, code, halo, ws, before, pres, grads, cots, ext, act, pg, spread, sums, taps):
+    cols = ext.shape[2]
     for b in range(3):
         taps[b] = mm(halo[...], ws[tap_at(code, 1), b])
     point_grads(True, cols, taps, pres, grads, act, pg, spread)
+    half_grads(ends, scale, 1 - code[1], code, halo, before, cots, ext, act, spread, sums)
+
+
+def own_kernel(ends, scale, code, halo, before, cots, ext, act, spread, sums):
+    half_grads(ends, scale, code[1], code, halo, before, cots, ext, act, spread, sums)
+
+
+def half_grads(ends, scale, half, code, halo, before, cots, ext, act, spread, sums):
+    _, planes, cols, chans = ext.shape
+    cells = planes * cols
     size = 2 * chans // ends
-    for kind in range(4):
-        if kind == 3:
-            out = outer(act[...], cots[...].reshape(cells, 3 * chans))
-        elif kind == 2:
-            out = outer(halo[...], spread[...])
-        else:
-            out = outer(ext[kind].reshape(cells, chans), spread[...])
-        block = 3 if kind == 3 else tap_at(code, kind - 1)
-        out = (before[pl.ds(pl.multiple_of(block * chans, chans), chans)] + out) * scale
+
+    def put(block, a, b):
+        at = block * chans
+        out = (before[at : at + chans] + outer(a, b)) * scale
         for n in range(chans // size):
-            half, piece = lax.div(block, 2), lax.rem(block, 2) * (chans // size) + n
-            here = pl.multiple_of((piece ^ code[2]) * size, size)
-            sums[half ^ code[1], pl.ds(here, size)] = out[n * size : (n + 1) * size].astype(BF16)
+            here = pl.multiple_of(((block % 2 * (chans // size) + n) ^ code[2]) * size, size)
+            sums[pl.ds(here, size)] = out[n * size : (n + 1) * size].astype(BF16)
+
+    for odd in range(2):
+        for side in range(2):
+
+            @pl.when((code[0] == odd) & (half == side))
+            def _():
+                for block in (2 * side, 2 * side + 1):
+                    if block == 3:
+                        put(block, act[...], cots[...].reshape(cells, 3 * chans))
+                        continue
+                    kind = 2 - block if odd else block
+                    put(block, halo[...] if kind == 2 else ext[kind].reshape(cells, chans), spread[...])
 
 
 def out_kernel(shift, code, lat, *refs):
@@ -266,25 +281,30 @@
     spatial, temporal, blocks, sems = refs[-4:]
     chans = spatial.shape[-1]
     size = 2 * chans // ends
-    for slot in range(ends):
-        piece = slot ^ code[2]
-        block, at = lax.div(piece, chans // size), lax.rem(piece, chans // size) * size
-        for b in range(3):
-            found = sums[slot * size : (slot + 1) * size, b * chans : (b + 1) * chans]
-            blocks[block, b, pl.ds(pl.multiple_of(at, size), size)] = found.astype(F32)
     half = code[1] if own else 1 - code[1]
+    first = pltpu.make_async_copy(blocks.at[0], spatial.at[2 * half], sems.at[0])
+    second = pltpu.make_async_copy(blocks.at[1], spatial.at[1], sems.at[1])
+    second_last = pltpu.make_async_copy(blocks.at[1], temporal, sems.at[1])
+    for block in range(2):
+        for n in range(chans // size):
+            slot = (block * (chans // size) + n) ^ code[2]
+            found = sums[pl.ds(pl.multiple_of(slot * size, size), size)].astype(F32)
+            for b in range(3):
+                blocks[block, b, n * size : (n + 1) * size] = found[:, b * chans : (b + 1) * chans]
+        if block == 0:
+            first.start()
 
     @pl.when(half == 0)
     def _():
-        copies = [start(blocks.at[n], spatial.at[n], sems.at[n]) for n in range(2)]
-        for copy in copies:
-            copy.wait()
+        second.start()
+        second.wait()
 
     @pl.when(half != 0)
     def _():
-        copies = [start(blocks.at[0], spatial.at[2], sems.at[0]), start(blocks.at[1], temporal, sems.at[1])]
-        for copy in copies:
-            copy.wait()
+        second_last.start()
+        second_last.wait()
+
+    first.wait()
 
 
 def bits_of(axis):
@@ -435,11 +455,15 @@
     )
     acts, pgs = list(early[:count]), list(early[count : 2 * count])
     there["far"] = from_far(after(pgs[0], lat_near))
-    act, pg, sums = call(
+    half = pltpu.VMEM((2 * chans, 3 * chans), BF16)
+    act, pg, spread, other = call(
         functools.partial(late_kernel, ends, scale),
-        [narrow, narrow, jax.ShapeDtypeStruct((2, 2 * chans, 3 * chans), BF16)],
-        [taps, pltpu.VMEM((cells, 3 * chans), BF16)], 12, 15 * unit,
+        [narrow, narrow, pltpu.VMEM((cells, 3 * chans), BF16), half], [taps], 8, 9 * unit,
         [code, *map(keep, (lat_near, spatial_weight, *early[2 * count :]))],
+    )
+    (mine,) = call(
+        functools.partial(own_kernel, ends, scale), [half], [], 8, 6 * unit,
+        [code, *map(keep, (lat_near, early[2 * count], *early[2 * count + 3 :], act, spread))],
     )
     acts, pgs = acts + [act], pgs + [pg]
     image = jax.ShapeDtypeStruct(lat.shape, BF16)
@@ -477,7 +501,7 @@
 
     later = []
     beside = [beside_first, beside_second, lambda _: {}, lambda _: {}, beside_last]
-    mine, other = add_up(sums[0], sums[1], groups, beside, there)
+    mine, other = add_up(mine, other, groups, beside, there)
     block_out, latents_grad = there["out"], there["grad"]
     spatial_grad, temporal_grad = ordered(other, *ordered(mine))
 

time: 90.1 us -> 88.7 us (0.984)
  waiting for transfers between devices: 26.5 us -> 24.2 us
  starting transfers between devices: 25.7 us -> 26.7 us
    ppermute x15 -> x11, waiting for transfers between devices: 19.1 us -> 16.7 us  [send(): lax.ppermute(x, ('dp', 'tm'), [(i, i ^ mask) for i in range(wide * tall)])]
    pallas_call x9 -> x10, Pallas kernels: 31.9 us -> 32.7 us  [call(): pl.pallas_call(kernel, out_shape=outs, in_specs=specs, out_specs=[ANY if...]
    ppermute x15 -> x11, starting transfers between devices: 18.3 us -> 18 us  [send(): lax.ppermute(x, ('dp', 'tm'), [(i, i ^ mask) for i in range(wide * tall)])]
  transfers between devices with their start and end apart: 19 -> 15, of which waited for: 14 -> 8; matrix products, arithmetic and copies ran while one was open for 1% -> 1% of each run, Pallas kernels for 29% -> 31%
where the time goes in v5:
time: 88.7 us; the launch traced here: 88.5 us
  Pallas kernels  32.7 us (37%)
  starting transfers between devices  26.7 us (30%)
  waiting for transfers between devices  24.2 us (27%)
  local copies, waits for them, and re-layouts  3.5 us (4%)
  between operations  0.99 us (1%)
    pallas_call x10, Pallas kernels, call(): pl.pallas_call(kernel, out_shape=outs, in_specs=specs, out_specs=[ANY if...  32.7 us
    ppermute x11, starting transfers between devices, send(): lax.ppermute(x, ('dp', 'tm'), [(i, i ^ mask) for i in range(wide * tall)])  18 us
    ppermute x11, waiting for transfers between devices, send(): lax.ppermute(x, ('dp', 'tm'), [(i, i ^ mask) for i in range(wide * tall)])  16.7 us
    ppermute x2, starting transfers between devices, from_near(): lax.ppermute(x, 'tm', [(i, i ^ 1) for i in range(count) if i ^ 1 < count])  7.68 us
    ppermute x2, waiting for transfers between devices, from_near(): lax.ppermute(x, 'tm', [(i, i ^ 1) for i in range(count) if i ^ 1 < count])  7.48 us
    unnamed x17, local copies, waits for them, and re-layouts  2.3 us
  transfers between devices with their start and end apart: 15, of which 8 were waited for; matrix products, arithmetic and copies ran while one was open for 1% of the time, Pallas kernels for 31%

profile of v5, /device:TPU:0, one launch (start us, length us, event | category | flops | bytes accessed | tf_op | source)
XLA Modules:
  0.0 88.5 jit_solution(13221022131164985988)
XLA Ops:
  0.6 1.1 %constant_dynamic-slice_fusion = bf16[1,17,1,64,256]{4,3,2,1,0:T(8,128)(2,1)S(1)} fusion(bf16[1,17,2,64,256]{4,3,2,1,0:T(8,128)(2,1)} %param.4, s32[]{:T(128)S(6)} %select_n.60), kind=kLoop, calls=%fused_computation.11 | loop fusion | bytes 1114116 | tf_op jit(solution)/shard_map/jit(dynamic_index_in_dim)/dynamic_slice | solution.py:416
  1.8 0.5 collective-permute-start.1
  2.3 0.1 pad_add_fusion.code
  2.3 0.0 copy-start.3
  2.3 1.0 %copy-done.3 = bf16[3,256,256]{2,1,0:T(8,128)(2,1)S(1)} copy-done((bf16[3,256,256]{2,1,0:T(8,128)(2,1)S(1)}, bf16[3,256,256]{2,1,0:T(8,128)(2,1)}, u32[]{:S(2)}) %copy-start.3) | copy-done | bytes 393240
  3.3 0.0 copy-start.5
  3.3 1.2 %copy-done.5 = bf16[1,17,2,64,256]{4,3,2,1,0:T(8,128)(2,1)S(1)} copy-done((bf16[1,17,2,64,256]{4,3,2,1,0:T(8,128)(2,1)S(1)}, bf16[1,17,2,64,256]{4,3,2,1,0:T(8,128)(2,1)}, u32[]{:S(2)}) %copy-start.5) | copy-done | bytes 1114136
  4.6 0.0 copy-start.1
  4.6 0.0 copy-start
  4.6 2.6 %shard_map.75.act_grad = bf16[2,1088,256]{2,1,0:T(8,128)(2,1)} custom-call(s32[4]{0:T(128)S(1)} %pad_add_fusion.code, bf16[17,2,64,256]{3,2,1,0:T(8,128)(2,1)S(1)} %bitcast.15, bf16[3,256,256]{2,1,0:T(8,128)(2,1)S(1)} %copy-done.3), custom_call_target="tpu_custom_call" | custom-call | flops 855638016 | bytes 2621456 | tf_op jit(solution)/shard_map/pallas_call | solution.py:45
  7.2 0.0 copy-done.1
  7.2 4.1 %collective-permute-start = (bf16[1088,256]{1,0:T(8,128)(2,1)S(1)}, bf16[1088,256]{1,0:T(8,128)(2,1)S(1)}, u32[]{:S(2)}, u32[]{:S(2)}) collective-permute-start(bf16[1088,256]{1,0:T(8,128)(2,1)S(1)} %bitcast.20), channel_id=1, source_target_pairs={{0,1},{1,0},{2,3},{3,2},{4,5},{5,4},{6,7},{7,6},{8,9},{9,8},{10,11... | collective-permute-start | bytes 1671176 | tf_op jit(solution)/shard_map/ppermute | solution.py:386
  11.3 0.0 copy-done
  11.3 5.2 %shard_map.76.pre_loc = f32[2,1088,256]{2,1,0:T(8,128)} custom-call(s32[4]{0:T(128)S(1)} %pad_add_fusion.code, bf16[17,2,64,256]{3,2,1,0:T(8,128)(2,1)S(1)} %bitcast.12, bf16[3,3,256,256]{3,2,1,0:T(8,128)(2,1)S(1)} %copy-done), custom_call_target="tpu_custom_call" | custom-call | flops 1711276032 | bytes 4522000 | tf_op jit(solution)/shard_map/pallas_call | solution.py:45
  16.5 0.0 collective-permute-done.1.halo
  16.5 5.5 %shard_map.77 = (bf16[1088,256]{1,0:T(8,128)(2,1)S(1)}, bf16[1088,256]{1,0:T(8,128)(2,1)S(1)}, f32[1024,768]{1,0:T(8,128)S(1)}, f32[1088,256]{1,0:T(8,128)S(1)},...) custom-call(s32[4]{0:T(128)S(1)} %pad_add_fusion.code, ...), custom_call_target="tpu_custom_call" | custom-call | flops 2139095040 | bytes 16023568 | tf_op jit(solution)/shard_map/pallas_call | solution.py:45
  22.1 7.5 %collective-permute-done.halo = bf16[1088,256]{1,0:T(8,128)(2,1)S(1)} collective-permute-done((bf16[1088,256]{1,0:T(8,128)(2,1)S(1)}, bf16[1088,256]{1,0:T(8,128)(2,1)S(1)}, u32[]{:S(2)}, u32[]{:S(2)}) %collective-permute-start) | collective-permute-done | bytes 557088 | tf_op jit(solution)/shard_map/ppermute | solution.py:386
  29.5 3.3 %shard_map.78 = (bf16[1088,256]{1,0:T(8,128)(2,1)S(1)}, bf16[1088,256]{1,0:T(8,128)(2,1)S(1)}, bf16[1088,768]{1,0:T(8,128)(2,1)S(1)}, bf16[512,768]{1,0:T(8,128)(2,1)S(1)}) custom-call(s32[4]{0:T(128)S(1)} %pad_add_fusion.code, bf16[1088,256]{1,0:T(8,128)(2,1)S(1)} %collective-permute-done.halo, bf16[3,3,256,256]{3,2,1,0:T(8,128)(2,1)S(1)} %copy-done, ...), custom_call_target="tpu_custom_call" | custom-call | flops 1283457024 | bytes 12910608 | tf_op jit(solution)/shard_map/pallas_call | solution.py:45
  32.8 0.1 collective-permute-start.2
  32.9 0.5 collective-permute-start.4
  33.4 2.0 %shard_map.79 = bf16[512,768]{1,0:T(8,128)(2,1)S(1)} custom-call(s32[4]{0:T(128)S(1)} %pad_add_fusion.code, bf16[1088,256]{1,0:T(8,128)(2,1)S(1)} %collective-permute-done.halo, f32[1024,768]{1,0:T(8,128)S(1)} %get-tuple-element.35.before, bf16[17,64,768]{2,1,0:T(8,128)(2,1)S(1)} %get-tuple-element.36.cots, ...), custom_call_target="tpu_custom_call" | custom-call | flops 855638016 | bytes 9502736 | tf_op jit(solution)/shard_map/pallas_call | solution.py:45
  35.4 0.0 copy-start.2
  35.4 0.0 copy-start.4
  35.4 0.0 collective-permute-done.2
  35.4 0.2 add_convert_fusion
  35.7 1.5 %collective-permute-start.3 = (bf16[256,768]{1,0:T(8,128)(2,1)S(1)}, bf16[256,768]{1,0:T(8,128)(2,1)S(1)}, u32[]{:S(2)}, u32[]{:S(2)}) collective-permute-start(bf16[256,768]{1,0:T(8,128)(2,1)S(1)} %slice.24), channel_id=1, source_target_pairs={{0,16},{1,17},{2,18},{3,19},{4,20},{5,21},{6,22},{7,23},{8,24},{9,... | collective-permute-start | bytes 1179656 | tf_op jit(solution)/shard_map/ppermute | solution.py:318
  37.2 0.0 copy-done.2
  37.2 0.0 copy-done.4
  37.2 2.6 %shard_map.80 = bf16[17,2,64,256]{3,2,1,0:T(8,128)(2,1)} custom-call(s32[4]{0:T(128)S(1)} %pad_add_fusion.code, bf16[17,2,64,256]{3,2,1,0:T(8,128)(2,1)S(1)} %bitcast.13, bf16[1088,256]{1,0:T(8,128)(2,1)S(1)} %get-tuple-element.45.refs_0_, bf16[1088,256]{1,0:T(8,128)(2,1)S(1)} %get-tuple-element.40.act.refs_1_, bf16[3,256,256]{2,1,0:T(8,128)(2,1)S(1)} %copy-done.4), custom_call_target="tpu_custom_call" | custom-call | flops 855638016 | bytes 3735568 | tf_op jit(solution)/shard_map/pallas_call | solution.py:45
  39.8 0.0 copy-start.6
  39.8 3.6 %collective-permute-start.8 = (bf16[1088,256]{1,0:T(8,128)(2,1)S(1)}, bf16[1088,256]{1,0:T(8,128)(2,1)S(1)}, u32[]{:S(2)}, u32[]{:S(2)}) collective-permute-start(bf16[1088,256]{1,0:T(8,128)(2,1)S(1)} %get-tuple-element.49.refs_1_), channel_id=1, source_target_pairs={{0,1},{1,0},{2,3},{3,2},{4,5},{5,4},{6,7},{7,6},{8,9},{9,8},{10,11... | collective-permute-start | bytes 1671176 | tf_op jit(solution)/shard_map/ppermute | solution.py:386
  43.4 0.0 collective-permute-done.4.far
  43.4 3.4 %collective-permute-done.3 = bf16[256,768]{1,0:T(8,128)(2,1)S(1)} collective-permute-done((bf16[256,768]{1,0:T(8,128)(2,1)S(1)}, bf16[256,768]{1,0:T(8,128)(2,1)S(1)}, u32[]{:S(2)}, u32[]{:S(2)}) %collective-permute-start.3) | collective-permute-done | bytes 393248 | tf_op jit(solution)/shard_map/ppermute | solution.py:318
  46.8 0.1 add_convert_fusion.1
  46.9 5.8 %collective-permute-start.5 = (bf16[64,768]{1,0:T(8,128)(2,1)S(1)}, bf16[64,768]{1,0:T(8,128)(2,1)S(1)}, u32[]{:S(2)}, u32[]{:S(2)}) collective-permute-start(bf16[64,768]{1,0:T(8,128)(2,1)S(1)} %get-tuple-element.68), channel_id=1, source_target_pairs={{0,4},{1,5},{2,6},{3,7},{4,0},{5,1},{6,2},{7,3},{8,12},{9,13},{10,... | collective-permute-start | bytes 294920 | tf_op jit(solution)/shard_map/ppermute | solution.py:318
  52.7 1.6 %collective-permute-start.6 = (bf16[64,768]{1,0:T(8,128)(2,1)S(1)}, bf16[64,768]{1,0:T(8,128)(2,1)S(1)}, u32[]{:S(2)}, u32[]{:S(2)}) collective-permute-start(bf16[64,768]{1,0:T(8,128)(2,1)S(1)} %get-tuple-element.67), channel_id=1, source_target_pairs={{0,2},{1,3},{2,0},{3,1},{4,6},{5,7},{6,4},{7,5},{8,10},{9,11},{10,... | collective-permute-start | bytes 294920 | tf_op jit(solution)/shard_map/ppermute | solution.py:318
  54.3 0.0 collective-permute-start.7
  54.3 0.0 copy-done.6
  54.3 4.0 %shard_map.81.back_loc = f32[2,1088,256]{2,1,0:T(8,128)S(1)} custom-call(s32[4]{0:T(128)S(1)} %pad_add_fusion.code, bf16[17,2,64,256]{3,2,1,0:T(8,128)(2,1)S(1)} %bitcast.16, bf16[1088,256]{1,0:T(8,128)(2,1)S(1)} %get-tuple-element.44.refs_0_, bf16[1088,256]{1,0:T(8,128)(2,1)S(1)} %get-tuple-element.49.refs_1_, bf16[3,3,256,256]{3,2,1,0:T(8,128)(2,1)S(1)} %copy-done), custom_call_target="tpu_custom_call" | custom-call | flops 1711276032 | bytes 5636112 | tf_op jit(solution)/shard_map/pallas_call | solution.py:45
  58.3 0.0 collective-permute-done.5
  58.3 0.0 collective-permute-done.6
  58.3 2.4 %collective-permute-done.7 = bf16[64,768]{1,0:T(8,128)(2,1)S(1)} collective-permute-done((bf16[64,768]{1,0:T(8,128)(2,1)S(1)}, bf16[64,768]{1,0:T(8,128)(2,1)S(1)}, u32[]{:S(2)}, u32[]{:S(2)}) %collective-permute-start.7) | collective-permute-done | bytes 98336 | tf_op jit(solution)/shard_map/ppermute | solution.py:318
  60.8 0.0 collective-permute-done.8.near
  60.8 0.1 add_convert_fusion.3
  60.8 2.5 %collective-permute-start.9 = (bf16[64,768]{1,0:T(8,128)(2,1)S(1)}, bf16[64,768]{1,0:T(8,128)(2,1)S(1)}, u32[]{:S(2)}, u32[]{:S(2)}) collective-permute-start(bf16[64,768]{1,0:T(8,128)(2,1)S(1)} %add_convert_fusion.3), channel_id=1, source_target_pairs={{0,1},{1,0},{2,3},{3,2},{4,5},{5,4},{6,7},{7,6},{8,9},{9,8},{10,11... | collective-permute-start | bytes 294920 | tf_op jit(solution)/shard_map/ppermute | solution.py:318
  63.4 3.0 %collective-permute-done.9 = bf16[64,768]{1,0:T(8,128)(2,1)S(1)} collective-permute-done((bf16[64,768]{1,0:T(8,128)(2,1)S(1)}, bf16[64,768]{1,0:T(8,128)(2,1)S(1)}, u32[]{:S(2)}, u32[]{:S(2)}) %collective-permute-start.9) | collective-permute-done | bytes 98336 | tf_op jit(solution)/shard_map/ppermute | solution.py:318
  66.4 2.9 %collective-permute-start.10 = (bf16[64,768]{1,0:T(8,128)(2,1)S(1)}, bf16[64,768]{1,0:T(8,128)(2,1)S(1)}, u32[]{:S(2)}, u32[]{:S(2)}) collective-permute-start(bf16[64,768]{1,0:T(8,128)(2,1)S(1)} %get-tuple-element.65), channel_id=1, source_target_pairs={{0,4},{1,5},{2,6},{3,7},{4,0},{5,1},{6,2},{7,3},{8,12},{9,13},{10,... | collective-permute-start | bytes 294920 | tf_op jit(solution)/shard_map/ppermute | solution.py:318
  69.3 4.4 %collective-permute-done.10 = bf16[64,768]{1,0:T(8,128)(2,1)S(1)} collective-permute-done((bf16[64,768]{1,0:T(8,128)(2,1)S(1)}, bf16[64,768]{1,0:T(8,128)(2,1)S(1)}, u32[]{:S(2)}, u32[]{:S(2)}) %collective-permute-start.10) | collective-permute-done | bytes 98336 | tf_op jit(solution)/shard_map/ppermute | solution.py:318
  73.7 0.6 collective-permute-start.11
  74.3 1.5 %collective-permute-start.12 = (bf16[128,768]{1,0:T(8,128)(2,1)S(1)}, bf16[128,768]{1,0:T(8,128)(2,1)S(1)}, u32[]{:S(2)}, u32[]{:S(2)}) collective-permute-start(bf16[128,768]{1,0:T(8,128)(2,1)S(1)} %pad_maximum_fusion), channel_id=1, source_target_pairs={{0,16},{1,17},{2,18},{3,19},{4,20},{5,21},{6,22},{7,23},{8,24},{9,... | collective-permute-start | bytes 589832 | tf_op jit(solution)/shard_map/ppermute | solution.py:318
  75.9 1.4 %collective-permute-start.13 = (bf16[128,768]{1,0:T(8,128)(2,1)S(1)}, bf16[128,768]{1,0:T(8,128)(2,1)S(1)}, u32[]{:S(2)}, u32[]{:S(2)}) collective-permute-start(bf16[128,768]{1,0:T(8,128)(2,1)S(1)} %pad_maximum_fusion), channel_id=1, source_target_pairs={{0,18},{1,19},{2,16},{3,17},{4,22},{5,23},{6,20},{7,21},{8,26},{9,... | collective-permute-start | bytes 589832 | tf_op jit(solution)/shard_map/ppermute | solution.py:318
  77.2 3.9 %shard_map.82 = bf16[17,2,64,256]{3,2,1,0:T(8,128)(2,1)} custom-call(s32[4]{0:T(128)S(1)} %pad_add_fusion.code, f32[2,1088,256]{2,1,0:T(8,128)S(1)} %shard_map.81.back_loc, bf16[3,3,256,256]{3,2,1,0:T(8,128)(2,1)S(1)} %copy-done, bf16[1088,256]{1,0:T(8,128)(2,1)S(1)} %collective-permute-done.4.far, bf16[1088,256]{1,0:T(8,128)(2,1)S(1)} %collective-permute-done.8.near), custom_call_target="tpu_custom_call" | custom-call | flops 855638016 | bytes 5636112 | tf_op jit(solution)/shard_map/pallas_call | solution.py:45
  81.2 0.0 collective-permute-done.11
  81.2 2.0 %collective-permute-done.12 = bf16[128,768]{1,0:T(8,128)(2,1)S(1)} collective-permute-done((bf16[128,768]{1,0:T(8,128)(2,1)S(1)}, bf16[128,768]{1,0:T(8,128)(2,1)S(1)}, u32[]{:S(2)}, u32[]{:S(2)}) %collective-permute-start.12) | collective-permute-done | bytes 196640 | tf_op jit(solution)/shard_map/ppermute | solution.py:318
  83.2 1.0 %collective-permute-done.13 = bf16[128,768]{1,0:T(8,128)(2,1)S(1)} collective-permute-done((bf16[128,768]{1,0:T(8,128)(2,1)S(1)}, bf16[128,768]{1,0:T(8,128)(2,1)S(1)}, u32[]{:S(2)}, u32[]{:S(2)}) %collective-permute-start.13) | collective-permute-done | bytes 196640 | tf_op jit(solution)/shard_map/ppermute | solution.py:318
  84.2 0.1 collective-permute-start.14
  84.3 1.8 %shard_map.83 = (f32[3,3,256,256]{3,2,1,0:T(8,128)}, f32[3,256,256]{2,1,0:T(8,128)}) custom-call(s32[4]{0:T(128)S(1)} %pad_add_fusion.code, bf16[512,768]{1,0:T(8,128)(2,1)S(1)} %constant_dynamic-update-slice_fusion.sums), custom_call_target="tpu_custom_call" | custom-call | bytes 3932176 | tf_op jit(solution)/shard_map/pallas_call | solution.py:45
  86.1 0.5 collective-permute-done.14.sums
  86.6 1.8 %shard_map.84 = (f32[3,3,256,256]{3,2,1,0:T(8,128)}, f32[3,256,256]{2,1,0:T(8,128)}) custom-call(s32[4]{0:T(128)S(1)} %pad_add_fusion.code, bf16[512,768]{1,0:T(8,128)(2,1)S(1)} %collective-permute-done.14.sums, f32[3,3,256,256]{3,2,1,0:T(8,128)} %get-tuple-element.60.refs_0_, ...), custom_call_target="tpu_custom_call", output_to_operand_aliasing={{0}: (2, {}), {1}: (3, {})} | custom-call | bytes 7077904 | tf_op jit(solution)/shard_map/pallas_call | solution.py:45
  (9 shorter events, 0.2 us)
Async XLA Ops:
  1.8 14.8 %collective-permute-start.1 = (bf16[1088,256]{1,0:T(8,128)(2,1)S(1)}, bf16[1088,256]{1,0:T(8,128)(2,1)S(1)}, u32[]{:S(2)}, u32[]{:S(2)}) collective-permute-start(bf16[1088,256]{1,0:T(8,128)(2,1)S(1)} %bitcast.19), channel_id=1, source_target_pairs={{0,8},{1,2},{2,1},{3,4},{4,3},{5,6},{6,5},{7,15},{8,0},{9,10},{10,... | collective-permute-start | bytes 1671176 | tf_op jit(solution)/shard_map/ppermute | solution.py:396
  2.3 1.0 %copy-start.3 = (bf16[3,256,256]{2,1,0:T(8,128)(2,1)S(1)}, bf16[3,256,256]{2,1,0:T(8,128)(2,1)}, u32[]{:S(2)}) copy-start(bf16[3,256,256]{2,1,0:T(8,128)(2,1)} %refs_2_.2) | copy-start | bytes 1179652
  3.3 1.2 %copy-start.5 = (bf16[1,17,2,64,256]{4,3,2,1,0:T(8,128)(2,1)S(1)}, bf16[1,17,2,64,256]{4,3,2,1,0:T(8,128)(2,1)}, u32[]{:S(2)}) copy-start(bf16[1,17,2,64,256]{4,3,2,1,0:T(8,128)(2,1)} %param.5) | copy-start | bytes 3342340
  4.6 2.6 %copy-start.1 = (bf16[1,17,2,64,256]{4,3,2,1,0:T(8,128)(2,1)S(1)}, bf16[1,17,2,64,256]{4,3,2,1,0:T(8,128)(2,1)}, u32[]{:S(2)}) copy-start(bf16[1,17,2,64,256]{4,3,2,1,0:T(8,128)(2,1)} %param.4) | copy-start | bytes 3342340
  4.6 6.8 %copy-start = (bf16[3,3,256,256]{3,2,1,0:T(8,128)(2,1)S(1)}, bf16[3,3,256,256]{3,2,1,0:T(8,128)(2,1)}, u32[]{:S(2)}) copy-start(bf16[3,3,256,256]{3,2,1,0:T(8,128)(2,1)} %ws.7) | copy-start | bytes 3538948
  7.2 22.3 %collective-permute-start = (bf16[1088,256]{1,0:T(8,128)(2,1)S(1)}, bf16[1088,256]{1,0:T(8,128)(2,1)S(1)}, u32[]{:S(2)}, u32[]{:S(2)}) collective-permute-start(bf16[1088,256]{1,0:T(8,128)(2,1)S(1)} %bitcast.20), channel_id=1, source_target_pairs={{0,1},{1,0},{2,3},{3,2},{4,5},{5,4},{6,7},{7,6},{8,9},{9,8},{10,11... | collective-permute-start | bytes 1671176 | tf_op jit(solution)/shard_map/ppermute | solution.py:386
  32.8 2.6 %collective-permute-start.2 = (bf16[512,768]{1,0:T(8,128)(2,1)S(1)}, bf16[512,768]{1,0:T(8,128)(2,1)S(1)}, u32[]{:S(2)}, u32[]{:S(2)}) collective-permute-start(bf16[512,768]{1,0:T(8,128)(2,1)S(1)} %get-tuple-element.42), channel_id=1, source_target_pairs={{0,8},{1,9},{2,10},{3,11},{4,12},{5,13},{6,14},{7,15},{8,0},{9,1},... | collective-permute-start | bytes 2359304 | tf_op jit(solution)/shard_map/ppermute | solution.py:318
  32.9 10.5 %collective-permute-start.4 = (bf16[1088,256]{1,0:T(8,128)(2,1)S(1)}, bf16[1088,256]{1,0:T(8,128)(2,1)S(1)}, u32[]{:S(2)}, u32[]{:S(2)}) collective-permute-start(bf16[1088,256]{1,0:T(8,128)(2,1)S(1)} %get-tuple-element.44.refs_0_), channel_id=1, source_target_pairs={{0,8},{1,2},{2,1},{3,4},{4,3},{5,6},{6,5},{7,15},{8,0},{9,10},{10,... | collective-permute-start | bytes 1671176 | tf_op jit(solution)/shard_map/ppermute | solution.py:396
  35.4 1.8 %copy-start.2 = (bf16[1,17,2,64,256]{4,3,2,1,0:T(8,128)(2,1)S(1)}, bf16[1,17,2,64,256]{4,3,2,1,0:T(8,128)(2,1)}, u32[]{:S(2)}) copy-start(bf16[1,17,2,64,256]{4,3,2,1,0:T(8,128)(2,1)} %param.4) | copy-start | bytes 3342340
  35.4 1.8 %copy-start.4 = (bf16[3,256,256]{2,1,0:T(8,128)(2,1)S(1)}, bf16[3,256,256]{2,1,0:T(8,128)(2,1)}, u32[]{:S(2)}) copy-start(bf16[3,256,256]{2,1,0:T(8,128)(2,1)} %refs_2_.2) | copy-start | bytes 1179652
  35.7 11.2 %collective-permute-start.3 = (bf16[256,768]{1,0:T(8,128)(2,1)S(1)}, bf16[256,768]{1,0:T(8,128)(2,1)S(1)}, u32[]{:S(2)}, u32[]{:S(2)}) collective-permute-start(bf16[256,768]{1,0:T(8,128)(2,1)S(1)} %slice.24), channel_id=1, source_target_pairs={{0,16},{1,17},{2,18},{3,19},{4,20},{5,21},{6,22},{7,23},{8,24},{9,... | collective-permute-start | bytes 1179656 | tf_op jit(solution)/shard_map/ppermute | solution.py:318
  39.8 14.5 %copy-start.6 = (bf16[1,17,2,64,256]{4,3,2,1,0:T(8,128)(2,1)S(1)}, bf16[1,17,2,64,256]{4,3,2,1,0:T(8,128)(2,1)}, u32[]{:S(2)}) copy-start(bf16[1,17,2,64,256]{4,3,2,1,0:T(8,128)(2,1)} %param.5) | copy-start | bytes 3342340
  39.8 21.0 %collective-permute-start.8 = (bf16[1088,256]{1,0:T(8,128)(2,1)S(1)}, bf16[1088,256]{1,0:T(8,128)(2,1)S(1)}, u32[]{:S(2)}, u32[]{:S(2)}) collective-permute-start(bf16[1088,256]{1,0:T(8,128)(2,1)S(1)} %get-tuple-element.49.refs_1_), channel_id=1, source_target_pairs={{0,1},{1,0},{2,3},{3,2},{4,5},{5,4},{6,7},{7,6},{8,9},{9,8},{10,11... | collective-permute-start | bytes 1671176 | tf_op jit(solution)/shard_map/ppermute | solution.py:386
  46.9 11.4 %collective-permute-start.5 = (bf16[64,768]{1,0:T(8,128)(2,1)S(1)}, bf16[64,768]{1,0:T(8,128)(2,1)S(1)}, u32[]{:S(2)}, u32[]{:S(2)}) collective-permute-start(bf16[64,768]{1,0:T(8,128)(2,1)S(1)} %get-tuple-element.68), channel_id=1, source_target_pairs={{0,4},{1,5},{2,6},{3,7},{4,0},{5,1},{6,2},{7,3},{8,12},{9,13},{10,... | collective-permute-start | bytes 294920 | tf_op jit(solution)/shard_map/ppermute | solution.py:318
  52.7 5.6 %collective-permute-start.6 = (bf16[64,768]{1,0:T(8,128)(2,1)S(1)}, bf16[64,768]{1,0:T(8,128)(2,1)S(1)}, u32[]{:S(2)}, u32[]{:S(2)}) collective-permute-start(bf16[64,768]{1,0:T(8,128)(2,1)S(1)} %get-tuple-element.67), channel_id=1, source_target_pairs={{0,2},{1,3},{2,0},{3,1},{4,6},{5,7},{6,4},{7,5},{8,10},{9,11},{10,... | collective-permute-start | bytes 294920 | tf_op jit(solution)/shard_map/ppermute | solution.py:318
  54.3 6.5 %collective-permute-start.7 = (bf16[64,768]{1,0:T(8,128)(2,1)S(1)}, bf16[64,768]{1,0:T(8,128)(2,1)S(1)}, u32[]{:S(2)}, u32[]{:S(2)}) collective-permute-start(bf16[64,768]{1,0:T(8,128)(2,1)S(1)} %get-tuple-element.66), channel_id=1, source_target_pairs={{0,6},{1,7},{2,4},{3,5},{4,2},{5,3},{6,0},{7,1},{8,14},{9,15},{10,... | collective-permute-start | bytes 294920 | tf_op jit(solution)/shard_map/ppermute | solution.py:318
  60.8 5.5 %collective-permute-start.9 = (bf16[64,768]{1,0:T(8,128)(2,1)S(1)}, bf16[64,768]{1,0:T(8,128)(2,1)S(1)}, u32[]{:S(2)}, u32[]{:S(2)}) collective-permute-start(bf16[64,768]{1,0:T(8,128)(2,1)S(1)} %add_convert_fusion.3), channel_id=1, source_target_pairs={{0,1},{1,0},{2,3},{3,2},{4,5},{5,4},{6,7},{7,6},{8,9},{9,8},{10,11... | collective-permute-start | bytes 294920 | tf_op jit(solution)/shard_map/ppermute | solution.py:318
  66.4 7.3 %collective-permute-start.10 = (bf16[64,768]{1,0:T(8,128)(2,1)S(1)}, bf16[64,768]{1,0:T(8,128)(2,1)S(1)}, u32[]{:S(2)}, u32[]{:S(2)}) collective-permute-start(bf16[64,768]{1,0:T(8,128)(2,1)S(1)} %get-tuple-element.65), channel_id=1, source_target_pairs={{0,4},{1,5},{2,6},{3,7},{4,0},{5,1},{6,2},{7,3},{8,12},{9,13},{10,... | collective-permute-start | bytes 294920 | tf_op jit(solution)/shard_map/ppermute | solution.py:318
  73.7 7.5 %collective-permute-start.11 = (bf16[128,768]{1,0:T(8,128)(2,1)S(1)}, bf16[128,768]{1,0:T(8,128)(2,1)S(1)}, u32[]{:S(2)}, u32[]{:S(2)}) collective-permute-start(bf16[128,768]{1,0:T(8,128)(2,1)S(1)} %pad_maximum_fusion), channel_id=1, source_target_pairs={{0,2},{1,3},{2,0},{3,1},{4,6},{5,7},{6,4},{7,5},{8,10},{9,11},{10,... | collective-permute-start | bytes 589832 | tf_op jit(solution)/shard_map/ppermute | solution.py:318
  74.3 8.9 %collective-permute-start.12 = (bf16[128,768]{1,0:T(8,128)(2,1)S(1)}, bf16[128,768]{1,0:T(8,128)(2,1)S(1)}, u32[]{:S(2)}, u32[]{:S(2)}) collective-permute-start(bf16[128,768]{1,0:T(8,128)(2,1)S(1)} %pad_maximum_fusion), channel_id=1, source_target_pairs={{0,16},{1,17},{2,18},{3,19},{4,20},{5,21},{6,22},{7,23},{8,24},{9,... | collective-permute-start | bytes 589832 | tf_op jit(solution)/shard_map/ppermute | solution.py:318
  75.9 8.3 %collective-permute-start.13 = (bf16[128,768]{1,0:T(8,128)(2,1)S(1)}, bf16[128,768]{1,0:T(8,128)(2,1)S(1)}, u32[]{:S(2)}, u32[]{:S(2)}) collective-permute-start(bf16[128,768]{1,0:T(8,128)(2,1)S(1)} %pad_maximum_fusion), channel_id=1, source_target_pairs={{0,18},{1,19},{2,16},{3,17},{4,22},{5,23},{6,20},{7,21},{8,26},{9,... | collective-permute-start | bytes 589832 | tf_op jit(solution)/shard_map/ppermute | solution.py:318
  84.2 2.4 %collective-permute-start.14 = (bf16[512,768]{1,0:T(8,128)(2,1)S(1)}, bf16[512,768]{1,0:T(8,128)(2,1)S(1)}, u32[]{:S(2)}, u32[]{:S(2)}) collective-permute-start(bf16[512,768]{1,0:T(8,128)(2,1)S(1)} %constant_dynamic-update-slice_fusion.sums), channel_id=1, source_target_pairs={{0,8},{1,9},{2,10},{3,11},{4,12},{5,13},{6,14},{7,15},{8,0},{9,1},... | collective-permute-start | bytes 2359304 | tf_op jit(solution)/shard_map/ppermute | solution.py:318

commit v6 on v5

--- a/solution.py
+++ b/solution.py
@@ -11,6 +11,7 @@
 BF16 = jnp.bfloat16
 F32 = jnp.float32
 TILE_ROWS = 16
+FAR_CUT, NEAR_CUT = 0.8, 0.7
 PIECE_ROWS = 512
 VMEM = pl.BlockSpec(memory_space=pltpu.VMEM)
 SMEM = pl.BlockSpec(memory_space=pltpu.SMEM)
@@ -256,8 +257,13 @@
             back_loc[place, at] = cot[f, row].astype(F32) + back
 
 
-def last_kernel(code, back_loc, ws, far, near, latents_grad, taps):
+def last_kernel(code, back_loc, ws, far_one, far_two, near_one, near_two, latents_grad, taps, both):
     planes, rows, cols, chans = latents_grad.shape
+    far, near = both.at[0], both.at[1]
+    for whole, one, two in ((far, far_one, far_two), (near, near_one, near_two)):
+        cut = one.shape[0]
+        whole[:cut] = one[...]
+        whole[cut:] = two[...]
     for place in range(rows):
         row = row_at(code, place, rows)
         halos = [(1, far)] if place == 0 else []
@@ -454,7 +460,8 @@
         far=(1, 2, 4, 5),
     )
     acts, pgs = list(early[:count]), list(early[count : 2 * count])
-    there["far"] = from_far(after(pgs[0], lat_near))
+    cut, near_cut = (round(planes * part) * cols for part in (FAR_CUT, NEAR_CUT))
+    there["far"] = from_far(after(pgs[0][:cut], lat_near))
     half = pltpu.VMEM((2 * chans, 3 * chans), BF16)
     act, pg, spread, other = call(
         functools.partial(late_kernel, ends, scale),
@@ -473,7 +480,8 @@
             functools.partial(out_kernel, shift), [image], [padded], 12, 3 * rows * unit,
             [code, lat, *acts, temporal_weight],
         )
-        later.append(from_near(after(pgs[-1], gate)))
+        later.append(from_near(after(pgs[-1][:near_cut], gate)))
+        later.append(from_far(after(pgs[0][cut:], gate)))
         return {"far": there["far"], "out": block_out}
 
     def beside_second(_):
@@ -481,12 +489,15 @@
             back_kernel, [jax.ShapeDtypeStruct((rows, cells, chans), F32)], [taps], 12,
             (9 * rows - 6) * unit, [code, cot, *pgs, spatial_weight],
         )
-        return {"near": later[0], "back": back_loc}
+        return {"near": later[0], "back": back_loc, "rest": later[1]}
+
+    def beside_fourth(gate):
+        return {"last": from_near(after(pgs[-1][near_cut:], gate))}
 
     def beside_last(_):
         (latents_grad,) = call(
-            last_kernel, [image], [taps], 12, 6 * unit,
-            [code, there["back"], *map(keep, (spatial_weight, there["far"], there["near"]))],
+            last_kernel, [image], [taps, pltpu.VMEM((2, cells, chans), BF16)], 12, 6 * unit,
+            [code, there["back"], keep(spatial_weight), *(keep(there[name]) for name in ("far", "rest", "near", "last"))],
         )
         return {"grad": latents_grad}
 
@@ -500,7 +511,7 @@
         )
 
     later = []
-    beside = [beside_first, beside_second, lambda _: {}, lambda _: {}, beside_last]
+    beside = [beside_first, beside_second, lambda _: {}, beside_fourth, beside_last]
     mine, other = add_up(mine, other, groups, beside, there)
     block_out, latents_grad = there["out"], there["grad"]
     spatial_grad, temporal_grad = ordered(other, *ordered(mine))

time: 88.7 us -> 85.9 us (0.968)
  waiting for transfers between devices: 24.2 us -> 21 us
    ppermute x11, waiting for transfers between devices: 16.7 us -> 13.6 us  [send(): lax.ppermute(x, ('dp', 'tm'), [(i, i ^ mask) for i in range(wide * tall)])]
    ppermute x2 -> x3, starting transfers between devices: 7.68 us -> 10.3 us  [from_near(): lax.ppermute(x, 'tm', [(i, i ^ 1) for i in range(count) if i ^ 1 < count])]
    ppermute x11, starting transfers between devices: 18 us -> 15.5 us  [send(): lax.ppermute(x, ('dp', 'tm'), [(i, i ^ mask) for i in range(wide * tall)])]
    ppermute x2 -> x3, waiting for transfers between devices: 7.48 us -> 7.46 us  [from_near(): lax.ppermute(x, 'tm', [(i, i ^ 1) for i in range(count) if i ^ 1 < count])]
  transfers between devices with their start and end apart: 15 -> 17, of which waited for: 8 -> 8; matrix products, arithmetic and copies ran while one was open for 1% -> 1% of each run, Pallas kernels for 31% -> 32%
where the time goes in v6:
time: 85.9 us; the launch traced here: 85.7 us
  Pallas kernels  32.7 us (38%)
  starting transfers between devices  26.9 us (31%)
  waiting for transfers between devices  21 us (24%)
  local copies, waits for them, and re-layouts  3.58 us (4%)
  between operations  1.03 us (1%)
    pallas_call x10, Pallas kernels, call(): pl.pallas_call(kernel, out_shape=outs, in_specs=specs, out_specs=[ANY if...  32.7 us
    ppermute x11, starting transfers between devices, send(): lax.ppermute(x, ('dp', 'tm'), [(i, i ^ mask) for i in range(wide * tall)])  15.5 us
    ppermute x11, waiting for transfers between devices, send(): lax.ppermute(x, ('dp', 'tm'), [(i, i ^ mask) for i in range(wide * tall)])  13.6 us
    ppermute x3, starting transfers between devices, from_near(): lax.ppermute(x, 'tm', [(i, i ^ 1) for i in range(count) if i ^ 1 < count])  10.3 us
    ppermute x3, waiting for transfers between devices, from_near(): lax.ppermute(x, 'tm', [(i, i ^ 1) for i in range(count) if i ^ 1 < count])  7.46 us
    unnamed x17, local copies, waits for them, and re-layouts  2.3 us
  transfers between devices with their start and end apart: 17, of which 8 were waited for; matrix products, arithmetic and copies ran while one was open for 1% of the time, Pallas kernels for 32%

profile of v6, /device:TPU:0, one launch (start us, length us, event | category | flops | bytes accessed | tf_op | source)
XLA Modules:
  0.0 85.7 jit_solution(16848952561249821645)
XLA Ops:
  0.6 1.1 %constant_dynamic-slice_fusion = bf16[1,17,1,64,256]{4,3,2,1,0:T(8,128)(2,1)S(1)} fusion(bf16[1,17,2,64,256]{4,3,2,1,0:T(8,128)(2,1)} %param.4, s32[]{:T(128)S(6)} %select_n.60), kind=kLoop, calls=%fused_computation.11 | loop fusion | bytes 1114116 | tf_op jit(solution)/shard_map/jit(dynamic_index_in_dim)/dynamic_slice | solution.py:422
  1.8 0.5 collective-permute-start.1
  2.3 0.1 pad_add_fusion.code
  2.3 0.0 copy-start.3
  2.3 1.0 %copy-done.3 = bf16[3,256,256]{2,1,0:T(8,128)(2,1)S(1)} copy-done((bf16[3,256,256]{2,1,0:T(8,128)(2,1)S(1)}, bf16[3,256,256]{2,1,0:T(8,128)(2,1)}, u32[]{:S(2)}) %copy-start.3) | copy-done | bytes 393240
  3.3 0.0 copy-start.5
  3.3 1.2 %copy-done.5 = bf16[1,17,2,64,256]{4,3,2,1,0:T(8,128)(2,1)S(1)} copy-done((bf16[1,17,2,64,256]{4,3,2,1,0:T(8,128)(2,1)S(1)}, bf16[1,17,2,64,256]{4,3,2,1,0:T(8,128)(2,1)}, u32[]{:S(2)}) %copy-start.5) | copy-done | bytes 1114136
  4.6 0.0 copy-start.1
  4.6 0.0 copy-start
  4.6 2.6 %shard_map.75.act_grad = bf16[2,1088,256]{2,1,0:T(8,128)(2,1)} custom-call(s32[4]{0:T(128)S(1)} %pad_add_fusion.code, bf16[17,2,64,256]{3,2,1,0:T(8,128)(2,1)S(1)} %bitcast.15, bf16[3,256,256]{2,1,0:T(8,128)(2,1)S(1)} %copy-done.3), custom_call_target="tpu_custom_call" | custom-call | flops 855638016 | bytes 2621456 | tf_op jit(solution)/shard_map/pallas_call | solution.py:46
  7.2 0.0 copy-done.1
  7.2 4.1 %collective-permute-start = (bf16[1088,256]{1,0:T(8,128)(2,1)S(1)}, bf16[1088,256]{1,0:T(8,128)(2,1)S(1)}, u32[]{:S(2)}, u32[]{:S(2)}) collective-permute-start(bf16[1088,256]{1,0:T(8,128)(2,1)S(1)} %bitcast.20), channel_id=1, source_target_pairs={{0,1},{1,0},{2,3},{3,2},{4,5},{5,4},{6,7},{7,6},{8,9},{9,8},{10,11... | collective-permute-start | bytes 1671176 | tf_op jit(solution)/shard_map/ppermute | solution.py:392
  11.3 0.0 copy-done
  11.3 5.2 %shard_map.76.pre_loc = f32[2,1088,256]{2,1,0:T(8,128)} custom-call(s32[4]{0:T(128)S(1)} %pad_add_fusion.code, bf16[17,2,64,256]{3,2,1,0:T(8,128)(2,1)S(1)} %bitcast.12, bf16[3,3,256,256]{3,2,1,0:T(8,128)(2,1)S(1)} %copy-done), custom_call_target="tpu_custom_call" | custom-call | flops 1711276032 | bytes 4522000 | tf_op jit(solution)/shard_map/pallas_call | solution.py:46
  16.5 0.0 collective-permute-done.1.halo
  16.5 5.5 %shard_map.77 = (bf16[1088,256]{1,0:T(8,128)(2,1)S(1)}, bf16[1088,256]{1,0:T(8,128)(2,1)S(1)}, f32[1024,768]{1,0:T(8,128)S(1)}, f32[1088,256]{1,0:T(8,128)S(1)},...) custom-call(s32[4]{0:T(128)S(1)} %pad_add_fusion.code, ...), custom_call_target="tpu_custom_call" | custom-call | flops 2139095040 | bytes 16023568 | tf_op jit(solution)/shard_map/pallas_call | solution.py:46
  22.1 7.5 %collective-permute-done.halo = bf16[1088,256]{1,0:T(8,128)(2,1)S(1)} collective-permute-done((bf16[1088,256]{1,0:T(8,128)(2,1)S(1)}, bf16[1088,256]{1,0:T(8,128)(2,1)S(1)}, u32[]{:S(2)}, u32[]{:S(2)}) %collective-permute-start) | collective-permute-done | bytes 557088 | tf_op jit(solution)/shard_map/ppermute | solution.py:392
  29.5 3.3 %shard_map.78 = (bf16[1088,256]{1,0:T(8,128)(2,1)S(1)}, bf16[1088,256]{1,0:T(8,128)(2,1)S(1)}, bf16[1088,768]{1,0:T(8,128)(2,1)S(1)}, bf16[512,768]{1,0:T(8,128)(2,1)S(1)}) custom-call(s32[4]{0:T(128)S(1)} %pad_add_fusion.code, bf16[1088,256]{1,0:T(8,128)(2,1)S(1)} %collective-permute-done.halo, bf16[3,3,256,256]{3,2,1,0:T(8,128)(2,1)S(1)} %copy-done, ...), custom_call_target="tpu_custom_call" | custom-call | flops 1283457024 | bytes 12910608 | tf_op jit(solution)/shard_map/pallas_call | solution.py:46
  32.8 0.1 collective-permute-start.2
  33.0 0.5 collective-permute-start.4
  33.5 2.0 %shard_map.79 = bf16[512,768]{1,0:T(8,128)(2,1)S(1)} custom-call(s32[4]{0:T(128)S(1)} %pad_add_fusion.code, bf16[1088,256]{1,0:T(8,128)(2,1)S(1)} %collective-permute-done.halo, f32[1024,768]{1,0:T(8,128)S(1)} %get-tuple-element.40.before, bf16[17,64,768]{2,1,0:T(8,128)(2,1)S(1)} %get-tuple-element.41.cots, ...), custom_call_target="tpu_custom_call" | custom-call | flops 855638016 | bytes 9502736 | tf_op jit(solution)/shard_map/pallas_call | solution.py:46
  35.5 0.0 copy-start.2
  35.5 0.0 copy-start.4
  35.5 0.0 collective-permute-done.2
  35.5 0.2 add_convert_fusion
  35.8 1.6 %collective-permute-start.3 = (bf16[256,768]{1,0:T(8,128)(2,1)S(1)}, bf16[256,768]{1,0:T(8,128)(2,1)S(1)}, u32[]{:S(2)}, u32[]{:S(2)}) collective-permute-start(bf16[256,768]{1,0:T(8,128)(2,1)S(1)} %slice.40), channel_id=1, source_target_pairs={{0,16},{1,17},{2,18},{3,19},{4,20},{5,21},{6,22},{7,23},{8,24},{9,... | collective-permute-start | bytes 1179656 | tf_op jit(solution)/shard_map/ppermute | solution.py:324
  37.4 0.0 copy-done.2
  37.4 0.0 copy-done.4
  37.4 2.6 %shard_map.80 = bf16[17,2,64,256]{3,2,1,0:T(8,128)(2,1)} custom-call(s32[4]{0:T(128)S(1)} %pad_add_fusion.code, bf16[17,2,64,256]{3,2,1,0:T(8,128)(2,1)S(1)} %bitcast.13, bf16[1088,256]{1,0:T(8,128)(2,1)S(1)} %get-tuple-element.50.refs_0_, bf16[1088,256]{1,0:T(8,128)(2,1)S(1)} %get-tuple-element.45.act.refs_1_, bf16[3,256,256]{2,1,0:T(8,128)(2,1)S(1)} %copy-done.4), custom_call_target="tpu_custom_call" | custom-call | flops 855638016 | bytes 3735568 | tf_op jit(solution)/shard_map/pallas_call | solution.py:46
  40.0 0.0 copy-start.6
  40.0 0.0 collective-permute-start.9
  40.0 4.9 %collective-permute-start.8 = (bf16[768,256]{1,0:T(8,128)(2,1)S(1)}, bf16[768,256]{1,0:T(8,128)(2,1)S(1)}, u32[]{:S(2)}, u32[]{:S(2)}) collective-permute-start(bf16[768,256]{1,0:T(8,128)(2,1)S(1)} %slice.37), channel_id=1, source_target_pairs={{0,1},{1,0},{2,3},{3,2},{4,5},{5,4},{6,7},{7,6},{8,9},{9,8},{10,11... | collective-permute-start | bytes 1179656 | tf_op jit(solution)/shard_map/ppermute | solution.py:392
  44.9 0.0 collective-permute-done.4.far_one
  44.9 2.0 %collective-permute-done.3 = bf16[256,768]{1,0:T(8,128)(2,1)S(1)} collective-permute-done((bf16[256,768]{1,0:T(8,128)(2,1)S(1)}, bf16[256,768]{1,0:T(8,128)(2,1)S(1)}, u32[]{:S(2)}, u32[]{:S(2)}) %collective-permute-start.3) | collective-permute-done | bytes 393248 | tf_op jit(solution)/shard_map/ppermute | solution.py:324
  46.9 0.1 add_convert_fusion.1
  47.0 4.7 %collective-permute-start.5 = (bf16[64,768]{1,0:T(8,128)(2,1)S(1)}, bf16[64,768]{1,0:T(8,128)(2,1)S(1)}, u32[]{:S(2)}, u32[]{:S(2)}) collective-permute-start(bf16[64,768]{1,0:T(8,128)(2,1)S(1)} %get-tuple-element.78), channel_id=1, source_target_pairs={{0,4},{1,5},{2,6},{3,7},{4,0},{5,1},{6,2},{7,3},{8,12},{9,13},{10,... | collective-permute-start | bytes 294920 | tf_op jit(solution)/shard_map/ppermute | solution.py:324
  51.8 1.6 %collective-permute-start.6 = (bf16[64,768]{1,0:T(8,128)(2,1)S(1)}, bf16[64,768]{1,0:T(8,128)(2,1)S(1)}, u32[]{:S(2)}, u32[]{:S(2)}) collective-permute-start(bf16[64,768]{1,0:T(8,128)(2,1)S(1)} %get-tuple-element.77), channel_id=1, source_target_pairs={{0,2},{1,3},{2,0},{3,1},{4,6},{5,7},{6,4},{7,5},{8,10},{9,11},{10,... | collective-permute-start | bytes 294920 | tf_op jit(solution)/shard_map/ppermute | solution.py:324
  53.3 0.0 collective-permute-start.7
  53.3 0.0 copy-done.6
  53.3 4.0 %shard_map.81.back_loc = f32[2,1088,256]{2,1,0:T(8,128)S(1)} custom-call(s32[4]{0:T(128)S(1)} %pad_add_fusion.code, bf16[17,2,64,256]{3,2,1,0:T(8,128)(2,1)S(1)} %bitcast.16, bf16[1088,256]{1,0:T(8,128)(2,1)S(1)} %get-tuple-element.48.refs_0_, bf16[1088,256]{1,0:T(8,128)(2,1)S(1)} %get-tuple-element.53.refs_1_, bf16[3,3,256,256]{3,2,1,0:T(8,128)(2,1)S(1)} %copy-done), custom_call_target="tpu_custom_call" | custom-call | flops 1711276032 | bytes 5636112 | tf_op jit(solution)/shard_map/pallas_call | solution.py:46
  57.4 0.0 collective-permute-done.9.far_two
  57.4 0.0 collective-permute-done.8.near_one
  57.4 0.0 collective-permute-done.5
  57.4 0.0 collective-permute-done.6
  57.4 2.4 %collective-permute-done.7 = bf16[64,768]{1,0:T(8,128)(2,1)S(1)} collective-permute-done((bf16[64,768]{1,0:T(8,128)(2,1)S(1)}, bf16[64,768]{1,0:T(8,128)(2,1)S(1)}, u32[]{:S(2)}, u32[]{:S(2)}) %collective-permute-start.7) | collective-permute-done | bytes 98336 | tf_op jit(solution)/shard_map/ppermute | solution.py:324
  59.8 0.1 add_convert_fusion.3
  59.9 1.4 %collective-permute-start.10 = (bf16[64,768]{1,0:T(8,128)(2,1)S(1)}, bf16[64,768]{1,0:T(8,128)(2,1)S(1)}, u32[]{:S(2)}, u32[]{:S(2)}) collective-permute-start(bf16[64,768]{1,0:T(8,128)(2,1)S(1)} %add_convert_fusion.3), channel_id=1, source_target_pairs={{0,1},{1,0},{2,3},{3,2},{4,5},{5,4},{6,7},{7,6},{8,9},{9,8},{10,11... | collective-permute-start | bytes 294920 | tf_op jit(solution)/shard_map/ppermute | solution.py:324
  61.3 3.3 %collective-permute-done.10 = bf16[64,768]{1,0:T(8,128)(2,1)S(1)} collective-permute-done((bf16[64,768]{1,0:T(8,128)(2,1)S(1)}, bf16[64,768]{1,0:T(8,128)(2,1)S(1)}, u32[]{:S(2)}, u32[]{:S(2)}) %collective-permute-start.10) | collective-permute-done | bytes 98336 | tf_op jit(solution)/shard_map/ppermute | solution.py:324
  64.6 1.3 %collective-permute-start.12 = (bf16[320,256]{1,0:T(8,128)(2,1)S(1)}, bf16[320,256]{1,0:T(8,128)(2,1)S(1)}, u32[]{:S(2)}, u32[]{:S(2)}) collective-permute-start(bf16[320,256]{1,0:T(8,128)(2,1)S(1)} %slice.39), channel_id=1, source_target_pairs={{0,1},{1,0},{2,3},{3,2},{4,5},{5,4},{6,7},{7,6},{8,9},{9,8},{10,11... | collective-permute-start | bytes 491528 | tf_op jit(solution)/shard_map/ppermute | solution.py:392
  66.0 2.0 %collective-permute-start.11 = (bf16[64,768]{1,0:T(8,128)(2,1)S(1)}, bf16[64,768]{1,0:T(8,128)(2,1)S(1)}, u32[]{:S(2)}, u32[]{:S(2)}) collective-permute-start(bf16[64,768]{1,0:T(8,128)(2,1)S(1)} %get-tuple-element.75), channel_id=1, source_target_pairs={{0,4},{1,5},{2,6},{3,7},{4,0},{5,1},{6,2},{7,3},{8,12},{9,13},{10,... | collective-permute-start | bytes 294920 | tf_op jit(solution)/shard_map/ppermute | solution.py:324
  68.0 3.6 %collective-permute-done.11 = bf16[64,768]{1,0:T(8,128)(2,1)S(1)} collective-permute-done((bf16[64,768]{1,0:T(8,128)(2,1)S(1)}, bf16[64,768]{1,0:T(8,128)(2,1)S(1)}, u32[]{:S(2)}, u32[]{:S(2)}) %collective-permute-start.11) | collective-permute-done | bytes 98336 | tf_op jit(solution)/shard_map/ppermute | solution.py:324
  71.5 0.0 collective-permute-done.12.near_two
  71.6 1.6 %collective-permute-start.13 = (bf16[128,768]{1,0:T(8,128)(2,1)S(1)}, bf16[128,768]{1,0:T(8,128)(2,1)S(1)}, u32[]{:S(2)}, u32[]{:S(2)}) collective-permute-start(bf16[128,768]{1,0:T(8,128)(2,1)S(1)} %pad_maximum_fusion), channel_id=1, source_target_pairs={{0,2},{1,3},{2,0},{3,1},{4,6},{5,7},{6,4},{7,5},{8,10},{9,11},{10,... | collective-permute-start | bytes 589832 | tf_op jit(solution)/shard_map/ppermute | solution.py:324
  73.2 1.5 %collective-permute-start.14 = (bf16[128,768]{1,0:T(8,128)(2,1)S(1)}, bf16[128,768]{1,0:T(8,128)(2,1)S(1)}, u32[]{:S(2)}, u32[]{:S(2)}) collective-permute-start(bf16[128,768]{1,0:T(8,128)(2,1)S(1)} %pad_maximum_fusion), channel_id=1, source_target_pairs={{0,16},{1,17},{2,18},{3,19},{4,20},{5,21},{6,22},{7,23},{8,24},{9,... | collective-permute-start | bytes 589832 | tf_op jit(solution)/shard_map/ppermute | solution.py:324
  74.7 0.9 %collective-permute-start.15 = (bf16[128,768]{1,0:T(8,128)(2,1)S(1)}, bf16[128,768]{1,0:T(8,128)(2,1)S(1)}, u32[]{:S(2)}, u32[]{:S(2)}) collective-permute-start(bf16[128,768]{1,0:T(8,128)(2,1)S(1)} %pad_maximum_fusion), channel_id=1, source_target_pairs={{0,18},{1,19},{2,16},{3,17},{4,22},{5,23},{6,20},{7,21},{8,26},{9,... | collective-permute-start | bytes 589832 | tf_op jit(solution)/shard_map/ppermute | solution.py:324
  75.6 4.0 %shard_map.82 = bf16[17,2,64,256]{3,2,1,0:T(8,128)(2,1)} custom-call(s32[4]{0:T(128)S(1)} %pad_add_fusion.code, f32[2,1088,256]{2,1,0:T(8,128)S(1)} %shard_map.81.back_loc, bf16[3,3,256,256]{3,2,1,0:T(8,128)(2,1)S(1)} %copy-done, bf16[896,256]{1,0:T(8,128)(2,1)S(1)} %collective-permute-done.4.far_one, bf16[192,256]{1,0:T(8,128)(2,1)S(1)} %collective-permute-done.9.far_two, ...), custom_call_target="tpu_custom_call" | custom-call | flops 855638016 | bytes 5636112 | tf_op jit(solution)/shard_map/pallas_call | solution.py:46
  79.6 0.0 collective-permute-done.13
  79.6 0.4 collective-permute-done.14
  80.0 1.3 %collective-permute-done.15 = bf16[128,768]{1,0:T(8,128)(2,1)S(1)} collective-permute-done((bf16[128,768]{1,0:T(8,128)(2,1)S(1)}, bf16[128,768]{1,0:T(8,128)(2,1)S(1)}, u32[]{:S(2)}, u32[]{:S(2)}) %collective-permute-start.15) | collective-permute-done | bytes 196640 | tf_op jit(solution)/shard_map/ppermute | solution.py:324
  81.4 0.1 collective-permute-start.16
  81.5 1.8 %shard_map.83 = (f32[3,3,256,256]{3,2,1,0:T(8,128)}, f32[3,256,256]{2,1,0:T(8,128)}) custom-call(s32[4]{0:T(128)S(1)} %pad_add_fusion.code, bf16[512,768]{1,0:T(8,128)(2,1)S(1)} %constant_dynamic-update-slice_fusion.sums), custom_call_target="tpu_custom_call" | custom-call | bytes 3932176 | tf_op jit(solution)/shard_map/pallas_call | solution.py:46
  83.3 0.5 collective-permute-done.16.sums
  83.8 1.8 %shard_map.84 = (f32[3,3,256,256]{3,2,1,0:T(8,128)}, f32[3,256,256]{2,1,0:T(8,128)}) custom-call(s32[4]{0:T(128)S(1)} %pad_add_fusion.code, bf16[512,768]{1,0:T(8,128)(2,1)S(1)} %collective-permute-done.16.sums, f32[3,3,256,256]{3,2,1,0:T(8,128)} %get-tuple-element.70.refs_0_, ...), custom_call_target="tpu_custom_call", output_to_operand_aliasing={{0}: (2, {}), {1}: (3, {})} | custom-call | bytes 7077904 | tf_op jit(solution)/shard_map/pallas_call | solution.py:46
  (13 shorter events, 0.3 us)
Async XLA Ops:
  1.8 14.8 %collective-permute-start.1 = (bf16[1088,256]{1,0:T(8,128)(2,1)S(1)}, bf16[1088,256]{1,0:T(8,128)(2,1)S(1)}, u32[]{:S(2)}, u32[]{:S(2)}) collective-permute-start(bf16[1088,256]{1,0:T(8,128)(2,1)S(1)} %bitcast.19), channel_id=1, source_target_pairs={{0,8},{1,2},{2,1},{3,4},{4,3},{5,6},{6,5},{7,15},{8,0},{9,10},{10,... | collective-permute-start | bytes 1671176 | tf_op jit(solution)/shard_map/ppermute | solution.py:402
  2.3 1.0 %copy-start.3 = (bf16[3,256,256]{2,1,0:T(8,128)(2,1)S(1)}, bf16[3,256,256]{2,1,0:T(8,128)(2,1)}, u32[]{:S(2)}) copy-start(bf16[3,256,256]{2,1,0:T(8,128)(2,1)} %refs_2_.2) | copy-start | bytes 1179652
  3.3 1.2 %copy-start.5 = (bf16[1,17,2,64,256]{4,3,2,1,0:T(8,128)(2,1)S(1)}, bf16[1,17,2,64,256]{4,3,2,1,0:T(8,128)(2,1)}, u32[]{:S(2)}) copy-start(bf16[1,17,2,64,256]{4,3,2,1,0:T(8,128)(2,1)} %param.5) | copy-start | bytes 3342340
  4.6 2.6 %copy-start.1 = (bf16[1,17,2,64,256]{4,3,2,1,0:T(8,128)(2,1)S(1)}, bf16[1,17,2,64,256]{4,3,2,1,0:T(8,128)(2,1)}, u32[]{:S(2)}) copy-start(bf16[1,17,2,64,256]{4,3,2,1,0:T(8,128)(2,1)} %param.4) | copy-start | bytes 3342340
  4.6 6.8 %copy-start = (bf16[3,3,256,256]{3,2,1,0:T(8,128)(2,1)S(1)}, bf16[3,3,256,256]{3,2,1,0:T(8,128)(2,1)}, u32[]{:S(2)}) copy-start(bf16[3,3,256,256]{3,2,1,0:T(8,128)(2,1)} %ws.7) | copy-start | bytes 3538948
  7.2 22.3 %collective-permute-start = (bf16[1088,256]{1,0:T(8,128)(2,1)S(1)}, bf16[1088,256]{1,0:T(8,128)(2,1)S(1)}, u32[]{:S(2)}, u32[]{:S(2)}) collective-permute-start(bf16[1088,256]{1,0:T(8,128)(2,1)S(1)} %bitcast.20), channel_id=1, source_target_pairs={{0,1},{1,0},{2,3},{3,2},{4,5},{5,4},{6,7},{7,6},{8,9},{9,8},{10,11... | collective-permute-start | bytes 1671176 | tf_op jit(solution)/shard_map/ppermute | solution.py:392
  32.8 2.7 %collective-permute-start.2 = (bf16[512,768]{1,0:T(8,128)(2,1)S(1)}, bf16[512,768]{1,0:T(8,128)(2,1)S(1)}, u32[]{:S(2)}, u32[]{:S(2)}) collective-permute-start(bf16[512,768]{1,0:T(8,128)(2,1)S(1)} %get-tuple-element.47), channel_id=1, source_target_pairs={{0,8},{1,9},{2,10},{3,11},{4,12},{5,13},{6,14},{7,15},{8,0},{9,1},... | collective-permute-start | bytes 2359304 | tf_op jit(solution)/shard_map/ppermute | solution.py:324
  33.0 12.0 %collective-permute-start.4 = (bf16[896,256]{1,0:T(8,128)(2,1)S(1)}, bf16[896,256]{1,0:T(8,128)(2,1)S(1)}, u32[]{:S(2)}, u32[]{:S(2)}) collective-permute-start(bf16[896,256]{1,0:T(8,128)(2,1)S(1)} %slice.31), channel_id=1, source_target_pairs={{0,8},{1,2},{2,1},{3,4},{4,3},{5,6},{6,5},{7,15},{8,0},{9,10},{10,... | collective-permute-start | bytes 1376264 | tf_op jit(solution)/shard_map/ppermute | solution.py:402
  35.5 1.9 %copy-start.2 = (bf16[1,17,2,64,256]{4,3,2,1,0:T(8,128)(2,1)S(1)}, bf16[1,17,2,64,256]{4,3,2,1,0:T(8,128)(2,1)}, u32[]{:S(2)}) copy-start(bf16[1,17,2,64,256]{4,3,2,1,0:T(8,128)(2,1)} %param.4) | copy-start | bytes 3342340
  35.5 1.9 %copy-start.4 = (bf16[3,256,256]{2,1,0:T(8,128)(2,1)S(1)}, bf16[3,256,256]{2,1,0:T(8,128)(2,1)}, u32[]{:S(2)}) copy-start(bf16[3,256,256]{2,1,0:T(8,128)(2,1)} %refs_2_.2) | copy-start | bytes 1179652
  35.8 11.1 %collective-permute-start.3 = (bf16[256,768]{1,0:T(8,128)(2,1)S(1)}, bf16[256,768]{1,0:T(8,128)(2,1)S(1)}, u32[]{:S(2)}, u32[]{:S(2)}) collective-permute-start(bf16[256,768]{1,0:T(8,128)(2,1)S(1)} %slice.40), channel_id=1, source_target_pairs={{0,16},{1,17},{2,18},{3,19},{4,20},{5,21},{6,22},{7,23},{8,24},{9,... | collective-permute-start | bytes 1179656 | tf_op jit(solution)/shard_map/ppermute | solution.py:324
  40.0 13.3 %copy-start.6 = (bf16[1,17,2,64,256]{4,3,2,1,0:T(8,128)(2,1)S(1)}, bf16[1,17,2,64,256]{4,3,2,1,0:T(8,128)(2,1)}, u32[]{:S(2)}) copy-start(bf16[1,17,2,64,256]{4,3,2,1,0:T(8,128)(2,1)} %param.5) | copy-start | bytes 3342340
  40.0 17.4 %collective-permute-start.9 = (bf16[192,256]{1,0:T(8,128)(2,1)S(1)}, bf16[192,256]{1,0:T(8,128)(2,1)S(1)}, u32[]{:S(2)}, u32[]{:S(2)}) collective-permute-start(bf16[192,256]{1,0:T(8,128)(2,1)S(1)} %slice.38), channel_id=1, source_target_pairs={{0,8},{1,2},{2,1},{3,4},{4,3},{5,6},{6,5},{7,15},{8,0},{9,10},{10,... | collective-permute-start | bytes 294920 | tf_op jit(solution)/shard_map/ppermute | solution.py:402
  40.0 17.4 %collective-permute-start.8 = (bf16[768,256]{1,0:T(8,128)(2,1)S(1)}, bf16[768,256]{1,0:T(8,128)(2,1)S(1)}, u32[]{:S(2)}, u32[]{:S(2)}) collective-permute-start(bf16[768,256]{1,0:T(8,128)(2,1)S(1)} %slice.37), channel_id=1, source_target_pairs={{0,1},{1,0},{2,3},{3,2},{4,5},{5,4},{6,7},{7,6},{8,9},{9,8},{10,11... | collective-permute-start | bytes 1179656 | tf_op jit(solution)/shard_map/ppermute | solution.py:392
  47.0 10.4 %collective-permute-start.5 = (bf16[64,768]{1,0:T(8,128)(2,1)S(1)}, bf16[64,768]{1,0:T(8,128)(2,1)S(1)}, u32[]{:S(2)}, u32[]{:S(2)}) collective-permute-start(bf16[64,768]{1,0:T(8,128)(2,1)S(1)} %get-tuple-element.78), channel_id=1, source_target_pairs={{0,4},{1,5},{2,6},{3,7},{4,0},{5,1},{6,2},{7,3},{8,12},{9,13},{10,... | collective-permute-start | bytes 294920 | tf_op jit(solution)/shard_map/ppermute | solution.py:324
  51.8 5.6 %collective-permute-start.6 = (bf16[64,768]{1,0:T(8,128)(2,1)S(1)}, bf16[64,768]{1,0:T(8,128)(2,1)S(1)}, u32[]{:S(2)}, u32[]{:S(2)}) collective-permute-start(bf16[64,768]{1,0:T(8,128)(2,1)S(1)} %get-tuple-element.77), channel_id=1, source_target_pairs={{0,2},{1,3},{2,0},{3,1},{4,6},{5,7},{6,4},{7,5},{8,10},{9,11},{10,... | collective-permute-start | bytes 294920 | tf_op jit(solution)/shard_map/ppermute | solution.py:324
  53.3 6.5 %collective-permute-start.7 = (bf16[64,768]{1,0:T(8,128)(2,1)S(1)}, bf16[64,768]{1,0:T(8,128)(2,1)S(1)}, u32[]{:S(2)}, u32[]{:S(2)}) collective-permute-start(bf16[64,768]{1,0:T(8,128)(2,1)S(1)} %get-tuple-element.76), channel_id=1, source_target_pairs={{0,6},{1,7},{2,4},{3,5},{4,2},{5,3},{6,0},{7,1},{8,14},{9,15},{10,... | collective-permute-start | bytes 294920 | tf_op jit(solution)/shard_map/ppermute | solution.py:324
  59.9 4.8 %collective-permute-start.10 = (bf16[64,768]{1,0:T(8,128)(2,1)S(1)}, bf16[64,768]{1,0:T(8,128)(2,1)S(1)}, u32[]{:S(2)}, u32[]{:S(2)}) collective-permute-start(bf16[64,768]{1,0:T(8,128)(2,1)S(1)} %add_convert_fusion.3), channel_id=1, source_target_pairs={{0,1},{1,0},{2,3},{3,2},{4,5},{5,4},{6,7},{7,6},{8,9},{9,8},{10,11... | collective-permute-start | bytes 294920 | tf_op jit(solution)/shard_map/ppermute | solution.py:324
  64.6 6.9 %collective-permute-start.12 = (bf16[320,256]{1,0:T(8,128)(2,1)S(1)}, bf16[320,256]{1,0:T(8,128)(2,1)S(1)}, u32[]{:S(2)}, u32[]{:S(2)}) collective-permute-start(bf16[320,256]{1,0:T(8,128)(2,1)S(1)} %slice.39), channel_id=1, source_target_pairs={{0,1},{1,0},{2,3},{3,2},{4,5},{5,4},{6,7},{7,6},{8,9},{9,8},{10,11... | collective-permute-start | bytes 491528 | tf_op jit(solution)/shard_map/ppermute | solution.py:392
  66.0 5.6 %collective-permute-start.11 = (bf16[64,768]{1,0:T(8,128)(2,1)S(1)}, bf16[64,768]{1,0:T(8,128)(2,1)S(1)}, u32[]{:S(2)}, u32[]{:S(2)}) collective-permute-start(bf16[64,768]{1,0:T(8,128)(2,1)S(1)} %get-tuple-element.75), channel_id=1, source_target_pairs={{0,4},{1,5},{2,6},{3,7},{4,0},{5,1},{6,2},{7,3},{8,12},{9,13},{10,... | collective-permute-start | bytes 294920 | tf_op jit(solution)/shard_map/ppermute | solution.py:324
  71.6 8.0 %collective-permute-start.13 = (bf16[128,768]{1,0:T(8,128)(2,1)S(1)}, bf16[128,768]{1,0:T(8,128)(2,1)S(1)}, u32[]{:S(2)}, u32[]{:S(2)}) collective-permute-start(bf16[128,768]{1,0:T(8,128)(2,1)S(1)} %pad_maximum_fusion), channel_id=1, source_target_pairs={{0,2},{1,3},{2,0},{3,1},{4,6},{5,7},{6,4},{7,5},{8,10},{9,11},{10,... | collective-permute-start | bytes 589832 | tf_op jit(solution)/shard_map/ppermute | solution.py:324
  73.2 6.8 %collective-permute-start.14 = (bf16[128,768]{1,0:T(8,128)(2,1)S(1)}, bf16[128,768]{1,0:T(8,128)(2,1)S(1)}, u32[]{:S(2)}, u32[]{:S(2)}) collective-permute-start(bf16[128,768]{1,0:T(8,128)(2,1)S(1)} %pad_maximum_fusion), channel_id=1, source_target_pairs={{0,16},{1,17},{2,18},{3,19},{4,20},{5,21},{6,22},{7,23},{8,24},{9,... | collective-permute-start | bytes 589832 | tf_op jit(solution)/shard_map/ppermute | solution.py:324
  74.7 6.7 %collective-permute-start.15 = (bf16[128,768]{1,0:T(8,128)(2,1)S(1)}, bf16[128,768]{1,0:T(8,128)(2,1)S(1)}, u32[]{:S(2)}, u32[]{:S(2)}) collective-permute-start(bf16[128,768]{1,0:T(8,128)(2,1)S(1)} %pad_maximum_fusion), channel_id=1, source_target_pairs={{0,18},{1,19},{2,16},{3,17},{4,22},{5,23},{6,20},{7,21},{8,26},{9,... | collective-permute-start | bytes 589832 | tf_op jit(solution)/shard_map/ppermute | solution.py:324
  81.4 2.4 %collective-permute-start.16 = (bf16[512,768]{1,0:T(8,128)(2,1)S(1)}, bf16[512,768]{1,0:T(8,128)(2,1)S(1)}, u32[]{:S(2)}, u32[]{:S(2)}) collective-permute-start(bf16[512,768]{1,0:T(8,128)(2,1)S(1)} %constant_dynamic-update-slice_fusion.sums), channel_id=1, source_target_pairs={{0,8},{1,9},{2,10},{3,11},{4,12},{5,13},{6,14},{7,15},{8,0},{9,1},... | collective-permute-start | bytes 2359304 | tf_op jit(solution)/shard_map/ppermute | solution.py:324

commit v7 on v6

--- a/solution.py
+++ b/solution.py
@@ -132,7 +132,7 @@
 def point_grads(halo_taps, cols, taps, pres, grads, act_ref, pg_ref, spread):
     chans = pres.shape[-1]
 
-    @pl.loop(0, pres.shape[0] // cols)
+    @pl.loop(0, pres.shape[0] // cols, unroll=True)
     def _(f):
         at = pl.ds(pl.multiple_of(f * cols, cols), cols)
         pre = pres[at]

time: 85.9 us -> 85.7 us (level)
  transfers between devices with their start and end apart: 17 -> 17, of which waited for: 8 -> 7; matrix products, arithmetic and copies ran while one was open for 1% -> 1% of each run, Pallas kernels for 32% -> 32%
where the time goes in v7:
time: 85.7 us; the launch traced here: 85.4 us
  Pallas kernels  32.5 us (38%)
  starting transfers between devices  26.4 us (31%)
  waiting for transfers between devices  21.5 us (25%)
  local copies, waits for them, and re-layouts  3.58 us (4%)
  between operations  1.04 us (1%)
    pallas_call x10, Pallas kernels, call(): pl.pallas_call(kernel, out_shape=outs, in_specs=specs, out_specs=[ANY if...  32.5 us
    ppermute x11, starting transfers between devices, send(): lax.ppermute(x, ('dp', 'tm'), [(i, i ^ mask) for i in range(wide * tall)])  15 us
    ppermute x11, waiting for transfers between devices, send(): lax.ppermute(x, ('dp', 'tm'), [(i, i ^ mask) for i in range(wide * tall)])  14 us
    ppermute x3, starting transfers between devices, from_near(): lax.ppermute(x, 'tm', [(i, i ^ 1) for i in range(count) if i ^ 1 < count])  10.3 us
    ppermute x3, waiting for transfers between devices, from_near(): lax.ppermute(x, 'tm', [(i, i ^ 1) for i in range(count) if i ^ 1 < count])  7.44 us
    unnamed x17, local copies, waits for them, and re-layouts  2.3 us
  transfers between devices with their start and end apart: 17, of which 7 were waited for; matrix products, arithmetic and copies ran while one was open for 1% of the time, Pallas kernels for 32%

profile of v7, /device:TPU:0, one launch (start us, length us, event | category | flops | bytes accessed | tf_op | source)
XLA Modules:
  0.0 85.4 jit_solution(7400156564810506953)
XLA Ops:
  0.6 1.1 %constant_dynamic-slice_fusion = bf16[1,17,1,64,256]{4,3,2,1,0:T(8,128)(2,1)S(1)} fusion(bf16[1,17,2,64,256]{4,3,2,1,0:T(8,128)(2,1)} %param.4, s32[]{:T(128)S(6)} %select_n.60), kind=kLoop, calls=%fused_computation.11 | loop fusion | bytes 1114116 | tf_op jit(solution)/shard_map/jit(dynamic_index_in_dim)/dynamic_slice | solution.py:422
  1.8 0.5 collective-permute-start.1
  2.3 0.1 pad_add_fusion.code
  2.3 0.0 copy-start.3
  2.3 1.0 %copy-done.3 = bf16[3,256,256]{2,1,0:T(8,128)(2,1)S(1)} copy-done((bf16[3,256,256]{2,1,0:T(8,128)(2,1)S(1)}, bf16[3,256,256]{2,1,0:T(8,128)(2,1)}, u32[]{:S(2)}) %copy-start.3) | copy-done | bytes 393240
  3.3 0.0 copy-start.5
  3.3 1.2 %copy-done.5 = bf16[1,17,2,64,256]{4,3,2,1,0:T(8,128)(2,1)S(1)} copy-done((bf16[1,17,2,64,256]{4,3,2,1,0:T(8,128)(2,1)S(1)}, bf16[1,17,2,64,256]{4,3,2,1,0:T(8,128)(2,1)}, u32[]{:S(2)}) %copy-start.5) | copy-done | bytes 1114136
  4.6 0.0 copy-start.1
  4.6 0.0 copy-start
  4.6 2.6 %shard_map.75.act_grad = bf16[2,1088,256]{2,1,0:T(8,128)(2,1)} custom-call(s32[4]{0:T(128)S(1)} %pad_add_fusion.code, bf16[17,2,64,256]{3,2,1,0:T(8,128)(2,1)S(1)} %bitcast.15, bf16[3,256,256]{2,1,0:T(8,128)(2,1)S(1)} %copy-done.3), custom_call_target="tpu_custom_call" | custom-call | flops 855638016 | bytes 2621456 | tf_op jit(solution)/shard_map/pallas_call | solution.py:46
  7.2 0.0 copy-done.1
  7.2 4.1 %collective-permute-start = (bf16[1088,256]{1,0:T(8,128)(2,1)S(1)}, bf16[1088,256]{1,0:T(8,128)(2,1)S(1)}, u32[]{:S(2)}, u32[]{:S(2)}) collective-permute-start(bf16[1088,256]{1,0:T(8,128)(2,1)S(1)} %bitcast.20), channel_id=1, source_target_pairs={{0,1},{1,0},{2,3},{3,2},{4,5},{5,4},{6,7},{7,6},{8,9},{9,8},{10,11... | collective-permute-start | bytes 1671176 | tf_op jit(solution)/shard_map/ppermute | solution.py:392
  11.3 0.0 copy-done
  11.3 5.2 %shard_map.76.pre_loc = f32[2,1088,256]{2,1,0:T(8,128)} custom-call(s32[4]{0:T(128)S(1)} %pad_add_fusion.code, bf16[17,2,64,256]{3,2,1,0:T(8,128)(2,1)S(1)} %bitcast.12, bf16[3,3,256,256]{3,2,1,0:T(8,128)(2,1)S(1)} %copy-done), custom_call_target="tpu_custom_call" | custom-call | flops 1711276032 | bytes 4522000 | tf_op jit(solution)/shard_map/pallas_call | solution.py:46
  16.5 0.0 collective-permute-done.1.halo
  16.5 5.5 %shard_map.77 = (bf16[1088,256]{1,0:T(8,128)(2,1)S(1)}, bf16[1088,256]{1,0:T(8,128)(2,1)S(1)}, f32[1024,768]{1,0:T(8,128)S(1)}, f32[1088,256]{1,0:T(8,128)S(1)},...) custom-call(s32[4]{0:T(128)S(1)} %pad_add_fusion.code, ...), custom_call_target="tpu_custom_call" | custom-call | flops 2139095040 | bytes 16023568 | tf_op jit(solution)/shard_map/pallas_call | solution.py:46
  22.1 7.4 %collective-permute-done.halo = bf16[1088,256]{1,0:T(8,128)(2,1)S(1)} collective-permute-done((bf16[1088,256]{1,0:T(8,128)(2,1)S(1)}, bf16[1088,256]{1,0:T(8,128)(2,1)S(1)}, u32[]{:S(2)}, u32[]{:S(2)}) %collective-permute-start) | collective-permute-done | bytes 557088 | tf_op jit(solution)/shard_map/ppermute | solution.py:392
  29.5 3.1 %shard_map.78 = (bf16[1088,256]{1,0:T(8,128)(2,1)S(1)}, bf16[1088,256]{1,0:T(8,128)(2,1)S(1)}, bf16[1088,768]{1,0:T(8,128)(2,1)S(1)}, bf16[512,768]{1,0:T(8,128)(2,1)S(1)}) custom-call(s32[4]{0:T(128)S(1)} %pad_add_fusion.code, bf16[1088,256]{1,0:T(8,128)(2,1)S(1)} %collective-permute-done.halo, bf16[3,3,256,256]{3,2,1,0:T(8,128)(2,1)S(1)} %copy-done, ...), custom_call_target="tpu_custom_call" | custom-call | flops 1283457024 | bytes 12910608 | tf_op jit(solution)/shard_map/pallas_call | solution.py:46
  32.6 0.1 collective-permute-start.2
  32.7 0.5 collective-permute-start.4
  33.3 2.0 %shard_map.79 = bf16[512,768]{1,0:T(8,128)(2,1)S(1)} custom-call(s32[4]{0:T(128)S(1)} %pad_add_fusion.code, bf16[1088,256]{1,0:T(8,128)(2,1)S(1)} %collective-permute-done.halo, f32[1024,768]{1,0:T(8,128)S(1)} %get-tuple-element.40.before, bf16[17,64,768]{2,1,0:T(8,128)(2,1)S(1)} %get-tuple-element.41.cots, ...), custom_call_target="tpu_custom_call" | custom-call | flops 855638016 | bytes 9502736 | tf_op jit(solution)/shard_map/pallas_call | solution.py:46
  35.3 0.0 copy-start.2
  35.3 0.0 copy-start.4
  35.3 0.0 collective-permute-done.2
  35.3 0.2 add_convert_fusion
  35.6 1.6 %collective-permute-start.3 = (bf16[256,768]{1,0:T(8,128)(2,1)S(1)}, bf16[256,768]{1,0:T(8,128)(2,1)S(1)}, u32[]{:S(2)}, u32[]{:S(2)}) collective-permute-start(bf16[256,768]{1,0:T(8,128)(2,1)S(1)} %slice.40), channel_id=1, source_target_pairs={{0,16},{1,17},{2,18},{3,19},{4,20},{5,21},{6,22},{7,23},{8,24},{9,... | collective-permute-start | bytes 1179656 | tf_op jit(solution)/shard_map/ppermute | solution.py:324
  37.2 0.0 copy-done.2
  37.2 0.0 copy-done.4
  37.2 2.6 %shard_map.80 = bf16[17,2,64,256]{3,2,1,0:T(8,128)(2,1)} custom-call(s32[4]{0:T(128)S(1)} %pad_add_fusion.code, bf16[17,2,64,256]{3,2,1,0:T(8,128)(2,1)S(1)} %bitcast.13, bf16[1088,256]{1,0:T(8,128)(2,1)S(1)} %get-tuple-element.50.refs_0_, bf16[1088,256]{1,0:T(8,128)(2,1)S(1)} %get-tuple-element.45.act.refs_1_, bf16[3,256,256]{2,1,0:T(8,128)(2,1)S(1)} %copy-done.4), custom_call_target="tpu_custom_call" | custom-call | flops 855638016 | bytes 3735568 | tf_op jit(solution)/shard_map/pallas_call | solution.py:46
  39.8 0.0 copy-start.6
  39.8 0.0 collective-permute-start.9
  39.8 4.9 %collective-permute-start.8 = (bf16[768,256]{1,0:T(8,128)(2,1)S(1)}, bf16[768,256]{1,0:T(8,128)(2,1)S(1)}, u32[]{:S(2)}, u32[]{:S(2)}) collective-permute-start(bf16[768,256]{1,0:T(8,128)(2,1)S(1)} %slice.37), channel_id=1, source_target_pairs={{0,1},{1,0},{2,3},{3,2},{4,5},{5,4},{6,7},{7,6},{8,9},{9,8},{10,11... | collective-permute-start | bytes 1179656 | tf_op jit(solution)/shard_map/ppermute | solution.py:392
  44.7 0.0 collective-permute-done.4.far_one
  44.7 2.0 %collective-permute-done.3 = bf16[256,768]{1,0:T(8,128)(2,1)S(1)} collective-permute-done((bf16[256,768]{1,0:T(8,128)(2,1)S(1)}, bf16[256,768]{1,0:T(8,128)(2,1)S(1)}, u32[]{:S(2)}, u32[]{:S(2)}) %collective-permute-start.3) | collective-permute-done | bytes 393248 | tf_op jit(solution)/shard_map/ppermute | solution.py:324
  46.7 0.1 add_convert_fusion.1
  46.8 4.7 %collective-permute-start.5 = (bf16[64,768]{1,0:T(8,128)(2,1)S(1)}, bf16[64,768]{1,0:T(8,128)(2,1)S(1)}, u32[]{:S(2)}, u32[]{:S(2)}) collective-permute-start(bf16[64,768]{1,0:T(8,128)(2,1)S(1)} %get-tuple-element.78), channel_id=1, source_target_pairs={{0,4},{1,5},{2,6},{3,7},{4,0},{5,1},{6,2},{7,3},{8,12},{9,13},{10,... | collective-permute-start | bytes 294920 | tf_op jit(solution)/shard_map/ppermute | solution.py:324
  51.5 1.6 %collective-permute-start.6 = (bf16[64,768]{1,0:T(8,128)(2,1)S(1)}, bf16[64,768]{1,0:T(8,128)(2,1)S(1)}, u32[]{:S(2)}, u32[]{:S(2)}) collective-permute-start(bf16[64,768]{1,0:T(8,128)(2,1)S(1)} %get-tuple-element.77), channel_id=1, source_target_pairs={{0,2},{1,3},{2,0},{3,1},{4,6},{5,7},{6,4},{7,5},{8,10},{9,11},{10,... | collective-permute-start | bytes 294920 | tf_op jit(solution)/shard_map/ppermute | solution.py:324
  53.1 0.0 collective-permute-start.7
  53.1 0.0 copy-done.6
  53.1 4.0 %shard_map.81.back_loc = f32[2,1088,256]{2,1,0:T(8,128)S(1)} custom-call(s32[4]{0:T(128)S(1)} %pad_add_fusion.code, bf16[17,2,64,256]{3,2,1,0:T(8,128)(2,1)S(1)} %bitcast.16, bf16[1088,256]{1,0:T(8,128)(2,1)S(1)} %get-tuple-element.48.refs_0_, bf16[1088,256]{1,0:T(8,128)(2,1)S(1)} %get-tuple-element.53.refs_1_, bf16[3,3,256,256]{3,2,1,0:T(8,128)(2,1)S(1)} %copy-done), custom_call_target="tpu_custom_call" | custom-call | flops 1711276032 | bytes 5636112 | tf_op jit(solution)/shard_map/pallas_call | solution.py:46
  57.1 0.0 collective-permute-done.9.far_two
  57.1 0.0 collective-permute-done.8.near_one
  57.2 0.0 collective-permute-done.5
  57.2 0.0 collective-permute-done.6
  57.2 2.4 %collective-permute-done.7 = bf16[64,768]{1,0:T(8,128)(2,1)S(1)} collective-permute-done((bf16[64,768]{1,0:T(8,128)(2,1)S(1)}, bf16[64,768]{1,0:T(8,128)(2,1)S(1)}, u32[]{:S(2)}, u32[]{:S(2)}) %collective-permute-start.7) | collective-permute-done | bytes 98336 | tf_op jit(solution)/shard_map/ppermute | solution.py:324
  59.6 0.1 add_convert_fusion.3
  59.6 1.4 %collective-permute-start.10 = (bf16[64,768]{1,0:T(8,128)(2,1)S(1)}, bf16[64,768]{1,0:T(8,128)(2,1)S(1)}, u32[]{:S(2)}, u32[]{:S(2)}) collective-permute-start(bf16[64,768]{1,0:T(8,128)(2,1)S(1)} %add_convert_fusion.3), channel_id=1, source_target_pairs={{0,1},{1,0},{2,3},{3,2},{4,5},{5,4},{6,7},{7,6},{8,9},{9,8},{10,11... | collective-permute-start | bytes 294920 | tf_op jit(solution)/shard_map/ppermute | solution.py:324
  61.1 3.3 %collective-permute-done.10 = bf16[64,768]{1,0:T(8,128)(2,1)S(1)} collective-permute-done((bf16[64,768]{1,0:T(8,128)(2,1)S(1)}, bf16[64,768]{1,0:T(8,128)(2,1)S(1)}, u32[]{:S(2)}, u32[]{:S(2)}) %collective-permute-start.10) | collective-permute-done | bytes 98336 | tf_op jit(solution)/shard_map/ppermute | solution.py:324
  64.4 1.3 %collective-permute-start.12 = (bf16[320,256]{1,0:T(8,128)(2,1)S(1)}, bf16[320,256]{1,0:T(8,128)(2,1)S(1)}, u32[]{:S(2)}, u32[]{:S(2)}) collective-permute-start(bf16[320,256]{1,0:T(8,128)(2,1)S(1)} %slice.39), channel_id=1, source_target_pairs={{0,1},{1,0},{2,3},{3,2},{4,5},{5,4},{6,7},{7,6},{8,9},{9,8},{10,11... | collective-permute-start | bytes 491528 | tf_op jit(solution)/shard_map/ppermute | solution.py:392
  65.8 2.0 %collective-permute-start.11 = (bf16[64,768]{1,0:T(8,128)(2,1)S(1)}, bf16[64,768]{1,0:T(8,128)(2,1)S(1)}, u32[]{:S(2)}, u32[]{:S(2)}) collective-permute-start(bf16[64,768]{1,0:T(8,128)(2,1)S(1)} %get-tuple-element.75), channel_id=1, source_target_pairs={{0,4},{1,5},{2,6},{3,7},{4,0},{5,1},{6,2},{7,3},{8,12},{9,13},{10,... | collective-permute-start | bytes 294920 | tf_op jit(solution)/shard_map/ppermute | solution.py:324
  67.7 4.6 %collective-permute-done.11 = bf16[64,768]{1,0:T(8,128)(2,1)S(1)} collective-permute-done((bf16[64,768]{1,0:T(8,128)(2,1)S(1)}, bf16[64,768]{1,0:T(8,128)(2,1)S(1)}, u32[]{:S(2)}, u32[]{:S(2)}) %collective-permute-start.11) | collective-permute-done | bytes 98336 | tf_op jit(solution)/shard_map/ppermute | solution.py:324
  72.3 0.0 collective-permute-done.12.near_two
  72.3 0.6 collective-permute-start.13
  73.0 1.5 %collective-permute-start.14 = (bf16[128,768]{1,0:T(8,128)(2,1)S(1)}, bf16[128,768]{1,0:T(8,128)(2,1)S(1)}, u32[]{:S(2)}, u32[]{:S(2)}) collective-permute-start(bf16[128,768]{1,0:T(8,128)(2,1)S(1)} %pad_maximum_fusion), channel_id=1, source_target_pairs={{0,16},{1,17},{2,18},{3,19},{4,20},{5,21},{6,22},{7,23},{8,24},{9,... | collective-permute-start | bytes 589832 | tf_op jit(solution)/shard_map/ppermute | solution.py:324
  74.5 1.4 %collective-permute-start.15 = (bf16[128,768]{1,0:T(8,128)(2,1)S(1)}, bf16[128,768]{1,0:T(8,128)(2,1)S(1)}, u32[]{:S(2)}, u32[]{:S(2)}) collective-permute-start(bf16[128,768]{1,0:T(8,128)(2,1)S(1)} %pad_maximum_fusion), channel_id=1, source_target_pairs={{0,18},{1,19},{2,16},{3,17},{4,22},{5,23},{6,20},{7,21},{8,26},{9,... | collective-permute-start | bytes 589832 | tf_op jit(solution)/shard_map/ppermute | solution.py:324
  75.9 4.0 %shard_map.82 = bf16[17,2,64,256]{3,2,1,0:T(8,128)(2,1)} custom-call(s32[4]{0:T(128)S(1)} %pad_add_fusion.code, f32[2,1088,256]{2,1,0:T(8,128)S(1)} %shard_map.81.back_loc, bf16[3,3,256,256]{3,2,1,0:T(8,128)(2,1)S(1)} %copy-done, bf16[896,256]{1,0:T(8,128)(2,1)S(1)} %collective-permute-done.4.far_one, bf16[192,256]{1,0:T(8,128)(2,1)S(1)} %collective-permute-done.9.far_two, ...), custom_call_target="tpu_custom_call" | custom-call | flops 855638016 | bytes 5636112 | tf_op jit(solution)/shard_map/pallas_call | solution.py:46
  79.9 0.0 collective-permute-done.13
  79.9 0.0 collective-permute-done.14
  79.9 1.2 %collective-permute-done.15 = bf16[128,768]{1,0:T(8,128)(2,1)S(1)} collective-permute-done((bf16[128,768]{1,0:T(8,128)(2,1)S(1)}, bf16[128,768]{1,0:T(8,128)(2,1)S(1)}, u32[]{:S(2)}, u32[]{:S(2)}) %collective-permute-start.15) | collective-permute-done | bytes 196640 | tf_op jit(solution)/shard_map/ppermute | solution.py:324
  81.2 0.1 collective-permute-start.16
  81.3 1.8 %shard_map.83 = (f32[3,3,256,256]{3,2,1,0:T(8,128)}, f32[3,256,256]{2,1,0:T(8,128)}) custom-call(s32[4]{0:T(128)S(1)} %pad_add_fusion.code, bf16[512,768]{1,0:T(8,128)(2,1)S(1)} %constant_dynamic-update-slice_fusion.sums), custom_call_target="tpu_custom_call" | custom-call | bytes 3932176 | tf_op jit(solution)/shard_map/pallas_call | solution.py:46
  83.0 0.5 collective-permute-done.16.sums
  83.5 1.8 %shard_map.84 = (f32[3,3,256,256]{3,2,1,0:T(8,128)}, f32[3,256,256]{2,1,0:T(8,128)}) custom-call(s32[4]{0:T(128)S(1)} %pad_add_fusion.code, bf16[512,768]{1,0:T(8,128)(2,1)S(1)} %collective-permute-done.16.sums, f32[3,3,256,256]{3,2,1,0:T(8,128)} %get-tuple-element.70.refs_0_, ...), custom_call_target="tpu_custom_call", output_to_operand_aliasing={{0}: (2, {}), {1}: (3, {})} | custom-call | bytes 7077904 | tf_op jit(solution)/shard_map/pallas_call | solution.py:46
  (13 shorter events, 0.3 us)
Async XLA Ops:
  1.8 14.8 %collective-permute-start.1 = (bf16[1088,256]{1,0:T(8,128)(2,1)S(1)}, bf16[1088,256]{1,0:T(8,128)(2,1)S(1)}, u32[]{:S(2)}, u32[]{:S(2)}) collective-permute-start(bf16[1088,256]{1,0:T(8,128)(2,1)S(1)} %bitcast.19), channel_id=1, source_target_pairs={{0,8},{1,2},{2,1},{3,4},{4,3},{5,6},{6,5},{7,15},{8,0},{9,10},{10,... | collective-permute-start | bytes 1671176 | tf_op jit(solution)/shard_map/ppermute | solution.py:402
  2.3 1.0 %copy-start.3 = (bf16[3,256,256]{2,1,0:T(8,128)(2,1)S(1)}, bf16[3,256,256]{2,1,0:T(8,128)(2,1)}, u32[]{:S(2)}) copy-start(bf16[3,256,256]{2,1,0:T(8,128)(2,1)} %refs_2_.2) | copy-start | bytes 1179652
  3.3 1.2 %copy-start.5 = (bf16[1,17,2,64,256]{4,3,2,1,0:T(8,128)(2,1)S(1)}, bf16[1,17,2,64,256]{4,3,2,1,0:T(8,128)(2,1)}, u32[]{:S(2)}) copy-start(bf16[1,17,2,64,256]{4,3,2,1,0:T(8,128)(2,1)} %param.5) | copy-start | bytes 3342340
  4.6 2.6 %copy-start.1 = (bf16[1,17,2,64,256]{4,3,2,1,0:T(8,128)(2,1)S(1)}, bf16[1,17,2,64,256]{4,3,2,1,0:T(8,128)(2,1)}, u32[]{:S(2)}) copy-start(bf16[1,17,2,64,256]{4,3,2,1,0:T(8,128)(2,1)} %param.4) | copy-start | bytes 3342340
  4.6 6.8 %copy-start = (bf16[3,3,256,256]{3,2,1,0:T(8,128)(2,1)S(1)}, bf16[3,3,256,256]{3,2,1,0:T(8,128)(2,1)}, u32[]{:S(2)}) copy-start(bf16[3,3,256,256]{3,2,1,0:T(8,128)(2,1)} %ws.7) | copy-start | bytes 3538948
  7.2 22.3 %collective-permute-start = (bf16[1088,256]{1,0:T(8,128)(2,1)S(1)}, bf16[1088,256]{1,0:T(8,128)(2,1)S(1)}, u32[]{:S(2)}, u32[]{:S(2)}) collective-permute-start(bf16[1088,256]{1,0:T(8,128)(2,1)S(1)} %bitcast.20), channel_id=1, source_target_pairs={{0,1},{1,0},{2,3},{3,2},{4,5},{5,4},{6,7},{7,6},{8,9},{9,8},{10,11... | collective-permute-start | bytes 1671176 | tf_op jit(solution)/shard_map/ppermute | solution.py:392
  32.6 2.7 %collective-permute-start.2 = (bf16[512,768]{1,0:T(8,128)(2,1)S(1)}, bf16[512,768]{1,0:T(8,128)(2,1)S(1)}, u32[]{:S(2)}, u32[]{:S(2)}) collective-permute-start(bf16[512,768]{1,0:T(8,128)(2,1)S(1)} %get-tuple-element.47), channel_id=1, source_target_pairs={{0,8},{1,9},{2,10},{3,11},{4,12},{5,13},{6,14},{7,15},{8,0},{9,1},... | collective-permute-start | bytes 2359304 | tf_op jit(solution)/shard_map/ppermute | solution.py:324
  32.7 12.0 %collective-permute-start.4 = (bf16[896,256]{1,0:T(8,128)(2,1)S(1)}, bf16[896,256]{1,0:T(8,128)(2,1)S(1)}, u32[]{:S(2)}, u32[]{:S(2)}) collective-permute-start(bf16[896,256]{1,0:T(8,128)(2,1)S(1)} %slice.31), channel_id=1, source_target_pairs={{0,8},{1,2},{2,1},{3,4},{4,3},{5,6},{6,5},{7,15},{8,0},{9,10},{10,... | collective-permute-start | bytes 1376264 | tf_op jit(solution)/shard_map/ppermute | solution.py:402
  35.3 1.9 %copy-start.2 = (bf16[1,17,2,64,256]{4,3,2,1,0:T(8,128)(2,1)S(1)}, bf16[1,17,2,64,256]{4,3,2,1,0:T(8,128)(2,1)}, u32[]{:S(2)}) copy-start(bf16[1,17,2,64,256]{4,3,2,1,0:T(8,128)(2,1)} %param.4) | copy-start | bytes 3342340
  35.3 1.9 %copy-start.4 = (bf16[3,256,256]{2,1,0:T(8,128)(2,1)S(1)}, bf16[3,256,256]{2,1,0:T(8,128)(2,1)}, u32[]{:S(2)}) copy-start(bf16[3,256,256]{2,1,0:T(8,128)(2,1)} %refs_2_.2) | copy-start | bytes 1179652
  35.6 11.1 %collective-permute-start.3 = (bf16[256,768]{1,0:T(8,128)(2,1)S(1)}, bf16[256,768]{1,0:T(8,128)(2,1)S(1)}, u32[]{:S(2)}, u32[]{:S(2)}) collective-permute-start(bf16[256,768]{1,0:T(8,128)(2,1)S(1)} %slice.40), channel_id=1, source_target_pairs={{0,16},{1,17},{2,18},{3,19},{4,20},{5,21},{6,22},{7,23},{8,24},{9,... | collective-permute-start | bytes 1179656 | tf_op jit(solution)/shard_map/ppermute | solution.py:324
  39.8 13.3 %copy-start.6 = (bf16[1,17,2,64,256]{4,3,2,1,0:T(8,128)(2,1)S(1)}, bf16[1,17,2,64,256]{4,3,2,1,0:T(8,128)(2,1)}, u32[]{:S(2)}) copy-start(bf16[1,17,2,64,256]{4,3,2,1,0:T(8,128)(2,1)} %param.5) | copy-start | bytes 3342340
  39.8 17.4 %collective-permute-start.9 = (bf16[192,256]{1,0:T(8,128)(2,1)S(1)}, bf16[192,256]{1,0:T(8,128)(2,1)S(1)}, u32[]{:S(2)}, u32[]{:S(2)}) collective-permute-start(bf16[192,256]{1,0:T(8,128)(2,1)S(1)} %slice.38), channel_id=1, source_target_pairs={{0,8},{1,2},{2,1},{3,4},{4,3},{5,6},{6,5},{7,15},{8,0},{9,10},{10,... | collective-permute-start | bytes 294920 | tf_op jit(solution)/shard_map/ppermute | solution.py:402
  39.8 17.4 %collective-permute-start.8 = (bf16[768,256]{1,0:T(8,128)(2,1)S(1)}, bf16[768,256]{1,0:T(8,128)(2,1)S(1)}, u32[]{:S(2)}, u32[]{:S(2)}) collective-permute-start(bf16[768,256]{1,0:T(8,128)(2,1)S(1)} %slice.37), channel_id=1, source_target_pairs={{0,1},{1,0},{2,3},{3,2},{4,5},{5,4},{6,7},{7,6},{8,9},{9,8},{10,11... | collective-permute-start | bytes 1179656 | tf_op jit(solution)/shard_map/ppermute | solution.py:392
  46.8 10.4 %collective-permute-start.5 = (bf16[64,768]{1,0:T(8,128)(2,1)S(1)}, bf16[64,768]{1,0:T(8,128)(2,1)S(1)}, u32[]{:S(2)}, u32[]{:S(2)}) collective-permute-start(bf16[64,768]{1,0:T(8,128)(2,1)S(1)} %get-tuple-element.78), channel_id=1, source_target_pairs={{0,4},{1,5},{2,6},{3,7},{4,0},{5,1},{6,2},{7,3},{8,12},{9,13},{10,... | collective-permute-start | bytes 294920 | tf_op jit(solution)/shard_map/ppermute | solution.py:324
  51.5 5.6 %collective-permute-start.6 = (bf16[64,768]{1,0:T(8,128)(2,1)S(1)}, bf16[64,768]{1,0:T(8,128)(2,1)S(1)}, u32[]{:S(2)}, u32[]{:S(2)}) collective-permute-start(bf16[64,768]{1,0:T(8,128)(2,1)S(1)} %get-tuple-element.77), channel_id=1, source_target_pairs={{0,2},{1,3},{2,0},{3,1},{4,6},{5,7},{6,4},{7,5},{8,10},{9,11},{10,... | collective-permute-start | bytes 294920 | tf_op jit(solution)/shard_map/ppermute | solution.py:324
  53.1 6.5 %collective-permute-start.7 = (bf16[64,768]{1,0:T(8,128)(2,1)S(1)}, bf16[64,768]{1,0:T(8,128)(2,1)S(1)}, u32[]{:S(2)}, u32[]{:S(2)}) collective-permute-start(bf16[64,768]{1,0:T(8,128)(2,1)S(1)} %get-tuple-element.76), channel_id=1, source_target_pairs={{0,6},{1,7},{2,4},{3,5},{4,2},{5,3},{6,0},{7,1},{8,14},{9,15},{10,... | collective-permute-start | bytes 294920 | tf_op jit(solution)/shard_map/ppermute | solution.py:324
  59.6 4.8 %collective-permute-start.10 = (bf16[64,768]{1,0:T(8,128)(2,1)S(1)}, bf16[64,768]{1,0:T(8,128)(2,1)S(1)}, u32[]{:S(2)}, u32[]{:S(2)}) collective-permute-start(bf16[64,768]{1,0:T(8,128)(2,1)S(1)} %add_convert_fusion.3), channel_id=1, source_target_pairs={{0,1},{1,0},{2,3},{3,2},{4,5},{5,4},{6,7},{7,6},{8,9},{9,8},{10,11... | collective-permute-start | bytes 294920 | tf_op jit(solution)/shard_map/ppermute | solution.py:324
  64.4 7.9 %collective-permute-start.12 = (bf16[320,256]{1,0:T(8,128)(2,1)S(1)}, bf16[320,256]{1,0:T(8,128)(2,1)S(1)}, u32[]{:S(2)}, u32[]{:S(2)}) collective-permute-start(bf16[320,256]{1,0:T(8,128)(2,1)S(1)} %slice.39), channel_id=1, source_target_pairs={{0,1},{1,0},{2,3},{3,2},{4,5},{5,4},{6,7},{7,6},{8,9},{9,8},{10,11... | collective-permute-start | bytes 491528 | tf_op jit(solution)/shard_map/ppermute | solution.py:392
  65.8 6.6 %collective-permute-start.11 = (bf16[64,768]{1,0:T(8,128)(2,1)S(1)}, bf16[64,768]{1,0:T(8,128)(2,1)S(1)}, u32[]{:S(2)}, u32[]{:S(2)}) collective-permute-start(bf16[64,768]{1,0:T(8,128)(2,1)S(1)} %get-tuple-element.75), channel_id=1, source_target_pairs={{0,4},{1,5},{2,6},{3,7},{4,0},{5,1},{6,2},{7,3},{8,12},{9,13},{10,... | collective-permute-start | bytes 294920 | tf_op jit(solution)/shard_map/ppermute | solution.py:324
  72.3 7.5 %collective-permute-start.13 = (bf16[128,768]{1,0:T(8,128)(2,1)S(1)}, bf16[128,768]{1,0:T(8,128)(2,1)S(1)}, u32[]{:S(2)}, u32[]{:S(2)}) collective-permute-start(bf16[128,768]{1,0:T(8,128)(2,1)S(1)} %pad_maximum_fusion), channel_id=1, source_target_pairs={{0,2},{1,3},{2,0},{3,1},{4,6},{5,7},{6,4},{7,5},{8,10},{9,11},{10,... | collective-permute-start | bytes 589832 | tf_op jit(solution)/shard_map/ppermute | solution.py:324
  73.0 6.9 %collective-permute-start.14 = (bf16[128,768]{1,0:T(8,128)(2,1)S(1)}, bf16[128,768]{1,0:T(8,128)(2,1)S(1)}, u32[]{:S(2)}, u32[]{:S(2)}) collective-permute-start(bf16[128,768]{1,0:T(8,128)(2,1)S(1)} %pad_maximum_fusion), channel_id=1, source_target_pairs={{0,16},{1,17},{2,18},{3,19},{4,20},{5,21},{6,22},{7,23},{8,24},{9,... | collective-permute-start | bytes 589832 | tf_op jit(solution)/shard_map/ppermute | solution.py:324
  74.5 6.7 %collective-permute-start.15 = (bf16[128,768]{1,0:T(8,128)(2,1)S(1)}, bf16[128,768]{1,0:T(8,128)(2,1)S(1)}, u32[]{:S(2)}, u32[]{:S(2)}) collective-permute-start(bf16[128,768]{1,0:T(8,128)(2,1)S(1)} %pad_maximum_fusion), channel_id=1, source_target_pairs={{0,18},{1,19},{2,16},{3,17},{4,22},{5,23},{6,20},{7,21},{8,26},{9,... | collective-permute-start | bytes 589832 | tf_op jit(solution)/shard_map/ppermute | solution.py:324
  81.2 2.4 %collective-permute-start.16 = (bf16[512,768]{1,0:T(8,128)(2,1)S(1)}, bf16[512,768]{1,0:T(8,128)(2,1)S(1)}, u32[]{:S(2)}, u32[]{:S(2)}) collective-permute-start(bf16[512,768]{1,0:T(8,128)(2,1)S(1)} %constant_dynamic-update-slice_fusion.sums), channel_id=1, source_target_pairs={{0,8},{1,9},{2,10},{3,11},{4,12},{5,13},{6,14},{7,15},{8,0},{9,1},... | collective-permute-start | bytes 2359304 | tf_op jit(solution)/shard_map/ppermute | solution.py:324
